TPU v7x, 32 devices: a whole 2x2x4 slice. The times are simulated.
32 devices in a mesh: section: 2 (over core), seq: 4 (over z), fsdp: 4 (over y, x).
Axes of the slice: x: 2, y: 2, z: 4, core: 2. Of those that a mesh axis runs over, the one named last changes fastest.
Arguments:
- activations: bfloat16 [2, 4, 1024, 1024], P(None, 'fsdp', 'seq'), may hold values from -6 to 6
- cotangent: bfloat16 [2, 4, 1024, 1024], P(None, 'fsdp', 'seq'), may hold values from -6 to 6
- lengths: int32 [2, 4], P(None, 'fsdp'), may hold values from 896 to 1024, as said below
- mixgain: bfloat16 [2, 1024], P('section', 'fsdp'), may hold values from 0.5 to 1.5
- mixshift: bfloat16 [2, 1024], P('section', 'fsdp'), may hold values from -1.75 to 1.75
- mixweight: bfloat16 [2, 1024, 3072], P('section', 'fsdp'), may hold values from -0.25 to 0.25
- mixbias: bfloat16 [2, 2, 1024], P('section', None, 'fsdp'), may hold values from -1.75 to 1.75
- outweight: bfloat16 [2, 1024, 1024], P('section', 'fsdp'), may hold values from -0.75 to 0.75
- outbias: bfloat16 [2, 1024], P('section', 'fsdp'), may hold values from -1.75 to 1.75
- mixscale: bfloat16 [2, 1024], P('section', 'fsdp'), may hold values from 0.5 to 2
- feedgain: bfloat16 [2, 1024], P('section', 'fsdp'), may hold values from 0.5 to 1.5
- feedshift: bfloat16 [2, 1024], P('section', 'fsdp'), may hold values from -1.75 to 1.75
- upweight: bfloat16 [2, 1024, 4096], P('section', 'fsdp'), may hold values from -0.1875 to 0.1875
- upbias: bfloat16 [2, 4096], P('section', 'fsdp'), may hold values from -1.75 to 1.75
- downweight: bfloat16 [2, 4096, 1024], P('section', 'fsdp'), may hold values from -0.09375 to 0.09375
- downbias: bfloat16 [2, 1024], P('section', 'fsdp'), may hold values from -1.75 to 1.75
- feedscale: bfloat16 [2, 1024], P('section', 'fsdp'), may hold values from 0.5 to 2
Outputs:
- section_output: bfloat16 [2, 2, 4, 1024, 1024], P('section', None, 'fsdp', 'seq')
- input_gradient: float32 [2, 2, 4, 1024, 1024], P('section', None, 'fsdp', 'seq')
- mixgain_gradient: float32 [2, 1024], P('section', 'fsdp')
- mixshift_gradient: float32 [2, 1024], P('section', 'fsdp')
- mixweight_gradient: float32 [2, 1024, 3072], P('section', 'fsdp')
- mixbias_gradient: float32 [2, 2, 1024], P('section', None, 'fsdp')
- outweight_gradient: float32 [2, 1024, 1024], P('section', 'fsdp')
- outbias_gradient: float32 [2, 1024], P('section', 'fsdp')
- mixscale_gradient: float32 [2, 1024], P('section', 'fsdp')
- feedgain_gradient: float32 [2, 1024], P('section', 'fsdp')
- feedshift_gradient: float32 [2, 1024], P('section', 'fsdp')
- upweight_gradient: float32 [2, 1024, 4096], P('section', 'fsdp')
- upbias_gradient: float32 [2, 4096], P('section', 'fsdp')
- downweight_gradient: float32 [2, 4096, 1024], P('section', 'fsdp')
- downbias_gradient: float32 [2, 1024], P('section', 'fsdp')
- feedscale_gradient: float32 [2, 1024], P('section', 'fsdp')
Inputs may be any that keep to these rules, and one draw needn't show every extreme that they name: `lengths`: each micro-batch has one image, drawn from the seed, of length 1024; keys at or past an image's length are masked.
All inputs are finite; a program needn't handle non-finite values.
Results may differ from a plain program's by a relative error of at most 0.019.
Values may be sent and summed in bfloat16 or wider, within the bound.
No kernel may reach another device: no remote copies, remote signals or barrier semaphores. Data moves between devices by JAX's collectives and lax.ppermute only.
A program may use at most 256 MiB of HBM per device.

v0:
```python
import jax
import jax.numpy as jnp
from jax import lax
from jax.sharding import PartitionSpec as P

HEAD_DIM = 64


EPSILON = 1e-06
NEGATIVE = -1000000000.0


def from_behind(value, axis, steps):
    count = lax.axis_size(axis)
    initial, last = (max(0, -steps), min(count, count - steps))
    return lax.ppermute(value, axis, [(source, source + steps) for source in range(initial, last)])


def norm_apply(values, gain, shift):
    center = jnp.mean(values, axis=-1, keepdims=True)
    centered = values - center
    spread = jnp.mean(centered * centered, axis=-1, keepdims=True)
    return centered * lax.rsqrt(spread + EPSILON) * gain + shift


def gelu_exact(values):
    return jax.nn.gelu(values, approximate=False)


def masked_scores(query_block, key_heads, key_mask):
    scores = jnp.einsum(
        "iqhd,ikhd->ihqk", query_block, key_heads, preferred_element_type=jnp.float32
    )
    scores = scores * query_block.shape[-1] ** (-0.5)
    return jnp.where(key_mask, scores, NEGATIVE)


def block_plan(full_rows):
    pieces = 2
    return (pieces, full_rows // pieces)


def attend_forward(query_heads, key_heads, value_heads, tick_lengths):
    full_rows = key_heads.shape[1]
    pieces, block_rows = block_plan(full_rows)
    key_mask = (jnp.arange(full_rows)[None, :] < tick_lengths[:, None])[:, None, None, :]
    out_blocks = []
    total_blocks = []
    for piece_index in range(pieces):
        query_block = query_heads[:, piece_index * block_rows : (piece_index + 1) * block_rows]
        scores = masked_scores(query_block, key_heads, key_mask)
        row_peak = jnp.max(scores, axis=-1, keepdims=True)
        row_total = row_peak + jnp.log(jnp.sum(jnp.exp(scores - row_peak), axis=-1, keepdims=True))
        probs_low = jnp.exp(scores - row_total).astype(jnp.bfloat16)
        out_blocks.append(
            jnp.einsum(
                "ihqk,ikhd->iqhd", probs_low, value_heads, preferred_element_type=jnp.float32
            ).astype(jnp.bfloat16)
        )
        total_blocks.append(row_total)
    return (jnp.concatenate(out_blocks, axis=1), jnp.concatenate(total_blocks, axis=2))


def attend_backward(query_heads, key_heads, value_heads, row_totals, grad_heads, tick_lengths):
    full_rows = key_heads.shape[1]
    pieces, block_rows = block_plan(full_rows)
    score_scale = query_heads.shape[-1] ** (-0.5)
    key_mask = (jnp.arange(full_rows)[None, :] < tick_lengths[:, None])[:, None, None, :]
    value_sum = jnp.zeros(value_heads.shape, jnp.float32)
    key_sum = jnp.zeros(key_heads.shape, jnp.float32)
    query_blocks = []
    for piece_index in range(pieces):
        start_row = piece_index * block_rows
        query_block = query_heads[:, start_row : start_row + block_rows]
        grad_block = grad_heads[:, start_row : start_row + block_rows]
        scores = masked_scores(query_block, key_heads, key_mask)
        probs = jnp.exp(scores - row_totals[:, :, start_row : start_row + block_rows])
        probs_low = probs.astype(jnp.bfloat16)
        value_sum = value_sum + jnp.einsum(
            "ihqk,iqhd->ikhd", probs_low, grad_block, preferred_element_type=jnp.float32
        )
        prob_grad = jnp.einsum(
            "iqhd,ikhd->ihqk", grad_block, value_heads, preferred_element_type=jnp.float32
        )
        score_grad = probs * (prob_grad - jnp.sum(prob_grad * probs, axis=-1, keepdims=True))
        score_grad = score_grad.astype(jnp.bfloat16)
        query_part = jnp.einsum(
            "ihqk,ikhd->iqhd", score_grad, key_heads, preferred_element_type=jnp.float32
        )
        query_blocks.append((query_part * score_scale).astype(jnp.bfloat16))
        key_sum = key_sum + jnp.einsum(
            "ihqk,iqhd->ikhd", score_grad, query_block, preferred_element_type=jnp.float32
        )
    return (
        jnp.concatenate(query_blocks, axis=1),
        (key_sum * score_scale).astype(jnp.bfloat16),
        value_sum.astype(jnp.bfloat16),
    )


def layer_forward(hidden, tick_lengths, params):
    (
        mixgain,
        mixshift,
        mixweight,
        mixbias,
        outweight,
        outbias,
        mixscale,
        feedgain,
        feedshift,
        upweight,
        upbias,
        downweight,
        downbias,
        feedscale,
    ) = params
    images, token_rows, model_width = hidden.shape
    groups = lax.axis_size("seq")
    group_width = model_width // groups
    group_heads = group_width // HEAD_DIM
    full_rows = token_rows * groups
    hidden_wide = hidden.astype(jnp.float32)
    normed = norm_apply(
        hidden_wide, mixgain.astype(jnp.float32), mixshift.astype(jnp.float32)
    ).astype(jnp.bfloat16)
    zeros_row = jnp.zeros_like(mixbias[0])
    bias_triple = jnp.concatenate([mixbias[0], zeros_row, mixbias[1]]).astype(jnp.float32)
    triple = (
        jnp.einsum("isd,de->ise", normed, mixweight, preferred_element_type=jnp.float32)
        + bias_triple
    )
    triple = triple.astype(jnp.bfloat16).reshape(images, token_rows, 3, groups, group_width)
    head_layout = lax.all_to_all(triple, "seq", split_axis=3, concat_axis=1, tiled=True)
    head_layout = head_layout.reshape(images, full_rows, 3, group_heads, HEAD_DIM)
    query_heads = head_layout[:, :, 0]
    key_heads = head_layout[:, :, 1]
    value_heads = head_layout[:, :, 2]
    mixed_heads, row_totals = attend_forward(query_heads, key_heads, value_heads, tick_lengths)
    mixed_flat = mixed_heads.reshape(images, full_rows, 1, group_width)
    mixed = lax.all_to_all(mixed_flat, "seq", split_axis=1, concat_axis=2, tiled=True).reshape(
        images, token_rows, model_width
    )
    branch = jnp.einsum("isd,de->ise", mixed, outweight, preferred_element_type=jnp.float32)
    branch = branch + outbias.astype(jnp.float32)
    residual = hidden_wide + mixscale.astype(jnp.float32) * branch
    normed_two = norm_apply(
        residual, feedgain.astype(jnp.float32), feedshift.astype(jnp.float32)
    ).astype(jnp.bfloat16)
    hidden_up = jnp.einsum("isd,df->isf", normed_two, upweight, preferred_element_type=jnp.float32)
    hidden_up = hidden_up + upbias.astype(jnp.float32)
    active = gelu_exact(hidden_up).astype(jnp.bfloat16)
    branch_two = jnp.einsum("isf,fd->isd", active, downweight, preferred_element_type=jnp.float32)
    branch_two = branch_two + downbias.astype(jnp.float32)
    result = (residual + feedscale.astype(jnp.float32) * branch_two).astype(jnp.bfloat16)
    saved_state = (
        hidden_wide,
        normed,
        query_heads,
        key_heads,
        value_heads,
        row_totals,
        mixed,
        branch,
        residual,
        normed_two,
        hidden_up,
        active,
        branch_two,
    )
    return (result, saved_state)


def layer_backward(incoming, tick_lengths, params, saved_state):
    (
        mixgain,
        mixshift,
        mixweight,
        mixbias,
        outweight,
        outbias,
        mixscale,
        feedgain,
        feedshift,
        upweight,
        upbias,
        downweight,
        downbias,
        feedscale,
    ) = params
    (
        hidden_wide,
        normed,
        query_heads,
        key_heads,
        value_heads,
        row_totals,
        mixed,
        branch,
        residual,
        normed_two,
        hidden_up,
        active,
        branch_two,
    ) = saved_state
    images, token_rows, model_width = incoming.shape
    groups = lax.axis_size("seq")
    group_width = model_width // groups
    group_heads = group_width // HEAD_DIM
    full_rows = token_rows * groups
    feed_scale = feedscale.astype(jnp.float32)
    scale_two_grad = jnp.sum(incoming * branch_two, axis=(0, 1))
    lower_grad = (feed_scale * incoming).astype(jnp.bfloat16)
    down_bias_grad = jnp.sum(lower_grad.astype(jnp.float32), axis=(0, 1))
    down_weight_grad = jnp.einsum(
        "isf,isd->fd", active, lower_grad, preferred_element_type=jnp.float32
    )
    active_grad = jnp.einsum(
        "isd,fd->isf", lower_grad, downweight, preferred_element_type=jnp.float32
    )
    gelu_back = jax.vjp(gelu_exact, hidden_up)[1]
    up_grad = gelu_back(active_grad)[0].astype(jnp.bfloat16)
    up_bias_grad = jnp.sum(up_grad.astype(jnp.float32), axis=(0, 1))
    up_weight_grad = jnp.einsum(
        "isd,isf->df", normed_two, up_grad, preferred_element_type=jnp.float32
    )
    normed_two_grad = jnp.einsum(
        "isf,df->isd", up_grad, upweight, preferred_element_type=jnp.float32
    )
    feed_back = jax.vjp(
        norm_apply, residual, feedgain.astype(jnp.float32), feedshift.astype(jnp.float32)
    )[1]
    residual_part, feed_gain_grad, feed_shift_grad = feed_back(normed_two_grad)
    residual_grad = incoming + residual_part
    scale_one_grad = jnp.sum(residual_grad * branch, axis=(0, 1))
    branch_grad = (mixscale.astype(jnp.float32) * residual_grad).astype(jnp.bfloat16)
    out_bias_grad = jnp.sum(branch_grad.astype(jnp.float32), axis=(0, 1))
    out_weight_grad = jnp.einsum(
        "isd,ise->de", mixed, branch_grad, preferred_element_type=jnp.float32
    )
    mixed_grad = jnp.einsum(
        "ise,de->isd", branch_grad, outweight, preferred_element_type=jnp.float32
    )
    mixed_grad = mixed_grad.astype(jnp.bfloat16).reshape(images, token_rows, groups, group_width)
    grad_heads = lax.all_to_all(mixed_grad, "seq", split_axis=2, concat_axis=1, tiled=True)
    grad_heads = grad_heads.reshape(images, full_rows, group_heads, HEAD_DIM)
    query_grad, key_grad, value_grad = attend_backward(
        query_heads, key_heads, value_heads, row_totals, grad_heads, tick_lengths
    )
    stacked = jnp.stack([query_grad, key_grad, value_grad], axis=2).reshape(
        images, full_rows, 3, 1, group_width
    )
    triple_grad = lax.all_to_all(stacked, "seq", split_axis=1, concat_axis=3, tiled=True)
    triple_grad = triple_grad.reshape(images, token_rows, 3 * model_width)
    mix_weight_grad = jnp.einsum(
        "isd,ise->de", normed, triple_grad, preferred_element_type=jnp.float32
    )
    triple_sum = jnp.sum(triple_grad.astype(jnp.float32), axis=(0, 1)).reshape(3, model_width)
    mix_bias_grad = jnp.stack([triple_sum[0], triple_sum[2]])
    normed_grad = jnp.einsum(
        "ise,de->isd", triple_grad, mixweight, preferred_element_type=jnp.float32
    )
    mix_back = jax.vjp(
        norm_apply, hidden_wide, mixgain.astype(jnp.float32), mixshift.astype(jnp.float32)
    )[1]
    hidden_part, mix_gain_grad, mix_shift_grad = mix_back(normed_grad)
    input_grad = residual_grad + hidden_part
    gradients = (
        mix_gain_grad,
        mix_shift_grad,
        mix_weight_grad,
        mix_bias_grad,
        out_weight_grad,
        out_bias_grad,
        scale_one_grad,
        feed_gain_grad,
        feed_shift_grad,
        up_weight_grad,
        up_bias_grad,
        down_weight_grad,
        down_bias_grad,
        scale_two_grad,
    )
    return (input_grad, gradients)


def body(
    activations,
    cotangent,
    lengths,
    mixgain,
    mixshift,
    mixweight,
    mixbias,
    outweight,
    outbias,
    mixscale,
    feedgain,
    feedshift,
    upweight,
    upbias,
    downweight,
    downbias,
    feedscale,
):
    full = (
        lax.all_gather(mixgain[0], "fsdp", axis=0, tiled=True),
        lax.all_gather(mixshift[0], "fsdp", axis=0, tiled=True),
        lax.all_gather(mixweight[0], "fsdp", axis=0, tiled=True),
        lax.all_gather(mixbias[0], "fsdp", axis=1, tiled=True),
        lax.all_gather(outweight[0], "fsdp", axis=0, tiled=True),
        lax.all_gather(outbias[0], "fsdp", axis=0, tiled=True),
        lax.all_gather(mixscale[0], "fsdp", axis=0, tiled=True),
        lax.all_gather(feedgain[0], "fsdp", axis=0, tiled=True),
        lax.all_gather(feedshift[0], "fsdp", axis=0, tiled=True),
        lax.all_gather(upweight[0], "fsdp", axis=0, tiled=True),
        lax.all_gather(upbias[0], "fsdp", axis=0, tiled=True),
        lax.all_gather(downweight[0], "fsdp", axis=0, tiled=True),
        lax.all_gather(downbias[0], "fsdp", axis=0, tiled=True),
        lax.all_gather(feedscale[0], "fsdp", axis=0, tiled=True),
    )
    section_index = lax.axis_index("section")
    on_first = section_index == 0
    micro = activations.shape[0]
    received = jnp.zeros(activations.shape[1:], jnp.bfloat16)
    results = []
    saved_list = []
    length_list = []
    for tick_index in range(micro + 1):
        current = min(tick_index, micro - 1)
        previous = max(tick_index - 1, 0)
        hidden = jnp.where(on_first, activations[current], received)
        tick_lengths = jnp.where(on_first, lengths[current], lengths[previous])
        result, saved_state = layer_forward(hidden, tick_lengths, full)
        results.append(result)
        saved_list.append(saved_state)
        length_list.append(tick_lengths)
        if tick_index < micro:
            received = from_behind(result, "section", 1)
    full = (
        lax.all_gather(mixgain[0], "fsdp", axis=0, tiled=True),
        lax.all_gather(mixshift[0], "fsdp", axis=0, tiled=True),
        lax.all_gather(mixweight[0], "fsdp", axis=0, tiled=True),
        lax.all_gather(mixbias[0], "fsdp", axis=1, tiled=True),
        lax.all_gather(outweight[0], "fsdp", axis=0, tiled=True),
        lax.all_gather(outbias[0], "fsdp", axis=0, tiled=True),
        lax.all_gather(mixscale[0], "fsdp", axis=0, tiled=True),
        lax.all_gather(feedgain[0], "fsdp", axis=0, tiled=True),
        lax.all_gather(feedshift[0], "fsdp", axis=0, tiled=True),
        lax.all_gather(upweight[0], "fsdp", axis=0, tiled=True),
        lax.all_gather(upbias[0], "fsdp", axis=0, tiled=True),
        lax.all_gather(downweight[0], "fsdp", axis=0, tiled=True),
        lax.all_gather(downbias[0], "fsdp", axis=0, tiled=True),
        lax.all_gather(feedscale[0], "fsdp", axis=0, tiled=True),
    )
    returned = jnp.zeros(activations.shape[1:], jnp.float32)
    summed = None
    input_grads = []
    for tick_index in range(micro + 1):
        later = min(tick_index + 1, micro)
        earlier = max(tick_index - 1, 0)
        saved_state = jax.tree.map(
            lambda upper_kept, lower_kept: jnp.where(on_first, lower_kept, upper_kept),
            saved_list[later],
            saved_list[earlier],
        )
        tick_lengths = jnp.where(on_first, length_list[earlier], length_list[later])
        valid_flag = jnp.where(on_first, float(tick_index >= 1), float(tick_index < micro))
        from_top = cotangent[min(tick_index, micro - 1)].astype(jnp.float32)
        incoming = jnp.where(on_first, returned, from_top) * valid_flag
        input_grad, gradients = layer_backward(incoming, tick_lengths, full, saved_state)
        summed = gradients if summed is None else jax.tree.map(jnp.add, summed, gradients)
        input_grads.append(input_grad)
        if tick_index < micro:
            returned = from_behind(input_grad.astype(jnp.bfloat16), "section", -1).astype(
                jnp.float32
            )
    section_output = jnp.stack(
        [
            jnp.where(on_first, results[micro_index], results[micro_index + 1])
            for micro_index in range(micro)
        ]
    )[None]
    input_gradient = jnp.stack(
        [
            jnp.where(on_first, input_grads[micro_index + 1], input_grads[micro_index])
            for micro_index in range(micro)
        ]
    )[None]
    shares = (
        lax.psum_scatter(
            summed[0].astype(jnp.bfloat16), "fsdp", scatter_dimension=0, tiled=True
        ).astype(jnp.float32),
        lax.psum_scatter(
            summed[1].astype(jnp.bfloat16), "fsdp", scatter_dimension=0, tiled=True
        ).astype(jnp.float32),
        lax.psum_scatter(
            summed[2].astype(jnp.bfloat16), "fsdp", scatter_dimension=0, tiled=True
        ).astype(jnp.float32),
        lax.psum_scatter(
            summed[3].astype(jnp.bfloat16), "fsdp", scatter_dimension=1, tiled=True
        ).astype(jnp.float32),
        lax.psum_scatter(
            summed[4].astype(jnp.bfloat16), "fsdp", scatter_dimension=0, tiled=True
        ).astype(jnp.float32),
        lax.psum_scatter(
            summed[5].astype(jnp.bfloat16), "fsdp", scatter_dimension=0, tiled=True
        ).astype(jnp.float32),
        lax.psum_scatter(
            summed[6].astype(jnp.bfloat16), "fsdp", scatter_dimension=0, tiled=True
        ).astype(jnp.float32),
        lax.psum_scatter(
            summed[7].astype(jnp.bfloat16), "fsdp", scatter_dimension=0, tiled=True
        ).astype(jnp.float32),
        lax.psum_scatter(
            summed[8].astype(jnp.bfloat16), "fsdp", scatter_dimension=0, tiled=True
        ).astype(jnp.float32),
        lax.psum_scatter(
            summed[9].astype(jnp.bfloat16), "fsdp", scatter_dimension=0, tiled=True
        ).astype(jnp.float32),
        lax.psum_scatter(
            summed[10].astype(jnp.bfloat16), "fsdp", scatter_dimension=0, tiled=True
        ).astype(jnp.float32),
        lax.psum_scatter(
            summed[11].astype(jnp.bfloat16), "fsdp", scatter_dimension=0, tiled=True
        ).astype(jnp.float32),
        lax.psum_scatter(
            summed[12].astype(jnp.bfloat16), "fsdp", scatter_dimension=0, tiled=True
        ).astype(jnp.float32),
        lax.psum_scatter(
            summed[13].astype(jnp.bfloat16), "fsdp", scatter_dimension=0, tiled=True
        ).astype(jnp.float32),
    )
    totals = (
        lax.psum(shares[0].astype(jnp.bfloat16), "seq").astype(jnp.float32),
        lax.psum(shares[1].astype(jnp.bfloat16), "seq").astype(jnp.float32),
        lax.psum(shares[2].astype(jnp.bfloat16), "seq").astype(jnp.float32),
        lax.psum(shares[3].astype(jnp.bfloat16), "seq").astype(jnp.float32),
        lax.psum(shares[4].astype(jnp.bfloat16), "seq").astype(jnp.float32),
        lax.psum(shares[5].astype(jnp.bfloat16), "seq").astype(jnp.float32),
        lax.psum(shares[6].astype(jnp.bfloat16), "seq").astype(jnp.float32),
        lax.psum(shares[7].astype(jnp.bfloat16), "seq").astype(jnp.float32),
        lax.psum(shares[8].astype(jnp.bfloat16), "seq").astype(jnp.float32),
        lax.psum(shares[9].astype(jnp.bfloat16), "seq").astype(jnp.float32),
        lax.psum(shares[10].astype(jnp.bfloat16), "seq").astype(jnp.float32),
        lax.psum(shares[11].astype(jnp.bfloat16), "seq").astype(jnp.float32),
        lax.psum(shares[12].astype(jnp.bfloat16), "seq").astype(jnp.float32),
        lax.psum(shares[13].astype(jnp.bfloat16), "seq").astype(jnp.float32),
    )
    return (
        section_output,
        input_gradient,
        totals[0][None],
        totals[1][None],
        totals[2][None],
        totals[3][None],
        totals[4][None],
        totals[5][None],
        totals[6][None],
        totals[7][None],
        totals[8][None],
        totals[9][None],
        totals[10][None],
        totals[11][None],
        totals[12][None],
        totals[13][None],
    )


def solution(mesh):
    placed = (
        P(None, "fsdp", "seq", None),
        P(None, "fsdp", "seq", None),
        P(None, "fsdp"),
        P("section", "fsdp"),
        P("section", "fsdp"),
        P("section", "fsdp", None),
        P("section", None, "fsdp"),
        P("section", "fsdp", None),
        P("section", "fsdp"),
        P("section", "fsdp"),
        P("section", "fsdp"),
        P("section", "fsdp"),
        P("section", "fsdp", None),
        P("section", "fsdp"),
        P("section", "fsdp", None),
        P("section", "fsdp"),
        P("section", "fsdp"),
    )
    return jax.shard_map(
        body,
        mesh=mesh,
        in_specs=placed,
        out_specs=(
            P("section", None, "fsdp", "seq", None),
            P("section", None, "fsdp", "seq", None),
            P("section", "fsdp"),
            P("section", "fsdp"),
            P("section", "fsdp", None),
            P("section", None, "fsdp"),
            P("section", "fsdp", None),
            P("section", "fsdp"),
            P("section", "fsdp"),
            P("section", "fsdp"),
            P("section", "fsdp"),
            P("section", "fsdp", None),
            P("section", "fsdp"),
            P("section", "fsdp", None),
            P("section", "fsdp"),
            P("section", "fsdp"),
        ),
        check_vma=False,
    )
```

profile of v0, /device:TPU:0, one launch (start us, length us, event | category | flops | bytes accessed | tf_op | source)
XLA Modules:
  0.0 1621.7 jit_solution(16469395910346066690)
XLA Ops:
  10.0 9.5 all-gather.4
  19.6 8.0 all-gather.2
  27.7 7.1 all-gather.1
  35.3 47.5 %all-gather.19.cloned.1.call-done = bf16[1,1024,3072]{2,1,0:T(8,128)(2,1)} async-done(((bf16[1,256,3072]{2,1,0:T(8,128)(2,1)}), bf16[1,1024,3072]{2,1,0:T(8,128)(2,1)}) %all-gather.19.cloned.1.call-update) | async-done | bytes 6291472 | tf_op jit(solution)/shard_map/all_gather | solution.py:309
  101.9 35.8 %all-to-all-done = bf16[1,256,3,4,256]{4,1,2,0,3:T(8,128)(2,1)} async-done(((bf16[1,256,3,4,256]{4,1,2,0,3:T(8,128)(2,1)}), bf16[1,256,3,4,256]{4,1,2,0,3:T(8,128)(2,1)}, u32[]{:S(2)}, u32[]{:S(2)}) %all-to-all-start) | async-done | bytes 1572896 | tf_op jit(solution)/shard_map/all_to_all | solution.py:134
  168.9 8.0 all-gather
  176.8 7.6 all-gather.6
  184.4 8.3 all-gather.11
  192.7 7.2 all-gather.9
  199.9 8.0 all-gather.8
  207.9 7.2 all-gather.13
  215.1 8.0 all-gather.7
  228.2 15.4 fusion.59
  243.5 55.8 %all-gather.25.cloned.1.call-done = bf16[1,4096,1024]{2,1,0:T(8,128)(2,1)} async-done(((bf16[1,1024,1024]{2,1,0:T(8,128)(2,1)}), bf16[1,4096,1024]{2,1,0:T(8,128)(2,1)}) %all-gather.25.cloned.1.call-update) | async-done | bytes 8388624 | tf_op jit(solution)/shard_map/all_gather | solution.py:318
  329.5 35.6 %all-to-all-done.2 = bf16[1,256,3,4,256]{4,1,2,0,3:T(8,128)(2,1)} async-done(((bf16[1,256,3,4,256]{4,1,2,0,3:T(8,128)(2,1)}), bf16[1,256,3,4,256]{4,1,2,0,3:T(8,128)(2,1)}, u32[]{:S(2)}, u32[]{:S(2)}) %all-to-all-start.2) | async-done | bytes 1572896 | tf_op jit(solution)/shard_map/all_to_all | solution.py:134
  424.5 13.9 fusion.62
  438.5 8.6 fusion.310
  449.1 16.4 %convert_reduce_fusion.2 = (f32[4096]{0:T(1024)}, bf16[256,4096]{1,0:T(8,128)(2,1)S(1)}) fusion(bf16[1,4096,1024]{2,1,0:T(8,128)(2,1)} %all-gather.25.cloned.1.call-done, f32[]{:T(128)S(6)} %select_n.476, f32[1024]{0:T(1024)S(1)} %bitcast.986, pred[]{:T(512)} %eq.3, bf16[2,1,256,1024]{3,2,1,0:T(8,128)(2,1)S(1)} %copy-done.43, ...), kind=kOutput, calls=%fused_computation.122 | convolution fusion | flops 2227433472 | bytes 19420164 | tf_op jit(solution)/shard_map/isd,fd->isf/dot_general | solution.py:218
  488.7 10.7 all-to-all-done.6
  515.3 9.7 multiply_reduce_fusion.4
  525.0 9.9 multiply_convert_fusion.4
  570.5 48.2 %all-to-all-done.7 = bf16[1,1024,3,1,256]{4,2,3,0,1:T(4,128)(2,1)} async-done(((bf16[1,1024,3,1,256]{4,2,3,0,1:T(4,128)(2,1)}), bf16[1,1024,3,1,256]{4,2,3,0,1:T(4,128)(2,1)}, u32[]{:S(2)}, u32[]{:S(2)}) %all-to-all-start.7) | async-done | bytes 1572896 | tf_op jit(solution)/shard_map/all_to_all | solution.py:253
  624.2 7.1 fusion.302
  657.9 27.2 %all-to-all-done.4 = bf16[1,256,3,4,256]{4,1,2,0,3:T(8,128)(2,1)} async-done(((bf16[1,256,3,4,256]{4,1,2,0,3:T(8,128)(2,1)}), bf16[1,256,3,4,256]{4,1,2,0,3:T(8,128)(2,1)}, u32[]{:S(2)}, u32[]{:S(2)}) %all-to-all-start.4) | async-done | bytes 1572896 | tf_op jit(solution)/shard_map/all_to_all | solution.py:134
  737.0 15.7 fusion.65
  752.7 14.7 convert_reduce_fusion.1
  785.2 8.1 all-to-all-done.8
  809.7 10.2 multiply_reduce_fusion.2
  819.9 9.9 multiply_convert_fusion.2
  873.8 32.6 %all-to-all-done.9 = bf16[1,1024,3,1,256]{4,2,3,0,1:T(4,128)(2,1)} async-done(((bf16[1,1024,3,1,256]{4,2,3,0,1:T(4,128)(2,1)}), bf16[1,1024,3,1,256]{4,2,3,0,1:T(4,128)(2,1)}, u32[]{:S(2)}, u32[]{:S(2)}) %all-to-all-start.9) | async-done | bytes 1572896 | tf_op jit(solution)/shard_map/all_to_all | solution.py:253
  930.4 15.8 convert_reduce_fusion
  965.3 11.1 all-to-all-done.10
  997.4 10.2 multiply_reduce_fusion
  1007.6 8.7 multiply_convert_fusion
  1037.9 8.3 fusion.332
  1053.1 33.2 %all-to-all-done.11 = bf16[1,1024,3,1,256]{4,2,3,0,1:T(4,128)(2,1)} async-done(((bf16[1,1024,3,1,256]{4,2,3,0,1:T(4,128)(2,1)}), bf16[1,1024,3,1,256]{4,2,3,0,1:T(4,128)(2,1)}, u32[]{:S(2)}, u32[]{:S(2)}) %all-to-all-start.11) | async-done | bytes 1572896 | tf_op jit(solution)/shard_map/all_to_all | solution.py:253
  1089.8 12.9 add_convert_fusion.2
  1104.2 10.2 fusion.327
  1114.4 8.5 fusion.325
  1123.0 18.0 %add_convert_fusion.1 = bf16[1024,4096]{1,0:T(8,128)(2,1)} fusion(f32[1024,4096]{1,0:T(8,128)} %fusion.327, f32[1024,4096]{1,0:T(8,128)} %fusion.325, bf16[256,4096]{1,0:T(8,128)(2,1)} %copy-done.114, bf16[1,256,1024]{2,1,0:T(8,128)(2,1)} %copy-done.73, pred[]{:T(512)} %eq.3, f32[1,256,1024]{2,1,0:T(8,128)S(1)} %copy-done.6, f32[1024]{0:T(1024)S(1)} %bitcast.953, ...), kind=kOutput, calls=%fused_computation.1 | convolution fusion | flops 2161639424 | bytes 45623296 | tf_op jit(solution)/shard_map/isd,isf->df/dot_general | solution.py:224
  1142.2 10.8 fusion.186
  1153.0 8.2 fusion.184
  1161.2 15.8 add_convert_fusion
  1181.9 79.1 %reduce-scatter.12.cloned.1.call-done = bf16[256,4096]{1,0:T(8,128)(2,1)} async-done(((bf16[1024,4096]{1,0:T(8,128)(2,1)}), bf16[256,4096]{1,0:T(8,128)(2,1)}) %reduce-scatter.12.cloned.1.call-update) | async-done | bytes 2097168 | tf_op jit(solution)/shard_map/reduce_scatter | solution.py:418
  1261.0 89.5 %reduce-scatter.14.cloned.1.call-done = bf16[1024,1024]{1,0:T(8,128)(2,1)} async-done(((bf16[4096,1024]{1,0:T(8,128)(2,1)}), bf16[1024,1024]{1,0:T(8,128)(2,1)}) %reduce-scatter.14.cloned.1.call-update) | async-done | bytes 2097168 | tf_op jit(solution)/shard_map/reduce_scatter | solution.py:424
  1368.4 15.7 all-reduce.9
  1389.2 20.5 %all-reduce.10 = (bf16[1,256]{1,0:T(2,128)(2,1)S(1)}, bf16[1,256]{1,0:T(2,128)(2,1)S(1)}, bf16[1,2,256]{2,1,0:T(2,128)(2,1)S(1)}, bf16[1,256]{1,0:T(2,128)(2,1)S...) all-reduce(bf16[1,256]{1,0:T(2,128)(2,1)S(1)} %broadcast_in_dim.335, ...), channel_id=1, replica_groups=mesh['section'=2,'seq'=4,'fsdp'=4] {'seq'}, use_global_device_ids=true, to_apply=%region_58.59 | all-reduce | flops 3584 | bytes 14336 | tf_op jit(solution)/shard_map/psum | solution.py:435
  1415.4 189.7 %all-reduce.14.cloned.1.call-done = (bf16[1,256,3072]{2,1,0:T(8,128)(2,1)}, bf16[1,256,1024]{2,1,0:T(8,128)(2,1)}, bf16[1,256,4096]{2,1,0:T(8,128)(2,1)}, bf16[1,1024,1024]{2,1,0:T(8,128)(2,1)}) async-done(((bf16[1,256,3072]{2,1,0:T(8,128)(2,1)}, bf16[1,256,1024]{2,1,0:T(8,128)(2,1)}, bf16[1,256,4096]{2,1,0:T(8,128)(2,1)}, bf16[1,1024,1024]{2,1,0:T(8,128)(2,1)}), (bf16[1,256,3072]{2,1,0:T(8,128)(2,1)}, ...) | async-done | bytes 6291472 | tf_op jit(solution)/shard_map/psum | solution.py:437
  (849 shorter events, 521.1 us)
Async XLA Ops:
  7.2 75.6 %all-gather.19.cloned.1.call-start = ((), (), s32[]{:S(2)}) async-start(), calls=%async_computation.21 | async-start | bytes 7864320 | tf_op jit(solution)/shard_map/all_gather | solution.py:309
  8.0 216.0 %all-gather.21.cloned.1.call-start = ((), (), s32[]{:S(2)}) async-start(), calls=%async_computation.22 | async-start | bytes 2621440 | tf_op jit(solution)/shard_map/all_gather | solution.py:311
  8.7 219.5 %all-gather.23.cloned.1.call-start = ((), (), s32[]{:S(2)}) async-start(), calls=%async_computation.23 | async-start | bytes 10485760 | tf_op jit(solution)/shard_map/all_gather | solution.py:316
  9.4 289.9 %all-gather.25.cloned.1.call-start = ((), (), s32[]{:S(2)}) async-start(), calls=%async_computation.24 | async-start | bytes 10485760 | tf_op jit(solution)/shard_map/all_gather | solution.py:318
  27.6 282.2 %copy-start.132 = (f32[1,1024]{1,0:T(1,128)}, f32[1,1024]{1,0:T(1,128)S(1)}, u32[]{:S(2)}) copy-start(f32[1,1024]{1,0:T(1,128)S(1)} %convert_element_type.802) | copy-start | bytes 12292
  34.8 275.1 %copy-start.126 = (f32[1,1024]{1,0:T(1,128)}, f32[1,1024]{1,0:T(1,128)S(1)}, u32[]{:S(2)}) copy-start(f32[1,1024]{1,0:T(1,128)S(1)} %convert_element_type.801) | copy-start | bytes 12292
  35.0 274.9 %copy-start.183 = (f32[3072]{0:T(1024)}, f32[3072]{0:T(1024)S(1)}, u32[]{:S(2)}) copy-start(f32[3072]{0:T(1024)S(1)} %maximum_convert_fusion) | copy-start | bytes 36868
  95.7 42.0 %all-to-all-start = ((bf16[1,256,3,4,256]{4,1,2,0,3:T(8,128)(2,1)}), bf16[1,256,3,4,256]{4,1,2,0,3:T(8,128)(2,1)}, u32[]{:S(2)}, u32[]{:S(2)}) async-start(bf16[1,256,3,4,256]{4,1,2,0,3:T(8,128)(2,1)} %copy.116), calls=%async_computation | async-start | bytes 3145728 | tf_op jit(solution)/shard_map/all_to_all | solution.py:134
  159.1 56.0 %copy-start.222 = (bf16[1,256]{1,0:T(2,128)(2,1)S(1)}, bf16[1,256]{1,0:T(2,128)(2,1)}, u32[]{:S(2)}) copy-start(bf16[1,256]{1,0:T(2,128)(2,1)} %param.33) | copy-start | bytes 1540
  165.4 57.7 %all-to-all-start.1 = ((bf16[4,2,32768]{2,1,0:T(2,128)(2,1)}), bf16[4,2,32768]{2,1,0:T(2,128)(2,1)S(1)}, u32[]{:S(2)}, u32[]{:S(2)}) async-start(bf16[4,2,32768]{2,1,0:T(2,128)(2,1)} %reshape.2615), calls=%async_computation.1 | async-start | bytes 1048576 | tf_op jit(solution)/shard_map/all_to_all | solution.py:141
  184.4 235.7 %copy-start.137 = (f32[1,1024]{1,0:T(1,128)}, f32[1,1024]{1,0:T(1,128)S(1)}, u32[]{:S(2)}) copy-start(f32[1,1024]{1,0:T(1,128)S(1)} %convert_element_type.803) | copy-start | bytes 12292
  199.9 536.3 %copy-start.117 = (f32[1,1024]{1,0:T(1,128)}, f32[1,1024]{1,0:T(1,128)S(1)}, u32[]{:S(2)}) copy-start(f32[1,1024]{1,0:T(1,128)S(1)} %convert_element_type.806) | copy-start | bytes 12292
  215.1 223.3 %copy-start.211 = (f32[1,1024]{1,0:T(1,128)}, f32[1,1024]{1,0:T(1,128)S(1)}, u32[]{:S(2)}) copy-start(f32[1,1024]{1,0:T(1,128)S(1)} %convert_element_type.808) | copy-start | bytes 12292
  223.1 433.2 %copy-start.135 = (f32[1,1024]{1,0:T(1,128)}, f32[1,1024]{1,0:T(1,128)S(1)}, u32[]{:S(2)}) copy-start(f32[1,1024]{1,0:T(1,128)S(1)} %convert_element_type.804) | copy-start | bytes 12292
  227.9 192.3 %copy-start.2 = (f32[256,1024]{1,0:T(8,128)}, f32[256,1024]{1,0:T(8,128)S(1)}, u32[]{:S(2)}) copy-start(f32[256,1024]{1,0:T(8,128)S(1)} %get-tuple-element.199) | copy-start | bytes 3145732
  305.9 3.3 collective-permute-start
  309.4 339.2 %copy-start.9 = (bf16[1,256,1024]{2,1,0:T(8,128)(2,1)}, bf16[1,256,1024]{2,1,0:T(8,128)(2,1)S(1)}, u32[]{:S(2)}) copy-start(bf16[1,256,1024]{2,1,0:T(8,128)(2,1)S(1)} %get-tuple-element.197) | copy-start | bytes 1572868
  322.7 42.4 %all-to-all-start.2 = ((bf16[1,256,3,4,256]{4,1,2,0,3:T(8,128)(2,1)}), bf16[1,256,3,4,256]{4,1,2,0,3:T(8,128)(2,1)}, u32[]{:S(2)}, u32[]{:S(2)}) async-start(bf16[1,256,3,4,256]{4,1,2,0,3:T(8,128)(2,1)} %copy.120), calls=%async_computation.2 | async-start | bytes 3145728 | tf_op jit(solution)/shard_map/all_to_all | solution.py:134
  381.7 102.3 %copy-start.145 = (f32[4,512]{1,0:T(4,128)}, f32[4,512]{1,0:T(4,128)S(1)}, u32[]{:S(2)}) copy-start(f32[4,512]{1,0:T(4,128)S(1)} %log_add_fusion.2) | copy-start | bytes 24580
  383.9 100.2 %copy-start.147 = (f32[4,512]{1,0:T(4,128)}, f32[4,512]{1,0:T(4,128)S(1)}, u32[]{:S(2)}) copy-start(f32[4,512]{1,0:T(4,128)S(1)} %log_add_fusion.3) | copy-start | bytes 24580
  395.8 18.6 %all-to-all-start.3 = ((bf16[4,2,32768]{2,1,0:T(2,128)(2,1)}), bf16[4,2,32768]{2,1,0:T(2,128)(2,1)}, u32[]{:S(2)}, u32[]{:S(2)}) async-start(bf16[4,2,32768]{2,1,0:T(2,128)(2,1)} %reshape.2617), calls=%async_computation.3 | async-start | bytes 1048576 | tf_op jit(solution)/shard_map/all_to_all | solution.py:141
  424.1 307.1 %copy-start.5 = (f32[1,256,1024]{2,1,0:T(8,128)}, f32[1,256,1024]{2,1,0:T(8,128)S(1)}, u32[]{:S(2)}) copy-start(f32[1,256,1024]{2,1,0:T(8,128)S(1)} %get-tuple-element.195) | copy-start | bytes 3145732
  468.8 3.1 collective-permute-start.1
  470.8 179.9 %copy-start.178 = (f32[256]{0:T(256)}, f32[256]{0:T(256)S(1)}, u32[]{:S(2)}) copy-start(f32[256]{0:T(256)S(1)} %negate_multiply_fusion.11) | copy-start | bytes 3076
  473.2 175.4 %copy-start.22 = (bf16[1,256,1024]{2,1,0:T(8,128)(2,1)}, bf16[1,256,1024]{2,1,0:T(8,128)(2,1)S(1)}, u32[]{:S(2)}) copy-start(bf16[1,256,1024]{2,1,0:T(8,128)(2,1)S(1)} %get-tuple-element.272) | copy-start | bytes 1572868
  479.7 19.7 %all-to-all-start.6 = ((bf16[1,256,4,256]{3,1,0,2:T(8,128)(2,1)}), bf16[1,256,4,256]{3,1,0,2:T(8,128)(2,1)}, u32[]{:S(2)}, u32[]{:S(2)}) async-start(bf16[1,256,4,256]{3,1,0,2:T(8,128)(2,1)} %copy.128), calls=%async_computation.6 | async-start | bytes 1048576 | tf_op jit(solution)/shard_map/all_to_all | solution.py:245
  565.9 52.7 %all-to-all-start.7 = ((bf16[1,1024,3,1,256]{4,2,3,0,1:T(4,128)(2,1)}), bf16[1,1024,3,1,256]{4,2,3,0,1:T(4,128)(2,1)}, u32[]{:S(2)}, u32[]{:S(2)}) async-start(bf16[1,1024,3,1,256]{4,2,3,0,1:T(4,128)(2,1)} %pad_maximum_fusion), calls=%async_computation.7 | async-start | bytes 4194304 | tf_op jit(solution)/shard_map/all_to_all | solution.py:253
  570.4 53.8 %copy-start.13 = (bf16[2,1,256,1024]{3,2,1,0:T(8,128)(2,1)S(1)}, bf16[2,1,256,1024]{3,2,1,0:T(8,128)(2,1)}, u32[]{:S(2)}) copy-start(bf16[2,1,256,1024]{3,2,1,0:T(8,128)(2,1)} %param.17) | copy-start | bytes 3145732
  570.4 53.8 %copy-start.127 = (f32[1,1024]{1,0:T(1,128)S(1)}, f32[1,1024]{1,0:T(1,128)}, u32[]{:S(2)}) copy-start(f32[1,1024]{1,0:T(1,128)} %copy-done.126) | copy-start | bytes 12292
  570.4 60.9 %copy-start.193 = (f32[256]{0:T(256)}, f32[256]{0:T(256)S(1)}, u32[]{:S(2)}) copy-start(f32[256]{0:T(256)S(1)} %broadcast_multiply_fusion) | copy-start | bytes 3076
  570.5 60.9 %copy-start.169 = (f32[256]{0:T(256)}, f32[256]{0:T(256)S(1)}, u32[]{:S(2)}) copy-start(f32[256]{0:T(256)S(1)} %broadcast_multiply_fusion.7) | copy-start | bytes 3076
  644.2 40.9 %all-to-all-start.4 = ((bf16[1,256,3,4,256]{4,1,2,0,3:T(8,128)(2,1)}), bf16[1,256,3,4,256]{4,1,2,0,3:T(8,128)(2,1)}, u32[]{:S(2)}, u32[]{:S(2)}) async-start(bf16[1,256,3,4,256]{4,1,2,0,3:T(8,128)(2,1)} %copy.124), calls=%async_computation.4 | async-start | bytes 3145728 | tf_op jit(solution)/shard_map/all_to_all | solution.py:134
  650.7 209.2 %copy-start.189 = (f32[256]{0:T(256)}, f32[256]{0:T(256)S(1)}, u32[]{:S(2)}) copy-start(f32[256]{0:T(256)S(1)} %get-tuple-element.206) | copy-start | bytes 3076
  652.4 3.8 collective-permute-start.2
  712.0 17.6 %all-to-all-start.5 = ((bf16[4,2,32768]{2,1,0:T(2,128)(2,1)}), bf16[4,2,32768]{2,1,0:T(2,128)(2,1)S(1)}, u32[]{:S(2)}, u32[]{:S(2)}) async-start(bf16[4,2,32768]{2,1,0:T(2,128)(2,1)} %reshape.2619), calls=%async_computation.5 | async-start | bytes 1048576 | tf_op jit(solution)/shard_map/all_to_all | solution.py:141
  775.8 17.4 %all-to-all-start.8 = ((bf16[1,256,4,256]{3,1,0,2:T(8,128)(2,1)}), bf16[1,256,4,256]{3,1,0,2:T(8,128)(2,1)S(1)}, u32[]{:S(2)}, u32[]{:S(2)}) async-start(bf16[1,256,4,256]{3,1,0,2:T(8,128)(2,1)} %copy.135), calls=%async_computation.8 | async-start | bytes 1048576 | tf_op jit(solution)/shard_map/all_to_all | solution.py:245
  854.2 52.2 %all-to-all-start.9 = ((bf16[1,1024,3,1,256]{4,2,3,0,1:T(4,128)(2,1)}), bf16[1,1024,3,1,256]{4,2,3,0,1:T(4,128)(2,1)}, u32[]{:S(2)}, u32[]{:S(2)}) async-start(bf16[1,1024,3,1,256]{4,2,3,0,1:T(4,128)(2,1)} %pad_maximum_fusion.1), calls=%async_computation.9 | async-start | bytes 4194304 | tf_op jit(solution)/shard_map/all_to_all | solution.py:253
  918.7 5.0 collective-permute-start.3
  956.5 19.9 %all-to-all-start.10 = ((bf16[1,256,4,256]{3,1,0,2:T(8,128)(2,1)}), bf16[1,256,4,256]{3,1,0,2:T(8,128)(2,1)}, u32[]{:S(2)}, u32[]{:S(2)}) async-start(bf16[1,256,4,256]{3,1,0,2:T(8,128)(2,1)} %copy.142), calls=%async_computation.10 | async-start | bytes 1048576 | tf_op jit(solution)/shard_map/all_to_all | solution.py:245
  960.6 221.3 %reduce-scatter.10.cloned.1.call-start = ((), (), s32[]{:S(2)}) async-start(), calls=%async_computation.18 | async-start | bytes 2621440 | tf_op jit(solution)/shard_map/reduce_scatter | solution.py:403
  1033.1 53.2 %all-to-all-start.11 = ((bf16[1,1024,3,1,256]{4,2,3,0,1:T(4,128)(2,1)}), bf16[1,1024,3,1,256]{4,2,3,0,1:T(4,128)(2,1)}, u32[]{:S(2)}, u32[]{:S(2)}) async-start(bf16[1,1024,3,1,256]{4,2,3,0,1:T(4,128)(2,1)} %pad_maximum_fusion.2), calls=%async_computation.11 | async-start | bytes 4194304 | tf_op jit(solution)/shard_map/all_to_all | solution.py:253
  1037.6 144.3 %reduce-scatter.8.cloned.1.call-start = ((), (), s32[]{:S(2)}) async-start(), calls=%async_computation.17 | async-start | bytes 7864320 | tf_op jit(solution)/shard_map/reduce_scatter | solution.py:397
  1102.7 158.3 %reduce-scatter.12.cloned.1.call-start = ((), (), s32[]{:S(2)}) async-start(), calls=%async_computation.19 | async-start | bytes 10485760 | tf_op jit(solution)/shard_map/reduce_scatter | solution.py:418
  1141.0 209.5 %reduce-scatter.14.cloned.1.call-start = ((), (), s32[]{:S(2)}) async-start(), calls=%async_computation.20 | async-start | bytes 10485760 | tf_op jit(solution)/shard_map/reduce_scatter | solution.py:424
  1177.1 211.2 %reduce-scatter.16.cloned.1.call-start = ((), (), s32[]{:S(2)}) async-start(), calls=%async_computation.25 | async-start | bytes 327680
  1180.6 170.0 %copy-start.223 = (u32[32]{0:T(128)S(1)}, u32[32]{0:T(128)}, u32[]{:S(2)}) copy-start(u32[32]{0:T(128)} %constant.145) | copy-start | bytes 388
  1180.6 171.8 %copy-start.83 = (f32[256,1024]{1,0:T(8,128)S(1)}, f32[256,1024]{1,0:T(8,128)}, u32[]{:S(2)}) copy-start(f32[256,1024]{1,0:T(8,128)} %copy-done.82) | copy-start | bytes 3145732
  1181.8 423.2 %all-reduce.14.cloned.1.call-start = ((), (), s32[]{:S(2)}) async-start(), calls=%async_computation.26 | async-start | bytes 12582912 | tf_op jit(solution)/shard_map/psum | solution.py:437
  (223 other events, 2088.3 us)
Sparse Core Ops, SparseCore 0:
  9.9 72.8 all-gather.18
  84.7 35.3 all-gather.20
  121.9 88.0 all-gather.22
  211.7 87.6 all-gather.24
  965.4 36.1 reduce-scatter.9
  1102.8 68.3 reduce-scatter.7
  1174.5 86.3 reduce-scatter.11
  1264.0 86.4 reduce-scatter.13
  1354.0 24.0 reduce-scatter.15
  1380.6 224.3 all-reduce.13
where the time goes:
time: 1630 us; the launch traced here: 1620 us
  waiting for transfers between devices  720 us (44%)
  matrix products  439 us (27%)
  local copies, waits for them, and re-layouts  138 us (8%)
  other arithmetic  128 us (8%)
  blocking collectives  115 us (7%)
  starting transfers between devices  58.8 us (4%)
  between operations  23 us (1%)
    psum x1, waiting for transfers between devices, body(): lax.psum(shares[2].astype(jnp.bfloat16), 'seq').astype(jnp.float32)  190 us
    all_to_all x3, waiting for transfers between devices, layer_backward(): lax.all_to_all(stacked, 'seq', split_axis=1, concat_axis=3, tiled=True)  114 us
    all_to_all x3, waiting for transfers between devices, layer_forward(): lax.all_to_all(triple, 'seq', split_axis=3, concat_axis=1, tiled=True)  98.6 us
    reduce_scatter x1, waiting for transfers between devices, body(): lax.psum_scatter(summed[11].astype(jnp.bfloat16), 'fsdp', scatter_dimensi...  89.5 us
    reduce_scatter x1, waiting for transfers between devices, body(): lax.psum_scatter(summed[9].astype(jnp.bfloat16), 'fsdp', scatter_dimensio...  79.1 us
    all_gather x1, waiting for transfers between devices, body(): lax.all_gather(downweight[0], 'fsdp', axis=0, tiled=True)  55.8 us
    dot_general x6, matrix products, attend_backward(): jnp.einsum('iqhd,ikhd->ihqk', grad_block, value_heads, preferred_element_...  49.8 us
    all_gather x1, waiting for transfers between devices, body(): lax.all_gather(mixweight[0], 'fsdp', axis=0, tiled=True)  47.5 us
  transfers between devices with their start and end apart: 26, of which 18 were waited for; matrix products, arithmetic and copies ran while one was open for 19% of the time, Pallas kernels for 0%

commit v1 on v0

v1 whole, which is shorter than its diff:
```python
import math

import jax
import jax.numpy as jnp
from jax import lax
from jax.experimental import pallas as pl
from jax.experimental.pallas import tpu as pltpu
from jax.sharding import PartitionSpec as P

HEAD_DIM = 64
EPSILON = 1e-06
NEGATIVE = -1000000000.0
F32 = jnp.float32
BF16 = jnp.bfloat16
GROUP = 256
MIN_LENGTH = 896
CHUNK = 256
ROWS = 64
MIB = 1024 * 1024


def dot_nn(left, right):
    return lax.dot_general(left, right, (((1,), (0,)), ((), ())), preferred_element_type=F32)


def dot_nt(left, right):
    return lax.dot_general(left, right, (((1,), (1,)), ((), ())), preferred_element_type=F32)


def dot_tn(left, right):
    return lax.dot_general(left, right, (((0,), (0,)), ((), ())), preferred_element_type=F32)


def size_of(shape, dtype):
    return math.prod(shape) * jnp.dtype(dtype).itemsize


def run_kernel(body, name, ins, outs, scratch, flops, exps=0):
    spaces = {"v": pltpu.VMEM, "a": pl.ANY, "s": pltpu.SMEM}
    moved = sum(size_of(a.shape, a.dtype) for a, _ in ins) + sum(size_of(s, d) for s, d, _ in outs)
    held = sum(size_of(a.shape, a.dtype) for a, k in ins if k == "v")
    held += sum(size_of(s, d) for s, d, k in outs if k == "v")
    held += sum(size_of(s.shape, s.dtype) for s in scratch if s.memory_space == pltpu.VMEM)
    return pl.pallas_call(
        body,
        name=name,
        out_shape=[jax.ShapeDtypeStruct(s, d) for s, d, _ in outs],
        in_specs=[pl.BlockSpec(memory_space=spaces[k]) for _, k in ins],
        out_specs=[pl.BlockSpec(memory_space=spaces[k]) for _, _, k in outs],
        scratch_shapes=scratch,
        compiler_params=pltpu.CompilerParams(vmem_limit_bytes=min(held + 14 * MIB, 58 * MIB)),
        cost_estimate=pl.CostEstimate(flops=flops, bytes_accessed=moved, transcendentals=exps),
    )(*[a for a, _ in ins])


def start_all(pairs, sems, first=0):
    copies = []
    for index, (source, target) in enumerate(pairs):
        copies.append(pltpu.make_async_copy(source, target, sems.at[first + index]))
        copies[-1].start()
    return copies


def wait_all(copies):
    for copy in copies:
        copy.wait()


def block_rows(scal, k, rows):
    return pl.ds(pl.multiple_of((scal[0] ^ k) * rows, rows), rows)


def mix_pairs(scal, pieces, full, rows, count):
    return [
        (
            pieces[2 * k + h].at[t * rows : (t + 1) * rows, :],
            full.at[block_rows(scal, k, rows), (3 * h + t) * GROUP : (3 * h + t + 1) * GROUP],
        )
        for k in range(count)
        for h in range(2)
        for t in range(3)
    ]


def out_pairs(scal, pieces, full, rows, count):
    half = rows // 2
    return [
        (
            pieces[2 * k + h].at[3 * rows + j * half : 3 * rows + (j + 1) * half, :],
            full.at[block_rows(scal, k, half), (2 * h + j) * GROUP : (2 * h + j + 1) * GROUP],
        )
        for k in range(count)
        for h in range(2)
        for j in range(2)
    ]


def up_pairs(scal, pieces, full, rows, count):
    width = pieces[0].shape[1]
    return [
        (
            pieces[2 * k + h].at[j * rows : (j + 1) * rows, :],
            full.at[block_rows(scal, k, rows), (2 * h + j) * width : (2 * h + j + 1) * width],
        )
        for k in range(count)
        for h in range(2)
        for j in range(2)
    ]


def down_pairs(scal, pieces, full, rows, count):
    width = pieces[0].shape[1]
    return [
        (
            pieces[2 * k + h].at[2 * rows : 4 * rows, :],
            full.at[block_rows(scal, k, 2 * rows), h * width : (h + 1) * width],
        )
        for k in range(count)
        for h in range(2)
    ]


def norm_parts(values):
    center = jnp.mean(values, axis=-1, keepdims=True)
    centered = values - center
    spread = jnp.mean(centered * centered, axis=-1, keepdims=True)
    inverse = lax.rsqrt(spread + EPSILON)
    return centered * inverse, inverse


def norm_back(values, gain, grad):
    unit, inverse = norm_parts(values)
    scaled = grad * gain
    mean_one = jnp.mean(scaled, axis=-1, keepdims=True)
    mean_two = jnp.mean(scaled * unit, axis=-1, keepdims=True)
    return inverse * (scaled - mean_one - unit * mean_two), unit


def column_sum(values):
    return jnp.sum(values, axis=0, keepdims=True)


def gelu_pair(values):
    energy = jnp.exp(values * values * -0.5)
    t = 1.0 / (1.0 + (0.3275911 * 0.7071067811865476) * jnp.abs(values))
    tail = 1.061405429 * 0.5
    for factor in (-1.453152027, 1.421413741, -0.284496736, 0.254829592):
        tail = tail * t + factor * 0.5
    tail = tail * t * energy
    below = jnp.where(values >= 0, 1.0 - tail, tail)
    return values * below, below + values * energy * 0.3989422804014327


def mix_forward(params, hidden, gain, shift, bias, scal, pieces):
    rows, count = params
    tokens, width = hidden.shape
    span = 3 * GROUP

    def body(scal, hidden, gain, shift, bias, *rest):
        pieces, (normed, keep, send, full, sems) = rest[: 2 * count], rest[2 * count :]
        copies = start_all(mix_pairs(scal, pieces, full, rows, count), sems)

        @pl.loop(0, tokens // ROWS)
        def _(i):
            part = pl.ds(pl.multiple_of(i * ROWS, ROWS), ROWS)
            unit, _ = norm_parts(hidden[part, :].astype(F32))
            normed[part, :] = (unit * gain[...] + shift[...]).astype(BF16)

        wait_all(copies)
        for target, group in ((send, 1 - scal[1]), (keep, scal[1])):
            for t in range(3):
                columns = pl.ds(pl.multiple_of((group * 3 + t) * GROUP, GROUP), GROUP)
                made = dot_nn(normed[...], full[:, columns]) + bias[:, columns]
                target[:, t * GROUP : (t + 1) * GROUP] = made.astype(BF16)

    return run_kernel(
        body,
        "mix_forward",
        [(scal, "s"), (hidden, "v"), (gain, "v"), (shift, "v"), (bias, "v")]
        + [(p, "a") for p in pieces],
        [((tokens, width), BF16, "v"), ((tokens, span), BF16, "v"), ((tokens, span), BF16, "v")],
        [pltpu.VMEM((width, 2 * span), BF16), pltpu.SemaphoreType.DMA((6 * count,))],
        4 * tokens * width * span,
    )


def place_tokens(scal, keep, other, full, sems, first=0):
    tokens = keep.shape[0]
    own = pl.ds(pl.multiple_of(scal[1] * tokens, tokens), tokens)
    far = pl.ds(pl.multiple_of((1 - scal[1]) * tokens, tokens), tokens)
    return start_all([(keep, full.at[own, :]), (other, full.at[far, :])], sems, first)


def split_tokens(scal, full, keep, send, sems):
    tokens = keep.shape[0]
    own = pl.ds(pl.multiple_of(scal[1] * tokens, tokens), tokens)
    far = pl.ds(pl.multiple_of((1 - scal[1]) * tokens, tokens), tokens)
    wait_all(start_all([(full.at[far, :], send), (full.at[own, :], keep)], sems))


def masked(scores, length):
    start = MIN_LENGTH
    tail = scores[start:, :]
    position = lax.broadcasted_iota(jnp.int32, tail.shape, 0) + start
    return scores[:start, :], jnp.where(position < length, tail, NEGATIVE)


def attend_forward(keep, other, scal):
    tokens = keep.shape[0]
    total = 2 * tokens
    heads = GROUP // HEAD_DIM

    def body(scal, keep, other, out_keep, out_send, peaks, full, out, sems):
        wait_all(place_tokens(scal, keep, other, full, sems))
        length = scal[2]
        for pair in range(heads // 2):

            @pl.loop(0, total // CHUNK)
            def _(i):
                part = pl.ds(pl.multiple_of(i * CHUNK, CHUNK), CHUNK)
                outs = []
                for head in (2 * pair, 2 * pair + 1):
                    at = head * HEAD_DIM
                    query = full[part, at : at + HEAD_DIM] * jnp.asarray(HEAD_DIM**-0.5, BF16)
                    key = full[:, GROUP + at : GROUP + at + HEAD_DIM]
                    value = full[:, 2 * GROUP + at : 2 * GROUP + at + HEAD_DIM]
                    low, high = masked(dot_nt(key, query), length)
                    peak = jnp.maximum(
                        jnp.max(low, axis=0, keepdims=True), jnp.max(high, axis=0, keepdims=True)
                    )
                    low = jnp.exp(low - peak)
                    high = jnp.exp(high - peak)
                    mass = column_sum(low) + column_sum(high)
                    probs = jnp.concatenate([low.astype(BF16), high.astype(BF16)], axis=0)
                    outs.append(dot_tn(value, probs) / mass)
                    peaks[head : head + 1, part] = peak + jnp.log(mass)
                made = jnp.concatenate(outs, axis=0)
                out[part, pair * 128 : (pair + 1) * 128] = made.T.astype(BF16)

        split_tokens(scal, out, out_keep, out_send, sems)

    return run_kernel(
        body,
        "attend_forward",
        [(scal, "s"), (keep, "a"), (other, "a")],
        [
            ((tokens, GROUP), BF16, "a"),
            ((tokens, GROUP), BF16, "a"),
            ((8, total), F32, "v"),
        ],
        [
            pltpu.VMEM((total, 3 * GROUP), BF16),
            pltpu.VMEM((total, GROUP), BF16),
            pltpu.SemaphoreType.DMA((2,)),
        ],
        heads * total * total * HEAD_DIM * 4,
        heads * total * total,
    )


def place_groups(scal, keep, other, full, sems, first=0):
    width = keep.shape[1]
    own = pl.ds(pl.multiple_of(scal[1] * width, width), width)
    far = pl.ds(pl.multiple_of((1 - scal[1]) * width, width), width)
    return start_all([(keep, full.at[:, own]), (other, full.at[:, far])], sems, first)


def out_forward(params, keep, other, scal, pieces, width):
    rows, count = params
    tokens = keep.shape[0]
    inner = 2 * GROUP

    def body(scal, keep, other, *rest):
        pieces, (mixed, own, send, full, sems) = rest[: 2 * count], rest[2 * count :]
        copies = place_groups(scal, keep, other, mixed, sems)
        copies += start_all(out_pairs(scal, pieces, full, rows, count), sems, 2)
        wait_all(copies)
        for j in range(width // GROUP):
            columns = slice(j * GROUP, (j + 1) * GROUP)
            made = dot_nn(mixed[...], full[:, columns])
            own[:, columns] = made
            send[:, columns] = made.astype(BF16)

    return run_kernel(
        body,
        "out_forward",
        [(scal, "s"), (keep, "a"), (other, "a")] + [(p, "a") for p in pieces],
        [((tokens, inner), BF16, "v"), ((tokens, width), F32, "v"), ((tokens, width), BF16, "v")],
        [pltpu.VMEM((inner, width), BF16), pltpu.SemaphoreType.DMA((4 * count + 2,))],
        2 * tokens * inner * width,
    )


def feed_forward(params, hidden, own, other, vectors, upbias, scal, pieces):
    rows, count = params
    tokens, width = hidden.shape
    inner = upbias.shape[1]
    tile = 512

    def body(scal, hidden, own, other, vectors, upbias, *rest):
        pieces = rest[: 2 * count]
        branch, residual, normed, active, slope, made_own, made_send, up, down, sems = rest[
            2 * count :
        ]
        up_copies = start_all(up_pairs(scal, pieces, up, rows, count), sems)
        down_copies = start_all(down_pairs(scal, pieces, down, rows, count), sems, 4 * count)

        @pl.loop(0, tokens // ROWS)
        def _(i):
            part = pl.ds(pl.multiple_of(i * ROWS, ROWS), ROWS)
            made = own[part, :] + other[part, :].astype(F32) + vectors[0:1, :]
            branch[part, :] = made
            made = hidden[part, :].astype(F32) + vectors[1:2, :] * made
            residual[part, :] = made
            unit, _ = norm_parts(made)
            normed[part, :] = (unit * vectors[2:3, :] + vectors[3:4, :]).astype(BF16)

        wait_all(up_copies)

        @pl.loop(0, inner // tile)
        def _(i):
            columns = pl.ds(pl.multiple_of(i * tile, tile), tile)
            for r in range(tokens // 256):
                part = slice(r * 256, (r + 1) * 256)
                made = dot_nn(normed[part, :], up[:, columns]) + upbias[:, columns]
                value, gradient = gelu_pair(made)
                active[part, columns] = value.astype(BF16)
                slope[part, columns] = gradient.astype(BF16)

        wait_all(down_copies)

        @pl.loop(0, width // GROUP)
        def _(i):
            columns = pl.ds(pl.multiple_of(i * GROUP, GROUP), GROUP)
            made = dot_nn(active[...], down[:, columns])
            made_own[:, columns] = made
            made_send[:, columns] = made.astype(BF16)

    return run_kernel(
        body,
        "feed_forward",
        [(scal, "s"), (hidden, "v"), (own, "v"), (other, "v"), (vectors, "v"), (upbias, "v")]
        + [(p, "a") for p in pieces],
        [
            ((tokens, width), F32, "v"),
            ((tokens, width), F32, "v"),
            ((tokens, width), BF16, "v"),
            ((tokens, inner), BF16, "v"),
            ((tokens, inner), BF16, "v"),
            ((tokens, width), F32, "v"),
            ((tokens, width), BF16, "v"),
        ],
        [
            pltpu.VMEM((width, inner), BF16),
            pltpu.VMEM((inner, width), BF16),
            pltpu.SemaphoreType.DMA((6 * count,)),
        ],
        4 * tokens * width * inner,
        2 * tokens * inner,
    )


def feed_backward(params, incoming, feedscale, slope, scal, pieces):
    rows, count = params
    tokens, width = incoming.shape
    inner = slope.shape[1]
    tile = 512

    def body(scal, incoming, feedscale, slope, *rest):
        pieces = rest[: 2 * count]
        lower, up_grad, bias_grad, made_own, made_send, up, down, sems = rest[2 * count :]
        down_copies = start_all(down_pairs(scal, pieces, down, rows, count), sems)
        up_copies = start_all(up_pairs(scal, pieces, up, rows, count), sems, 2 * count)

        @pl.loop(0, tokens // ROWS)
        def _(i):
            part = pl.ds(pl.multiple_of(i * ROWS, ROWS), ROWS)
            lower[part, :] = (incoming[part, :].astype(F32) * feedscale[...]).astype(BF16)

        wait_all(down_copies)

        @pl.loop(0, inner // tile)
        def _(i):
            columns = pl.ds(pl.multiple_of(i * tile, tile), tile)
            made = dot_nt(lower[...], down[columns, :])
            made = (made * slope[:, columns].astype(F32)).astype(BF16)
            up_grad[:, columns] = made
            bias_grad[:, columns] = column_sum(made.astype(F32))

        wait_all(up_copies)

        @pl.loop(0, width // GROUP)
        def _(i):
            columns = pl.ds(pl.multiple_of(i * GROUP, GROUP), GROUP)
            made = dot_nt(up_grad[...], up[columns, :])
            made_own[:, columns] = made
            made_send[:, columns] = made.astype(BF16)

    return run_kernel(
        body,
        "feed_backward",
        [(scal, "s"), (incoming, "v"), (feedscale, "v"), (slope, "v")]
        + [(p, "a") for p in pieces],
        [
            ((tokens, width), BF16, "v"),
            ((tokens, inner), BF16, "v"),
            ((1, inner), F32, "v"),
            ((tokens, width), F32, "v"),
            ((tokens, width), BF16, "v"),
        ],
        [
            pltpu.VMEM((width, inner), BF16),
            pltpu.VMEM((inner, width), BF16),
            pltpu.SemaphoreType.DMA((6 * count,)),
        ],
        4 * tokens * width * inner,
    )


def feed_weights(params, active, lower, normed, up_grad, scal):
    rows, count = params
    tokens, width = lower.shape
    inner = active.shape[1]
    shape = (4 * rows, inner // 4)
    tile = 512

    def body(scal, active, lower, normed, up_grad, *rest):
        pieces, (up, down, sems) = rest[: 2 * count], rest[2 * count :]

        @pl.loop(0, inner // tile)
        def _(i):
            part = pl.ds(pl.multiple_of(i * tile, tile), tile)
            down[part, :] = dot_tn(active[:, part], lower[...]).astype(BF16)

        pairs = [(b, a) for a, b in down_pairs(scal, pieces, down, rows, count)]
        copies = start_all(pairs, sems)

        @pl.loop(0, inner // tile)
        def _(i):
            part = pl.ds(pl.multiple_of(i * tile, tile), tile)
            up[:, part] = dot_tn(normed[...], up_grad[:, part]).astype(BF16)

        pairs = [(b, a) for a, b in up_pairs(scal, pieces, up, rows, count)]
        wait_all(copies + start_all(pairs, sems, 2 * count))

    return run_kernel(
        body,
        "feed_weights",
        [(scal, "s"), (active, "v"), (lower, "v"), (normed, "v"), (up_grad, "v")],
        [(shape, BF16, "a")] * (2 * count),
        [
            pltpu.VMEM((width, inner), BF16),
            pltpu.VMEM((inner, width), BF16),
            pltpu.SemaphoreType.DMA((6 * count,)),
        ],
        4 * tokens * width * inner,
    )


def feed_sums(incoming, own, other, downbias, lower):
    tokens, width = incoming.shape

    def body(incoming, own, other, downbias, lower, sums):
        sums[...] = jnp.zeros_like(sums)

        @pl.loop(0, tokens // ROWS)
        def _(i):
            part = pl.ds(pl.multiple_of(i * ROWS, ROWS), ROWS)
            branch = own[part, :] + other[part, :].astype(F32) + downbias[...]
            sums[0:1, :] += column_sum(branch * incoming[part, :].astype(F32))
            sums[1:2, :] += column_sum(lower[part, :].astype(F32))

    return run_kernel(
        body,
        "feed_sums",
        [(incoming, "v"), (own, "v"), (other, "v"), (downbias, "v"), (lower, "v")],
        [((8, width), F32, "v")],
        [],
        4 * tokens * width,
    )[0]


def out_backward(params, incoming, residual, own, other, branch, vectors, scal, pieces):
    rows, count = params
    tokens, width = incoming.shape
    inner = 2 * GROUP

    def body(scal, incoming, residual, own, other, branch, vectors, *rest):
        pieces = rest[: 2 * count]
        residual_grad, branch_grad, keep, send, sums, full, sems = rest[2 * count :]
        copies = start_all(out_pairs(scal, pieces, full, rows, count), sems)
        sums[...] = jnp.zeros_like(sums)

        @pl.loop(0, tokens // ROWS)
        def _(i):
            part = pl.ds(pl.multiple_of(i * ROWS, ROWS), ROWS)
            grad = own[part, :] + other[part, :].astype(F32)
            back, unit = norm_back(residual[part, :], vectors[2:3, :], grad)
            sums[0:1, :] += column_sum(grad * unit)
            sums[1:2, :] += column_sum(grad)
            back = incoming[part, :].astype(F32) + back
            residual_grad[part, :] = back
            sums[2:3, :] += column_sum(back * branch[part, :])
            low = (back * vectors[1:2, :]).astype(BF16)
            branch_grad[part, :] = low
            sums[3:4, :] += column_sum(low.astype(F32))

        wait_all(copies)
        for target, group in ((send, 1 - scal[1]), (keep, scal[1])):
            part = pl.ds(pl.multiple_of(group * GROUP, GROUP), GROUP)
            target[...] = dot_nt(branch_grad[...], full[part, :]).astype(BF16)

    return run_kernel(
        body,
        "out_backward",
        [(scal, "s"), (incoming, "v"), (residual, "v"), (own, "v"), (other, "v"), (branch, "v")]
        + [(vectors, "v")]
        + [(p, "a") for p in pieces],
        [
            ((tokens, width), F32, "v"),
            ((tokens, width), BF16, "v"),
            ((tokens, GROUP), BF16, "v"),
            ((tokens, GROUP), BF16, "v"),
            ((8, width), F32, "v"),
        ],
        [pltpu.VMEM((inner, width), BF16), pltpu.SemaphoreType.DMA((4 * count,))],
        2 * tokens * inner * width,
    )


def attend_backward(keep, other, grad_keep, grad_other, peaks, scal):
    tokens = keep.shape[0]
    total = 2 * tokens
    heads = GROUP // HEAD_DIM

    def body(scal, keep, other, grad_keep, grad_other, peaks, out_keep, out_send, *rest):
        full, grads, out, key_sum, value_sum, sems = rest
        copies = place_tokens(scal, keep, other, full, sems)
        copies += place_tokens(scal, grad_keep, grad_other, grads, sems, 2)
        wait_all(copies)
        length = scal[2]
        for pair in range(heads // 2):
            key_sum[...] = jnp.zeros_like(key_sum)
            value_sum[...] = jnp.zeros_like(value_sum)

            @pl.loop(0, total // CHUNK)
            def _(i):
                part = pl.ds(pl.multiple_of(i * CHUNK, CHUNK), CHUNK)
                query_parts = []
                for side, head in enumerate((2 * pair, 2 * pair + 1)):
                    at = head * HEAD_DIM
                    query = full[part, at : at + HEAD_DIM] * jnp.asarray(HEAD_DIM**-0.5, BF16)
                    key = full[:, GROUP + at : GROUP + at + HEAD_DIM]
                    value = full[:, 2 * GROUP + at : 2 * GROUP + at + HEAD_DIM]
                    grad = grads[part, at : at + HEAD_DIM]
                    low, high = masked(dot_nt(key, query), length)
                    peak = peaks[head : head + 1, part]
                    probs = jnp.concatenate([jnp.exp(low - peak), jnp.exp(high - peak)], axis=0)
                    prob_grad = dot_nt(value, grad)
                    mean = column_sum(probs * prob_grad)
                    score_grad = (probs * (prob_grad - mean)).astype(BF16)
                    lanes = slice(side * HEAD_DIM, (side + 1) * HEAD_DIM)
                    value_sum[:, lanes] += dot_nn(probs.astype(BF16), grad)
                    key_sum[:, lanes] += dot_nn(score_grad, query)
                    query_parts.append(dot_tn(key, score_grad) * HEAD_DIM**-0.5)
                made = jnp.concatenate(query_parts, axis=0)
                out[part, pair * 128 : (pair + 1) * 128] = made.T.astype(BF16)

            at = pair * 128
            out[:, GROUP + at : GROUP + at + 128] = key_sum[...].astype(BF16)
            out[:, 2 * GROUP + at : 2 * GROUP + at + 128] = value_sum[...].astype(BF16)

        split_tokens(scal, out, out_keep, out_send, sems)

    return run_kernel(
        body,
        "attend_backward",
        [(scal, "s"), (keep, "a"), (other, "a"), (grad_keep, "a"), (grad_other, "a")]
        + [(peaks, "v")],
        [((tokens, 3 * GROUP), BF16, "a"), ((tokens, 3 * GROUP), BF16, "a")],
        [
            pltpu.VMEM((total, 3 * GROUP), BF16),
            pltpu.VMEM((total, GROUP), BF16),
            pltpu.VMEM((total, 3 * GROUP), BF16),
            pltpu.VMEM((total, 128), F32),
            pltpu.VMEM((total, 128), F32),
            pltpu.SemaphoreType.DMA((4,)),
        ],
        heads * total * total * HEAD_DIM * 10,
        heads * total * total,
    )


def mix_backward(params, keep, other, scal, pieces, width):
    rows, count = params
    tokens = keep.shape[0]
    inner = 6 * GROUP

    def body(scal, keep, other, *rest):
        pieces = rest[: 2 * count]
        triple, own, send, full, sems = rest[2 * count :]
        copies = place_groups(scal, keep, other, triple, sems)
        copies += start_all(mix_pairs(scal, pieces, full, rows, count), sems, 2)
        wait_all(copies)

        @pl.loop(0, width // GROUP)
        def _(i):
            columns = pl.ds(pl.multiple_of(i * GROUP, GROUP), GROUP)
            made = dot_nt(triple[...], full[columns, :])
            own[:, columns] = made
            send[:, columns] = made.astype(BF16)

    return run_kernel(
        body,
        "mix_backward",
        [(scal, "s"), (keep, "a"), (other, "a")] + [(p, "a") for p in pieces],
        [((tokens, inner), BF16, "v"), ((tokens, width), F32, "v"), ((tokens, width), BF16, "v")],
        [pltpu.VMEM((width, inner), BF16), pltpu.SemaphoreType.DMA((6 * count + 2,))],
        2 * tokens * inner * width,
    )


def mix_weights(params, normed, triple, mixed, branch_grad, scal):
    rows, count = params
    tokens, width = normed.shape
    inner = triple.shape[1]

    def body(scal, normed, triple, mixed, branch_grad, *rest):
        pieces, (sums, full, out, sems) = rest[: 2 * count], rest[2 * count :]
        out[...] = dot_tn(mixed[...], branch_grad[...]).astype(BF16)
        pairs = [(b, a) for a, b in out_pairs(scal, pieces, out, rows, count)]
        copies = start_all(pairs, sems)

        @pl.loop(0, inner // GROUP)
        def _(i):
            part = pl.ds(pl.multiple_of(i * GROUP, GROUP), GROUP)
            full[:, part] = dot_tn(normed[...], triple[:, part]).astype(BF16)
            sums[:, part] = column_sum(triple[:, part].astype(F32))

        pairs = [(b, a) for a, b in mix_pairs(scal, pieces, full, rows, count)]
        wait_all(copies + start_all(pairs, sems, 4 * count))

    return run_kernel(
        body,
        "mix_weights",
        [(scal, "s"), (normed, "v"), (triple, "v"), (mixed, "v"), (branch_grad, "v")],
        [((4 * rows, GROUP), BF16, "a")] * (2 * count) + [((1, inner), F32, "v")],
        [
            pltpu.VMEM((width, inner), BF16),
            pltpu.VMEM((2 * GROUP, width), BF16),
            pltpu.SemaphoreType.DMA((10 * count,)),
        ],
        2 * tokens * width * (inner + 2 * GROUP),
    )


def input_backward(hidden, own, other, residual_grad, gain):
    tokens, width = hidden.shape

    def body(hidden, own, other, residual_grad, gain, input_grad, low_grad, sums):
        sums[...] = jnp.zeros_like(sums)

        @pl.loop(0, tokens // ROWS)
        def _(i):
            part = pl.ds(pl.multiple_of(i * ROWS, ROWS), ROWS)
            grad = own[part, :] + other[part, :].astype(F32)
            back, unit = norm_back(hidden[part, :].astype(F32), gain[...], grad)
            sums[0:1, :] += column_sum(grad * unit)
            sums[1:2, :] += column_sum(grad)
            back = residual_grad[part, :] + back
            input_grad[part, :] = back
            low_grad[part, :] = back.astype(BF16)

    return run_kernel(
        body,
        "input_backward",
        [(hidden, "v"), (own, "v"), (other, "v"), (residual_grad, "v"), (gain, "v")],
        [((tokens, width), F32, "v"), ((tokens, width), BF16, "v"), ((8, width), F32, "v")],
        [],
        20 * tokens * width,
    )


def swap(value, axis, bit):
    count = lax.axis_size(axis)
    return lax.ppermute(value, axis, [(i, i ^ bit) for i in range(count)])


def add_low(left, right):
    return (left.astype(F32) + right.astype(F32)).astype(BF16)


def gather_blocks(halves, bits):
    places = [1 << i for i in range(len(bits))]
    held = {}
    for h, value in enumerate(halves):
        order = list(zip(bits, places))
        order = order if h == 0 else order[::-1]
        blocks = {0: value}
        for bit, place in order:
            for k in list(blocks):
                blocks[k ^ place] = swap(blocks[k], "fsdp", bit)
        for k in blocks:
            held[k, h] = blocks[k]
    return [held[k, h] for k in range(1 << len(bits)) for h in range(2)]


def scatter_blocks(pieces, bits):
    places = [1 << i for i in range(len(bits))]
    results = []
    for h in range(2):
        blocks = {k: pieces[2 * k + h] for k in range(1 << len(bits))}
        order = list(zip(bits, places))
        order = order if h == 0 else order[::-1]
        for bit, place in order:
            for k in [k for k in blocks if k & place]:
                blocks[k ^ place] = add_low(blocks[k ^ place], swap(blocks.pop(k), "fsdp", bit))
        results.append(blocks[0])
    return results


def sum_line(value):
    place = lax.axis_index("seq")
    near = add_low(value, lax.ppermute(value, "seq", [(0, 1), (3, 2)]))
    both = add_low(near, lax.ppermute(near, "seq", [(1, 2), (2, 1)]))
    back = lax.ppermute(both, "seq", [(1, 0), (2, 3)])
    return jnp.where((place == 1) | (place == 2), both, back)


def pick(flag, first, second):
    return jnp.where(flag, first, second)


def pack_mix(mix, out, side, count):
    rows, width = mix.shape[0], out.shape[1]
    split = mix.reshape(rows, 3, count, 2, width // (2 * count))[:, :, :, side]
    split = split.reshape(rows, 3, width // 2)
    half = out[side * rows // 2 : (side + 1) * rows // 2]
    return [
        jnp.concatenate(
            [split[:, t, h * GROUP : (h + 1) * GROUP] for t in range(3)]
            + [half[:, (2 * h + j) * GROUP : (2 * h + j + 1) * GROUP] for j in range(2)],
            axis=0,
        )
        for h in range(2)
    ]


def unpack_mix(sides, count):
    rows = sides[0][0].shape[0] // 4
    width = 4 * GROUP
    mixes, outs = [], []
    for halves in sides:
        parts = [
            jnp.concatenate([halves[h][t * rows : (t + 1) * rows] for h in range(2)], axis=1)
            for t in range(3)
        ]
        mixes.append(jnp.stack(parts, axis=1).reshape(rows, 3, count, width // (2 * count)))
        half = rows // 2
        outs.append(
            jnp.concatenate(
                [
                    halves[h][3 * rows + j * half : 3 * rows + (j + 1) * half]
                    for h in range(2)
                    for j in range(2)
                ],
                axis=1,
            )
        )
    return jnp.stack(mixes, axis=3).reshape(rows, 3 * width), jnp.concatenate(outs, axis=0)


def pack_feed(up, down, side, count):
    rows, inner = up.shape
    split = up.reshape(rows, count, 2, inner // (2 * count))[:, :, side].reshape(rows, inner // 2)
    half = down[side * 2 * rows : (side + 1) * 2 * rows]
    wide, narrow = inner // 8, down.shape[1] // 2
    return [
        jnp.concatenate(
            [split[:, (2 * h + j) * wide : (2 * h + j + 1) * wide] for j in range(2)]
            + [half[:, h * narrow : (h + 1) * narrow]],
            axis=0,
        )
        for h in range(2)
    ]


def unpack_feed(sides, count):
    rows = sides[0][0].shape[0] // 4
    ups, downs = [], []
    for halves in sides:
        up = jnp.concatenate(
            [halves[h][j * rows : (j + 1) * rows] for h in range(2) for j in range(2)], axis=1
        )
        ups.append(up.reshape(rows, count, up.shape[1] // count))
        downs.append(jnp.concatenate([halves[h][2 * rows :] for h in range(2)], axis=1))
    up = jnp.stack(ups, axis=2)
    return up.reshape(rows, -1), jnp.concatenate(downs, axis=0)


def body(activations, cotangent, lengths, *weights):
    mixgain, mixshift, mixweight, mixbias, outweight, outbias, mixscale = weights[:7]
    feedgain, feedshift, upweight, upbias, downweight, downbias, feedscale = weights[7:]
    core, line, spot = (lax.axis_index(a) for a in ("section", "seq", "fsdp"))
    first = core == 0
    parity, micro = line % 2, line // 2
    shards = lax.axis_size("fsdp")
    width = activations.shape[-1]
    inner = upbias.shape[1] * shards
    base_rows = width // shards

    joined, rows = 0, base_rows
    while rows // 2 < HEAD_DIM:
        joined, rows = joined + 1, rows * 2
    count = shards >> joined
    bits = [1 << (joined + i) for i in range(count.bit_length() - 1)]
    params = (rows, count)
    block = spot >> joined

    def join(value):
        for i in range(joined):
            far = swap(value, "fsdp", 1 << i)
            upper = ((spot >> i) & 1) == 1
            value = jnp.concatenate(
                [pick(upper, far, value), pick(upper, value, far)], axis=0
            )
        return value

    def unjoin(value):
        for i in reversed(range(joined)):
            half = value.shape[0] // 2
            upper = ((spot >> i) & 1) == 1
            low, high = value[:half], value[half:]
            value = add_low(pick(upper, high, low), swap(pick(upper, low, high), "fsdp", 1 << i))
        return value

    def spread(packs):
        sides = [packs(0), packs(1)]
        layers = [[], []]
        for h in range(2):
            keep = pick(first, sides[0][h], sides[1][h])
            far = swap(pick(first, sides[1][h], sides[0][h]), "section", 1)
            layers[0].append(pick(first, keep, far))
            layers[1].append(pick(first, far, keep))
        return layers

    mix_shard, out_shard = join(mixweight[0]), join(outweight[0])
    up_shard, down_shard = join(upweight[0]), join(downweight[0])
    mix_halves = spread(lambda side: pack_mix(mix_shard, out_shard, side, count))
    feed_halves = spread(lambda side: pack_feed(up_shard, down_shard, side, count))
    mix_pieces, feed_pieces = [], []
    for layer in range(2):
        mix_pieces.append(gather_blocks(mix_halves[layer], bits))
        feed_pieces.append(gather_blocks(feed_halves[layer], bits))

    packed = jnp.concatenate(
        [mixgain[0], mixshift[0], mixbias[0, 0], mixbias[0, 1], outbias[0], mixscale[0]]
        + [feedgain[0], feedshift[0], downbias[0], feedscale[0], upbias[0]]
    )
    packed = lax.all_gather(packed, ("section", "fsdp"), axis=0)
    packed = packed.reshape(2, shards, -1).astype(F32)

    def vector(layer, index):
        taken = packed[layer, :, index * base_rows : (index + 1) * base_rows]
        return taken.reshape(1, width)

    def half_vector(value):
        value = value.reshape(count, 2, -1)
        return pick(first, value[:, 0], value[:, 1]).reshape(1, -1)

    def mix_bias(layer):
        query = half_vector(vector(layer, 2)).reshape(2, 1, GROUP)
        value = half_vector(vector(layer, 3)).reshape(2, 1, GROUP)
        return jnp.concatenate([query, jnp.zeros_like(query), value], axis=1).reshape(1, -1)

    low_micro = micro == 0
    tokens = activations.shape[2]

    def to_pair(value):
        keep = pick(low_micro, value[0, 0], value[1, 0])
        far = swap(pick(low_micro, value[1, 0], value[0, 0]), "seq", 2)
        return jnp.concatenate([pick(low_micro, keep, far), pick(low_micro, far, keep)], axis=0)

    def from_pair(value):
        low, high = value[:tokens], value[tokens:]
        far = swap(pick(low_micro, high, low).astype(BF16), "seq", 2).astype(value.dtype)
        keep = pick(low_micro, low, high)
        return jnp.stack([pick(low_micro, keep, far), pick(low_micro, far, keep)])[None, :, None]

    length = pick(low_micro, lengths[0, 0], lengths[1, 0])
    scal = jnp.stack([block, parity, length]).astype(jnp.int32)

    hidden = to_pair(activations)
    incoming = to_pair(cotangent)
    kept, results = [], []
    for layer in range(2):
        pieces, feeds = mix_pieces[layer], feed_pieces[layer]
        normed, keep, send = mix_forward(
            params, hidden, vector(layer, 0), vector(layer, 1), mix_bias(layer), scal, pieces
        )
        other = swap(send, "seq", 1)
        out_keep, out_send, peaks = attend_forward(keep, other, scal)
        out_other = swap(out_send, "seq", 1)
        mixed, own, send = out_forward(params, out_keep, out_other, scal, pieces, width)
        far = swap(send, "section", 1)
        vectors = jnp.concatenate([vector(layer, i) for i in (4, 5, 6, 7)], axis=0)
        up_bias = half_vector(packed[layer, :, 10 * base_rows :].reshape(1, inner))
        branch, residual, normed_two, active, slope, own, send = feed_forward(
            params, hidden, own, far, vectors, up_bias, scal, feeds
        )
        far = swap(send, "section", 1)
        kept.append(
            (hidden, normed, keep, other, peaks, mixed, branch, residual, normed_two, active)
            + (slope, own, far, vectors)
        )
        made = own + far.astype(F32) + vector(layer, 8)
        hidden = (residual + vector(layer, 9) * made).astype(BF16)
        results.append(hidden)

    gradients, sums, mix_shares, feed_shares = [None] * 2, [None] * 2, [None] * 2, [None] * 2
    for layer in (1, 0):
        pieces, feeds = mix_pieces[layer], feed_pieces[layer]
        hidden, normed, keep, other, peaks, mixed, branch, residual, normed_two, active = kept[
            layer
        ][:10]
        slope, branch_own, branch_far, vectors = kept[layer][10:]
        lower, up_grad, up_sum, own, send = feed_backward(
            params, incoming, vector(layer, 9), slope, scal, feeds
        )
        far = swap(send, "section", 1)
        grads = feed_weights(params, active, lower, normed_two, up_grad, scal)
        feed_shares[layer] = [sum_line(v) for v in scatter_blocks(grads, bits)]
        feed_sum = feed_sums(incoming, branch_own, branch_far, vector(layer, 8), lower)
        residual_grad, branch_grad, grad_keep, grad_send, out_sum = out_backward(
            params, incoming, residual, own, far, branch, vectors, scal, pieces
        )
        grad_other = swap(grad_send, "seq", 1)
        triple_keep, triple_send = attend_backward(
            keep, other, grad_keep, grad_other, peaks, scal
        )
        triple_other = swap(triple_send, "seq", 1)
        triple, own, send = mix_backward(params, triple_keep, triple_other, scal, pieces, width)
        far = swap(send, "section", 1)
        *grads, mix_sum = mix_weights(params, normed, triple, mixed, branch_grad, scal)
        mix_shares[layer] = [sum_line(v) for v in scatter_blocks(grads, bits)]
        input_grad, incoming, in_sum = input_backward(
            hidden, own, far, residual_grad, vector(layer, 0)
        )
        gradients[layer] = input_grad
        mix_sum = mix_sum.reshape(2, 3, GROUP)
        sums[layer] = (
            jnp.concatenate([in_sum[:2], out_sum[:4], feed_sum[:2]], axis=0).reshape(-1),
            jnp.concatenate([up_sum.reshape(-1), mix_sum[:, 0].reshape(-1), mix_sum[:, 2].reshape(-1)]),
        )

    whole = pick(first, sums[0][0], sums[1][0])
    own_half = pick(first, sums[0][1], sums[1][1])
    far_half = swap(pick(first, sums[1][1], sums[0][1]), "section", 1)
    totals = jnp.concatenate(
        [whole, pick(first, own_half, far_half), pick(first, far_half, own_half)]
    ).reshape(-1, 128)
    for axis in ("fsdp", "seq"):
        bit = 1
        while bit < lax.axis_size(axis):
            totals = totals + swap(totals, axis, bit)
            bit *= 2
    totals = totals.reshape(-1)
    whole = totals[: 8 * width].reshape(8, width)
    halves = totals[8 * width :].reshape(2, -1)
    half = inner // 2
    up_total = jnp.stack([halves[s, :half].reshape(count, -1) for s in range(2)], axis=1)
    bias_total = jnp.stack(
        [halves[s, half:].reshape(2, count, -1) for s in range(2)], axis=2
    ).reshape(2, width)

    def own_part(value, size):
        return lax.dynamic_slice_in_dim(value, spot * size, size, axis=value.ndim - 1)

    whole = own_part(whole, base_rows)[:, None]
    up_total = own_part(up_total.reshape(inner), inner // shards)[None]
    bias_total = own_part(bias_total, base_rows)[None]

    def collect(shares):
        sides = [[], []]
        for h in range(2):
            early = lax.ppermute(shares[1][h], "section", [(0, 1)])
            late = lax.ppermute(shares[0][h], "section", [(1, 0)])
            sides[0].append(pick(first, shares[0][h], early))
            sides[1].append(pick(first, late, shares[1][h]))
        return sides

    mix_total, out_total = unpack_mix(collect(mix_shares), count)
    up_weight, down_weight = unpack_feed(collect(feed_shares), count)

    def final(value):
        return unjoin(value).astype(F32)[None]

    return (
        from_pair(pick(first, results[0], results[1])),
        from_pair(pick(first, gradients[0], gradients[1])),
        whole[0],
        whole[1],
        final(mix_total),
        bias_total,
        final(out_total),
        whole[5],
        whole[4],
        whole[2],
        whole[3],
        final(up_weight),
        up_total,
        final(down_weight),
        whole[7],
        whole[6],
    )


def solution(mesh):
    rowed, flat = P("section", "fsdp", None), P("section", "fsdp")
    image = P(None, "fsdp", "seq", None)
    bias = P("section", None, "fsdp")
    kept = P("section", None, "fsdp", "seq", None)
    params = (flat, flat, rowed, bias, rowed, flat, flat, flat, flat, rowed, flat, rowed, flat, flat)
    return jax.shard_map(
        body,
        mesh=mesh,
        in_specs=(image, image, P(None, "fsdp")) + params,
        out_specs=(kept, kept) + params,
        check_vma=False,
    )
```

time: 1630 us -> 985 us (0.60)
  matrix products: 439 us -> 0 us
  waiting for transfers between devices: 720 us -> 393 us
  Pallas kernels: 0 us -> 184 us
  blocking collectives: 115 us -> 23.5 us
  starting transfers between devices: 58.8 us -> 139 us
  other arithmetic: 128 us -> 90.9 us
  between operations: 23 us -> 5.02 us
    dot_general x78 -> x0, matrix products: 439 us -> none  [the longest x6 49.8 us: attend_backward(): jnp.einsum('iqhd,ikhd->ihqk', grad_block, value_heads, preferred_element_...]
    ppermute x4 -> x109, waiting for transfers between devices: 2.56 us -> 393 us  [the longest x77 279 us: swap(): return lax.ppermute(value, axis, [(i, i ^ bit) for i in range(count)])]
    all_to_all x12 -> x0, waiting for transfers between devices: 253 us -> none  [the longest x3 114 us: layer_backward(): lax.all_to_all(stacked, 'seq', split_axis=1, concat_axis=3, tiled=True)]
    psum x1 -> x0, waiting for transfers between devices: 190 us -> none  [body(): lax.psum(shares[2].astype(jnp.bfloat16), 'seq').astype(jnp.float32)]
    pallas_call x0 -> x24, Pallas kernels: none -> 184 us  [run_kernel(): pl.pallas_call(body, name=name, out_shape=[jax.ShapeDtypeStruct(s, d) for...]
    reduce_scatter x4 -> x0, waiting for transfers between devices: 169 us -> none  [the longest x1 89.5 us: body(): lax.psum_scatter(summed[11].astype(jnp.bfloat16), 'fsdp', scatter_dimensi...]
    ppermute x4 -> x109, starting transfers between devices: 6.61 us -> 139 us  [the longest x77 76.6 us: swap(): return lax.ppermute(value, axis, [(i, i ^ bit) for i in range(count)])]
    all_gather x4 -> x0, waiting for transfers between devices: 103 us -> none  [the longest x1 55.8 us: body(): lax.all_gather(downweight[0], 'fsdp', axis=0, tiled=True)]
  transfers between devices with their start and end apart: 26 -> 109, of which waited for: 18 -> 42; matrix products, arithmetic and copies ran while one was open for 19% -> 15% of each run, Pallas kernels for 0% -> 14%
where the time goes in v1:
time: 985 us; the launch traced here: 975 us
  waiting for transfers between devices  393 us (40%)
  Pallas kernels  184 us (19%)
  local copies, waits for them, and re-layouts  139 us (14%)
  starting transfers between devices  139 us (14%)
  other arithmetic  90.9 us (9%)
  blocking collectives  23.5 us (2%)
    ppermute x77, waiting for transfers between devices, swap(): return lax.ppermute(value, axis, [(i, i ^ bit) for i in range(count)])  279 us
    pallas_call x24, Pallas kernels, run_kernel(): pl.pallas_call(body, name=name, out_shape=[jax.ShapeDtypeStruct(s, d) for...  184 us
    ppermute x8, waiting for transfers between devices, sum_line(): back = lax.ppermute(both, 'seq', [(1, 0), (2, 3)])  87.1 us
    ppermute x77, starting transfers between devices, swap(): return lax.ppermute(value, axis, [(i, i ^ bit) for i in range(count)])  76.6 us
    unnamed x401, local copies, waits for them, and re-layouts  72 us
    convert_element_type x32, other arithmetic, add_low(): return (left.astype(F32) + right.astype(F32)).astype(BF16)  31.6 us
    ppermute x8, starting transfers between devices, sum_line(): near = add_low(value, lax.ppermute(value, 'seq', [(0, 1), (3, 2)]))  30.3 us
    select_n x27, other arithmetic, pick(): return jnp.where(flag, first, second)  29.1 us
  transfers between devices with their start and end apart: 109, of which 42 were waited for; matrix products, arithmetic and copies ran while one was open for 15% of the time, Pallas kernels for 14%

profile of v1, /device:TPU:0, one launch (start us, length us, event | category | flops | bytes accessed | tf_op | source)
XLA Modules:
  0.0 974.9 jit_solution(5277501467028609933)
XLA Ops:
  30.9 9.4 slice_reduce_fusion.1
  47.6 10.8 %dynamic-update-slice.23 = bf16[3584]{0:T(1024)(128)(2,1)S(1)} dynamic-update-slice(bf16[3584]{0:T(1024)(128)(2,1)S(1)} %dynamic-update-slice.22, bf16[256]{0:T(256)(128)(2,1)S(1)} %get-tuple-element.300, s32[]{} %constant.116) | dynamic-update-slice | bytes 1028
  59.9 23.5 %all-gather.1 = bf16[8,1,3584]{2,1,0:T(2,128)(2,1)S(1)} all-gather(bf16[1,1,3584]{2,1,0:T(2,128)(2,1)S(1)} %reshape.338), channel_id=2, replica_groups=mesh['section'=2,'seq'=4,'fsdp'=4] {'section','fsdp'}, dimensions={0}, use_global_device_ids=true | all-gather | bytes 64512 | tf_op jit(solution)/shard_map/all_gather | solution.py:860
  92.7 6.5 collective-permute-done.6.rest_5_
  115.1 7.9 collective-permute-done.8.rest_7_
  135.6 10.6 %collective-permute-done.9.other = bf16[512,768]{1,0:T(8,128)(2,1)S(1)} collective-permute-done((bf16[512,768]{1,0:T(8,128)(2,1)S(1)}, bf16[512,768]{1,0:T(8,128)(2,1)S(1)}, u32[]{:S(2)}, u32[]{:S(2)}) %collective-permute-start.9) | collective-permute-done | bytes 786464 | tf_op jit(solution)/shard_map/ppermute | solution.py:686
  146.3 13.7 %attend_forward.2 = (bf16[512,256]{1,0:T(8,128)(2,1)S(1)}, bf16[512,256]{1,0:T(8,128)(2,1)S(1)}, f32[8,1024]{1,0:T(8,128)S(1)}) custom-call(s32[3]{0:T(128)S(1)} %pad_add_fusion.scal, bf16[512,768]{1,0:T(8,128)(2,1)S(1)} %get-tuple-element.117.keep, bf16[512,768]{1,0:T(8,128)(2,1)S(1)} %collective-permute-done.9.other), custom_call_target="tpu_custom_call" | custom-call | flops 1073741824 | bytes 2129932 | tf_op jit(solution)/shard_map/attend_forward/pallas_call | solution.py:44
  171.1 16.7 %collective-permute-done.15.rest_3_ = bf16[1024,512]{1,0:T(8,128)(2,1)S(1)} collective-permute-done((bf16[1024,512]{1,0:T(8,128)(2,1)S(1)}, bf16[1024,512]{1,0:T(8,128)(2,1)S(1)}, u32[]{:S(2)}, u32[]{:S(2)}) %collective-permute-start.15) | collective-permute-done | bytes 1048608 | tf_op jit(solution)/shard_map/ppermute | solution.py:686
  189.8 16.1 %collective-permute-done.19.rest_7_ = bf16[1024,512]{1,0:T(8,128)(2,1)S(1)} collective-permute-done((bf16[1024,512]{1,0:T(8,128)(2,1)S(1)}, bf16[1024,512]{1,0:T(8,128)(2,1)S(1)}, u32[]{:S(2)}, u32[]{:S(2)}) %collective-permute-start.19) | collective-permute-done | bytes 1048608 | tf_op jit(solution)/shard_map/ppermute | solution.py:686
  207.4 17.1 %feed_forward.2 = (f32[512,1024]{1,0:T(8,128)S(1)}, f32[512,1024]{1,0:T(8,128)}, bf16[512,1024]{1,0:T(8,128)(2,1)S(1)}, bf16[512,2048]{1,0:T(8,128)(2,1)}, bf16[...) custom-call(s32[3]{0:T(128)S(1)} %pad_add_fusion.scal, ...), custom_call_target="tpu_custom_call" | custom-call | flops 4294967296 | bytes 25190412 | tf_op jit(solution)/shard_map/feed_forward/pallas_call | solution.py:44
  231.0 10.8 %collective-permute-done.24.rest_5_ = bf16[1024,256]{1,0:T(8,128)(2,1)} collective-permute-done((bf16[1024,256]{1,0:T(8,128)(2,1)S(1)}, bf16[1024,256]{1,0:T(8,128)(2,1)}, u32[]{:S(2)}, u32[]{:S(2)}) %collective-permute-start.24) | collective-permute-done | bytes 524320 | tf_op jit(solution)/shard_map/ppermute | solution.py:686
  248.0 5.5 collective-permute-done.22.rest_3_
  253.5 10.5 %collective-permute-done.26.rest_7_ = bf16[1024,256]{1,0:T(8,128)(2,1)} collective-permute-done((bf16[1024,256]{1,0:T(8,128)(2,1)}, bf16[1024,256]{1,0:T(8,128)(2,1)}, u32[]{:S(2)}, u32[]{:S(2)}) %collective-permute-start.26) | collective-permute-done | bytes 524320 | tf_op jit(solution)/shard_map/ppermute | solution.py:686
  272.1 27.1 %collective-permute-done.27.other = bf16[512,768]{1,0:T(8,128)(2,1)S(1)} collective-permute-done((bf16[512,768]{1,0:T(8,128)(2,1)S(1)}, bf16[512,768]{1,0:T(8,128)(2,1)S(1)}, u32[]{:S(2)}, u32[]{:S(2)}) %collective-permute-start.27) | collective-permute-done | bytes 786464 | tf_op jit(solution)/shard_map/ppermute | solution.py:686
  299.2 13.7 %attend_forward.3 = (bf16[512,256]{1,0:T(8,128)(2,1)S(1)}, bf16[512,256]{1,0:T(8,128)(2,1)S(1)}, f32[8,1024]{1,0:T(8,128)S(1)}) custom-call(s32[3]{0:T(128)S(1)} %pad_add_fusion.scal, bf16[512,768]{1,0:T(8,128)(2,1)S(1)} %get-tuple-element.126.keep, bf16[512,768]{1,0:T(8,128)(2,1)S(1)} %collective-permute-done.27.other), custom_call_target="tpu_custom_call" | custom-call | flops 1073741824 | bytes 2129932 | tf_op jit(solution)/shard_map/attend_forward/pallas_call | solution.py:44
  325.3 13.9 %collective-permute-done.31.rest_3_ = bf16[1024,512]{1,0:T(8,128)(2,1)S(1)} collective-permute-done((bf16[1024,512]{1,0:T(8,128)(2,1)S(1)}, bf16[1024,512]{1,0:T(8,128)(2,1)S(1)}, u32[]{:S(2)}, u32[]{:S(2)}) %collective-permute-start.31) | collective-permute-done | bytes 1048608 | tf_op jit(solution)/shard_map/ppermute | solution.py:686
  340.4 18.8 %collective-permute-done.35.rest_7_ = bf16[1024,512]{1,0:T(8,128)(2,1)S(1)} collective-permute-done((bf16[1024,512]{1,0:T(8,128)(2,1)S(1)}, bf16[1024,512]{1,0:T(8,128)(2,1)S(1)}, u32[]{:S(2)}, u32[]{:S(2)}) %collective-permute-start.35) | collective-permute-done | bytes 1048608 | tf_op jit(solution)/shard_map/ppermute | solution.py:686
  360.1 16.7 %feed_forward.3 = (f32[512,1024]{1,0:T(8,128)S(1)}, f32[512,1024]{1,0:T(8,128)}, bf16[512,1024]{1,0:T(8,128)(2,1)S(1)}, bf16[512,2048]{1,0:T(8,128)(2,1)}, bf16[...) custom-call(s32[3]{0:T(128)S(1)} %pad_add_fusion.scal, ...), custom_call_target="tpu_custom_call" | custom-call | flops 4294967296 | bytes 25190412 | tf_op jit(solution)/shard_map/feed_forward/pallas_call | solution.py:44
  379.8 9.1 feed_backward.2
  390.2 8.4 feed_weights.3
  416.7 5.4 out_backward.2
  422.1 9.6 collective-permute-done.88
  439.7 16.7 %attend_backward.2 = (bf16[512,768]{1,0:T(8,128)(2,1)S(1)}, bf16[512,768]{1,0:T(8,128)(2,1)S(1)}) custom-call(s32[3]{0:T(128)S(1)} %pad_add_fusion.scal, bf16[512,768]{1,0:T(8,128)(2,1)S(1)} %copy-done.111, bf16[512,768]{1,0:T(8,128)(2,1)S(1)} %copy-done.91, bf16[512,256]{1,0:T(8,128)(2,1)S(1)} %get-tuple-element.139.grad_keep, ...), custom_call_target="tpu_custom_call" | custom-call | flops 2684354560 | bytes 3702796 | tf_op jit(solution)/shard_map/attend_backward/pallas_call | solution.py:44
  465.9 12.1 %collective-permute-done.89 = bf16[1024,512]{1,0:T(8,128)(2,1)S(1)} collective-permute-done((bf16[1024,512]{1,0:T(8,128)(2,1)S(1)}, bf16[1024,512]{1,0:T(8,128)(2,1)S(1)}, u32[]{:S(2)}, u32[]{:S(2)}) %collective-permute-start.89) | collective-permute-done | bytes 1048608 | tf_op jit(solution)/shard_map/ppermute | solution.py:686
  484.1 6.0 mix_backward.2
  491.5 6.0 mix_weights.3
  503.9 6.7 collective-permute-done.60
  518.5 9.1 collective-permute-done.103
  535.3 8.0 feed_backward.3
  544.4 8.9 collective-permute-start.62
  555.0 8.3 feed_weights.2
  565.8 7.4 collective-permute-done.75
  583.0 6.4 collective-permute-done.82
  591.1 6.0 collective-permute-start.44
  601.4 21.7 %collective-permute-done.44.grad_other = bf16[512,256]{1,0:T(8,128)(2,1)S(1)} collective-permute-done((bf16[512,256]{1,0:T(8,128)(2,1)S(1)}, bf16[512,256]{1,0:T(8,128)(2,1)S(1)}, u32[]{:S(2)}, u32[]{:S(2)}) %collective-permute-start.44) | collective-permute-done | bytes 262176 | tf_op jit(solution)/shard_map/ppermute | solution.py:686
  624.8 16.7 %attend_backward.3 = (bf16[512,768]{1,0:T(8,128)(2,1)S(1)}, bf16[512,768]{1,0:T(8,128)(2,1)S(1)}) custom-call(s32[3]{0:T(128)S(1)} %pad_add_fusion.scal, bf16[512,768]{1,0:T(8,128)(2,1)S(1)} %copy-done.109, bf16[512,768]{1,0:T(8,128)(2,1)S(1)} %copy-done.89, bf16[512,256]{1,0:T(8,128)(2,1)S(1)} %get-tuple-element.152.grad_keep, ...), custom_call_target="tpu_custom_call" | custom-call | flops 2684354560 | bytes 3702796 | tf_op jit(solution)/shard_map/attend_backward/pallas_call | solution.py:44
  649.1 18.9 %collective-permute-done.105 = bf16[1024,512]{1,0:T(8,128)(2,1)S(1)} collective-permute-done((bf16[1024,512]{1,0:T(8,128)(2,1)S(1)}, bf16[1024,512]{1,0:T(8,128)(2,1)S(1)}, u32[]{:S(2)}, u32[]{:S(2)}) %collective-permute-start.105) | collective-permute-done | bytes 1048608 | tf_op jit(solution)/shard_map/ppermute | solution.py:726
  674.5 5.3 collective-permute-done.45.other
  705.0 7.2 collective-permute-done.54
  725.4 10.1 %collective-permute-done.97 = bf16[1024,512]{1,0:T(8,128)(2,1)S(1)} collective-permute-done((bf16[1024,512]{1,0:T(8,128)(2,1)S(1)}, bf16[1024,512]{1,0:T(8,128)(2,1)S(1)}, u32[]{:S(2)}, u32[]{:S(2)}) %collective-permute-start.97) | collective-permute-done | bytes 1048608 | tf_op jit(solution)/shard_map/ppermute | solution.py:724
  748.8 5.6 collective-permute-start.56
  755.6 6.8 collective-permute-done.51
  766.7 17.0 %collective-permute-done.52 = f32[112,128]{1,0:T(8,128)S(1)} collective-permute-done((f32[112,128]{1,0:T(8,128)S(1)}, f32[112,128]{1,0:T(8,128)S(1)}, u32[]{:S(2)}, u32[]{:S(2)}) %collective-permute-start.52) | collective-permute-done | bytes 57376 | tf_op jit(solution)/shard_map/ppermute | solution.py:686
  789.9 12.9 %collective-permute-done.47 = bf16[256,1024]{1,0:T(8,128)(2,1)S(1)} collective-permute-done((bf16[256,1024]{1,0:T(8,128)(2,1)}, bf16[256,1024]{1,0:T(8,128)(2,1)S(1)}, u32[]{:S(2)}, u32[]{:S(2)}) %collective-permute-start.47) | collective-permute-done | bytes 524320 | tf_op jit(solution)/shard_map/ppermute | solution.py:686
  819.8 36.9 %collective-permute-done.58 = bf16[1024,256]{1,0:T(8,128)(2,1)S(1)} collective-permute-done((bf16[1024,256]{1,0:T(8,128)(2,1)S(1)}, bf16[1024,256]{1,0:T(8,128)(2,1)S(1)}, u32[]{:S(2)}, u32[]{:S(2)}) %collective-permute-start.58) | collective-permute-done | bytes 524320 | tf_op jit(solution)/shard_map/ppermute | solution.py:726
  861.0 29.5 %collective-permute-done.71 = bf16[1024,256]{1,0:T(8,128)(2,1)S(1)} collective-permute-done((bf16[1024,256]{1,0:T(8,128)(2,1)S(1)}, bf16[1024,256]{1,0:T(8,128)(2,1)S(1)}, u32[]{:S(2)}, u32[]{:S(2)}) %collective-permute-start.71) | collective-permute-done | bytes 524320 | tf_op jit(solution)/shard_map/ppermute | solution.py:726
  960.0 5.3 copy.146
  965.4 5.7 copy.150
  (786 shorter events, 387.0 us)
Async XLA Ops:
  20.3 64.1 %collective-permute-start.2 = (bf16[1024,256]{1,0:T(8,128)(2,1)}, bf16[1024,256]{1,0:T(8,128)(2,1)}, u32[]{:S(2)}, u32[]{:S(2)}) collective-permute-start(bf16[1024,256]{1,0:T(8,128)(2,1)} %broadcast_select_fusion.28), channel_id=1, source_target_pairs={{0,16},{16,0},{1,17},{17,1},{2,18},{18,2},{3,19},{19,3},{4,20},{20... | collective-permute-start | bytes 1572872 | tf_op jit(solution)/shard_map/ppermute | solution.py:686
  21.6 65.5 %collective-permute-start.1 = (bf16[1024,256]{1,0:T(8,128)(2,1)}, bf16[1024,256]{1,0:T(8,128)(2,1)}, u32[]{:S(2)}, u32[]{:S(2)}) collective-permute-start(bf16[1024,256]{1,0:T(8,128)(2,1)} %broadcast_select_fusion.31), channel_id=1, source_target_pairs={{0,16},{16,0},{1,17},{17,1},{2,18},{18,2},{3,19},{19,3},{4,20},{20... | collective-permute-start | bytes 1572872 | tf_op jit(solution)/shard_map/ppermute | solution.py:686
  23.5 67.7 %collective-permute-start = (bf16[256,1024]{1,0:T(8,128)(2,1)}, bf16[256,1024]{1,0:T(8,128)(2,1)}, u32[]{:S(2)}, u32[]{:S(2)}) collective-permute-start(bf16[256,1024]{1,0:T(8,128)(2,1)} %select_bitcast_fusion.3), channel_id=1, source_target_pairs={{0,8},{4,12},{8,0},{12,4},{1,9},{5,13},{9,1},{13,5},{2,10},{6,14},... | collective-permute-start | bytes 1572872 | tf_op jit(solution)/shard_map/ppermute | solution.py:686
  44.7 59.2 %collective-permute-start.13 = (bf16[1024,512]{1,0:T(8,128)(2,1)}, bf16[1024,512]{1,0:T(8,128)(2,1)}, u32[]{:S(2)}, u32[]{:S(2)}) collective-permute-start(bf16[1024,512]{1,0:T(8,128)(2,1)} %broadcast_select_fusion.11), channel_id=1, source_target_pairs={{0,16},{16,0},{1,17},{17,1},{2,18},{18,2},{3,19},{19,3},{4,20},{20... | collective-permute-start | bytes 3145736 | tf_op jit(solution)/shard_map/ppermute | solution.py:686
  46.1 86.4 %collective-permute-start.12 = (bf16[1024,512]{1,0:T(8,128)(2,1)}, bf16[1024,512]{1,0:T(8,128)(2,1)}, u32[]{:S(2)}, u32[]{:S(2)}) collective-permute-start(bf16[1024,512]{1,0:T(8,128)(2,1)} %broadcast_select_fusion.14), channel_id=1, source_target_pairs={{0,16},{16,0},{1,17},{17,1},{2,18},{18,2},{3,19},{19,3},{4,20},{20... | collective-permute-start | bytes 3145736 | tf_op jit(solution)/shard_map/ppermute | solution.py:686
  114.5 49.3 %collective-permute-start.17 = (bf16[1024,512]{1,0:T(8,128)(2,1)S(1)}, bf16[1024,512]{1,0:T(8,128)(2,1)S(1)}, u32[]{:S(2)}, u32[]{:S(2)}) collective-permute-start(bf16[1024,512]{1,0:T(8,128)(2,1)S(1)} %get-tuple-element.311.rest_1_), channel_id=1, source_target_pairs={{0,2},{1,3},{2,0},{3,1},{4,6},{5,7},{6,4},{7,5},{8,10},{9,11},{10,... | collective-permute-start | bytes 3145736 | tf_op jit(solution)/shard_map/ppermute | solution.py:686
  163.9 42.0 %collective-permute-start.19 = (bf16[1024,512]{1,0:T(8,128)(2,1)S(1)}, bf16[1024,512]{1,0:T(8,128)(2,1)S(1)}, u32[]{:S(2)}, u32[]{:S(2)}) collective-permute-start(bf16[1024,512]{1,0:T(8,128)(2,1)S(1)} %collective-permute-done.17.rest_5_), channel_id=1, source_target_pairs={{0,1},{1,0},{2,3},{3,2},{4,5},{5,4},{6,7},{7,6},{8,9},{9,8},{10,11... | collective-permute-start | bytes 3145736 | tf_op jit(solution)/shard_map/ppermute | solution.py:686
  165.6 41.7 %collective-permute-start.18 = (bf16[1024,512]{1,0:T(8,128)(2,1)S(1)}, bf16[1024,512]{1,0:T(8,128)(2,1)S(1)}, u32[]{:S(2)}, u32[]{:S(2)}) collective-permute-start(bf16[1024,512]{1,0:T(8,128)(2,1)S(1)} %collective-permute-done.14.rest_2_), channel_id=1, source_target_pairs={{0,2},{1,3},{2,0},{3,1},{4,6},{5,7},{6,4},{7,5},{8,10},{9,11},{10,... | collective-permute-start | bytes 3145736 | tf_op jit(solution)/shard_map/ppermute | solution.py:686
  170.3 37.1 %collective-permute-start.11 = (bf16[512,1024]{1,0:T(8,128)(2,1)S(1)}, bf16[512,1024]{1,0:T(8,128)(2,1)S(1)}, u32[]{:S(2)}, u32[]{:S(2)}) collective-permute-start(bf16[512,1024]{1,0:T(8,128)(2,1)S(1)} %get-tuple-element.122), channel_id=1, source_target_pairs={{0,16},{16,0},{1,17},{17,1},{2,18},{18,2},{3,19},{19,3},{4,20},{20... | collective-permute-start | bytes 3145736 | tf_op jit(solution)/shard_map/ppermute | solution.py:686
  269.4 44.9 %collective-permute-start.33 = (bf16[1024,512]{1,0:T(8,128)(2,1)S(1)}, bf16[1024,512]{1,0:T(8,128)(2,1)S(1)}, u32[]{:S(2)}, u32[]{:S(2)}) collective-permute-start(bf16[1024,512]{1,0:T(8,128)(2,1)S(1)} %copy-done.46), channel_id=1, source_target_pairs={{0,2},{1,3},{2,0},{3,1},{4,6},{5,7},{6,4},{7,5},{8,10},{9,11},{10,... | collective-permute-start | bytes 3145736 | tf_op jit(solution)/shard_map/ppermute | solution.py:686
  271.0 44.2 %collective-permute-start.30 = (bf16[1024,512]{1,0:T(8,128)(2,1)S(1)}, bf16[1024,512]{1,0:T(8,128)(2,1)S(1)}, u32[]{:S(2)}, u32[]{:S(2)}) collective-permute-start(bf16[1024,512]{1,0:T(8,128)(2,1)S(1)} %copy-done.47), channel_id=1, source_target_pairs={{0,1},{1,0},{2,3},{3,2},{4,5},{5,4},{6,7},{7,6},{8,9},{9,8},{10,11... | collective-permute-start | bytes 3145736 | tf_op jit(solution)/shard_map/ppermute | solution.py:686
  271.7 52.1 %collective-permute-start.38 = (bf16[256,1024]{1,0:T(8,128)(2,1)S(1)}, bf16[256,1024]{1,0:T(8,128)(2,1)S(1)}, u32[]{:S(2)}, u32[]{:S(2)}) collective-permute-start(bf16[256,1024]{1,0:T(8,128)(2,1)S(1)} %select_bitcast_fusion), channel_id=1, source_target_pairs={{0,8},{4,12},{8,0},{12,4},{1,9},{5,13},{9,1},{13,5},{2,10},{6,14},... | collective-permute-start | bytes 1572872 | tf_op jit(solution)/shard_map/ppermute | solution.py:686
  315.2 44.1 %collective-permute-start.35 = (bf16[1024,512]{1,0:T(8,128)(2,1)S(1)}, bf16[1024,512]{1,0:T(8,128)(2,1)S(1)}, u32[]{:S(2)}, u32[]{:S(2)}) collective-permute-start(bf16[1024,512]{1,0:T(8,128)(2,1)S(1)} %collective-permute-done.33.rest_5_), channel_id=1, source_target_pairs={{0,1},{1,0},{2,3},{3,2},{4,5},{5,4},{6,7},{7,6},{8,9},{9,8},{10,11... | collective-permute-start | bytes 3145736 | tf_op jit(solution)/shard_map/ppermute | solution.py:686
  319.9 40.2 %collective-permute-start.34 = (bf16[1024,512]{1,0:T(8,128)(2,1)S(1)}, bf16[1024,512]{1,0:T(8,128)(2,1)S(1)}, u32[]{:S(2)}, u32[]{:S(2)}) collective-permute-start(bf16[1024,512]{1,0:T(8,128)(2,1)S(1)} %collective-permute-done.30.rest_2_), channel_id=1, source_target_pairs={{0,2},{1,3},{2,0},{3,1},{4,6},{5,7},{6,4},{7,5},{8,10},{9,11},{10,... | collective-permute-start | bytes 3145736 | tf_op jit(solution)/shard_map/ppermute | solution.py:686
  323.8 36.3 %collective-permute-start.29 = (bf16[512,1024]{1,0:T(8,128)(2,1)S(1)}, bf16[512,1024]{1,0:T(8,128)(2,1)S(1)}, u32[]{:S(2)}, u32[]{:S(2)}) collective-permute-start(bf16[512,1024]{1,0:T(8,128)(2,1)S(1)} %get-tuple-element.131), channel_id=1, source_target_pairs={{0,16},{16,0},{1,17},{17,1},{2,18},{18,2},{3,19},{19,3},{4,20},{20... | collective-permute-start | bytes 3145736 | tf_op jit(solution)/shard_map/ppermute | solution.py:686
  406.7 59.2 %collective-permute-start.87 = (bf16[1024,512]{1,0:T(8,128)(2,1)}, bf16[1024,512]{1,0:T(8,128)(2,1)S(1)}, u32[]{:S(2)}, u32[]{:S(2)}) collective-permute-start(bf16[1024,512]{1,0:T(8,128)(2,1)} %copy-done.86), channel_id=1, source_target_pairs={{0,1},{1,0},{2,3},{3,2},{4,5},{5,4},{6,7},{7,6},{8,9},{9,8},{10,11... | collective-permute-start | bytes 3145736 | tf_op jit(solution)/shard_map/ppermute | solution.py:686
  407.8 48.6 %collective-permute-start.101 = (bf16[1024,512]{1,0:T(8,128)(2,1)}, bf16[1024,512]{1,0:T(8,128)(2,1)S(1)}, u32[]{:S(2)}, u32[]{:S(2)}) collective-permute-start(bf16[1024,512]{1,0:T(8,128)(2,1)} %copy-done.87), channel_id=1, source_target_pairs={{0,2},{1,3},{2,0},{3,1},{4,6},{5,7},{6,4},{7,5},{8,10},{9,11},{10,... | collective-permute-start | bytes 3145736 | tf_op jit(solution)/shard_map/ppermute | solution.py:686
  408.7 91.0 %collective-permute-start.100 = (bf16[1024,512]{1,0:T(8,128)(2,1)}, bf16[1024,512]{1,0:T(8,128)(2,1)S(1)}, u32[]{:S(2)}, u32[]{:S(2)}) collective-permute-start(bf16[1024,512]{1,0:T(8,128)(2,1)} %copy-done.85), channel_id=1, source_target_pairs={{0,2},{1,3},{2,0},{3,1},{4,6},{5,7},{6,4},{7,5},{8,10},{9,11},{10,... | collective-permute-start | bytes 3145736 | tf_op jit(solution)/shard_map/ppermute | solution.py:686
  434.9 43.1 %collective-permute-start.89 = (bf16[1024,512]{1,0:T(8,128)(2,1)S(1)}, bf16[1024,512]{1,0:T(8,128)(2,1)S(1)}, u32[]{:S(2)}, u32[]{:S(2)}) collective-permute-start(bf16[1024,512]{1,0:T(8,128)(2,1)S(1)} %add_convert_fusion.13), channel_id=1, source_target_pairs={{0,2},{1,3},{2,0},{3,1},{4,6},{5,7},{6,4},{7,5},{8,10},{9,11},{10,... | collective-permute-start | bytes 3145736 | tf_op jit(solution)/shard_map/ppermute | solution.py:686
  463.8 36.0 %collective-permute-start.102 = (bf16[1024,512]{1,0:T(8,128)(2,1)S(1)}, bf16[1024,512]{1,0:T(8,128)(2,1)S(1)}, u32[]{:S(2)}, u32[]{:S(2)}) collective-permute-start(bf16[1024,512]{1,0:T(8,128)(2,1)S(1)} %add_convert_fusion.3), channel_id=1, source_target_pairs={{0,1},{1,0},{2,3},{3,2},{4,5},{5,4},{6,7},{7,6},{8,9},{9,8},{10,11... | collective-permute-start | bytes 3145736 | tf_op jit(solution)/shard_map/ppermute | solution.py:686
  479.5 36.1 %collective-permute-start.90 = (bf16[1024,512]{1,0:T(8,128)(2,1)}, bf16[1024,512]{1,0:T(8,128)(2,1)}, u32[]{:S(2)}, u32[]{:S(2)}) collective-permute-start(bf16[1024,512]{1,0:T(8,128)(2,1)} %add_convert_fusion.12), channel_id=1, source_target_pairs={{0,4},{12,8},{1,5},{13,9},{2,6},{14,10},{3,7},{15,11},{16,20},{28,... | collective-permute-start | bytes 3145736 | tf_op jit(solution)/shard_map/ppermute | solution.py:724
  510.6 32.7 %collective-permute-start.59 = (bf16[1024,256]{1,0:T(8,128)(2,1)}, bf16[1024,256]{1,0:T(8,128)(2,1)S(1)}, u32[]{:S(2)}, u32[]{:S(2)}) collective-permute-start(bf16[1024,256]{1,0:T(8,128)(2,1)} %copy-done.101), channel_id=1, source_target_pairs={{0,1},{1,0},{2,3},{3,2},{4,5},{5,4},{6,7},{7,6},{8,9},{9,8},{10,11... | collective-permute-start | bytes 1572872 | tf_op jit(solution)/shard_map/ppermute | solution.py:686
  513.0 40.4 %collective-permute-start.72 = (bf16[1024,256]{1,0:T(8,128)(2,1)}, bf16[1024,256]{1,0:T(8,128)(2,1)S(1)}, u32[]{:S(2)}, u32[]{:S(2)}) collective-permute-start(bf16[1024,256]{1,0:T(8,128)(2,1)} %copy-done.100), channel_id=1, source_target_pairs={{0,2},{1,3},{2,0},{3,1},{4,6},{5,7},{6,4},{7,5},{8,10},{9,11},{10,... | collective-permute-start | bytes 1572872 | tf_op jit(solution)/shard_map/ppermute | solution.py:686
  530.4 44.1 %collective-permute-start.91 = (bf16[1024,512]{1,0:T(8,128)(2,1)S(1)}, bf16[1024,512]{1,0:T(8,128)(2,1)S(1)}, u32[]{:S(2)}, u32[]{:S(2)}) collective-permute-start(bf16[1024,512]{1,0:T(8,128)(2,1)S(1)} %add_convert_fusion.11), channel_id=1, source_target_pairs={{4,8},{8,4},{5,9},{9,5},{6,10},{10,6},{7,11},{11,7},{20,24},{24,20... | collective-permute-start | bytes 3145736 | tf_op jit(solution)/shard_map/ppermute | solution.py:725
  543.3 32.5 %collective-permute-start.104 = (bf16[1024,512]{1,0:T(8,128)(2,1)S(1)}, bf16[1024,512]{1,0:T(8,128)(2,1)S(1)}, u32[]{:S(2)}, u32[]{:S(2)}) collective-permute-start(bf16[1024,512]{1,0:T(8,128)(2,1)S(1)} %add_convert_fusion.1), channel_id=1, source_target_pairs={{4,8},{8,4},{5,9},{9,5},{6,10},{10,6},{7,11},{11,7},{20,24},{24,20... | collective-permute-start | bytes 3145736 | tf_op jit(solution)/shard_map/ppermute | solution.py:725
  573.3 96.9 %collective-permute-start.81 = (bf16[1024,512]{1,0:T(8,128)(2,1)S(1)}, bf16[1024,512]{1,0:T(8,128)(2,1)S(1)}, u32[]{:S(2)}, u32[]{:S(2)}) collective-permute-start(bf16[1024,512]{1,0:T(8,128)(2,1)S(1)} %get-tuple-element.200), channel_id=1, source_target_pairs={{0,1},{1,0},{2,3},{3,2},{4,5},{5,4},{6,7},{7,6},{8,9},{9,8},{10,11... | collective-permute-start | bytes 3145736 | tf_op jit(solution)/shard_map/ppermute | solution.py:686
  589.4 58.2 %collective-permute-start.92 = (bf16[1024,512]{1,0:T(8,128)(2,1)S(1)}, bf16[1024,512]{1,0:T(8,128)(2,1)S(1)}, u32[]{:S(2)}, u32[]{:S(2)}) collective-permute-start(bf16[1024,512]{1,0:T(8,128)(2,1)S(1)} %add_convert_fusion.10), channel_id=1, source_target_pairs={{4,0},{8,12},{5,1},{9,13},{6,2},{10,14},{7,3},{11,15},{20,16},{24,... | collective-permute-start | bytes 3145736 | tf_op jit(solution)/shard_map/ppermute | solution.py:726
  591.1 32.0 %collective-permute-start.44 = (bf16[512,256]{1,0:T(8,128)(2,1)S(1)}, bf16[512,256]{1,0:T(8,128)(2,1)S(1)}, u32[]{:S(2)}, u32[]{:S(2)}) collective-permute-start(bf16[512,256]{1,0:T(8,128)(2,1)S(1)} %get-tuple-element.153), channel_id=1, source_target_pairs={{0,4},{4,0},{8,12},{12,8},{1,5},{5,1},{9,13},{13,9},{2,6},{6,2},{1... | collective-permute-start | bytes 786440 | tf_op jit(solution)/shard_map/ppermute | solution.py:686
  597.2 44.2 %collective-permute-start.64 = (bf16[1024,256]{1,0:T(8,128)(2,1)S(1)}, bf16[1024,256]{1,0:T(8,128)(2,1)S(1)}, u32[]{:S(2)}, u32[]{:S(2)}) collective-permute-start(bf16[1024,256]{1,0:T(8,128)(2,1)S(1)} %add_convert_fusion.32), channel_id=1, source_target_pairs={{4,0},{8,12},{5,1},{9,13},{6,2},{10,14},{7,3},{11,15},{20,16},{24,... | collective-permute-start | bytes 1572872 | tf_op jit(solution)/shard_map/ppermute | solution.py:726
  598.8 46.7 %collective-permute-start.77 = (bf16[1024,256]{1,0:T(8,128)(2,1)S(1)}, bf16[1024,256]{1,0:T(8,128)(2,1)S(1)}, u32[]{:S(2)}, u32[]{:S(2)}) collective-permute-start(bf16[1024,256]{1,0:T(8,128)(2,1)S(1)} %add_convert_fusion.22), channel_id=1, source_target_pairs={{4,0},{8,12},{5,1},{9,13},{6,2},{10,14},{7,3},{11,15},{20,16},{24,... | collective-permute-start | bytes 1572872 | tf_op jit(solution)/shard_map/ppermute | solution.py:726
  623.0 44.9 %collective-permute-start.105 = (bf16[1024,512]{1,0:T(8,128)(2,1)S(1)}, bf16[1024,512]{1,0:T(8,128)(2,1)S(1)}, u32[]{:S(2)}, u32[]{:S(2)}) collective-permute-start(bf16[1024,512]{1,0:T(8,128)(2,1)S(1)} %add_convert_fusion), channel_id=1, source_target_pairs={{4,0},{8,12},{5,1},{9,13},{6,2},{10,14},{7,3},{11,15},{20,16},{24,... | collective-permute-start | bytes 3145736 | tf_op jit(solution)/shard_map/ppermute | solution.py:726
  645.5 52.5 %collective-permute-start.94 = (bf16[1024,512]{1,0:T(8,128)(2,1)}, bf16[1024,512]{1,0:T(8,128)(2,1)}, u32[]{:S(2)}, u32[]{:S(2)}) collective-permute-start(bf16[1024,512]{1,0:T(8,128)(2,1)} %get-tuple-element.211), channel_id=1, source_target_pairs={{0,2},{1,3},{2,0},{3,1},{4,6},{5,7},{6,4},{7,5},{8,10},{9,11},{10,... | collective-permute-start | bytes 3145736 | tf_op jit(solution)/shard_map/ppermute | solution.py:686
  647.6 32.1 %collective-permute-start.45 = (bf16[512,768]{1,0:T(8,128)(2,1)S(1)}, bf16[512,768]{1,0:T(8,128)(2,1)S(1)}, u32[]{:S(2)}, u32[]{:S(2)}) collective-permute-start(bf16[512,768]{1,0:T(8,128)(2,1)S(1)} %get-tuple-element.156), channel_id=1, source_target_pairs={{0,4},{4,0},{8,12},{12,8},{1,5},{5,1},{9,13},{13,9},{2,6},{6,2},{1... | collective-permute-start | bytes 2359304 | tf_op jit(solution)/shard_map/ppermute | solution.py:686
  668.0 31.2 %collective-permute-start.96 = (bf16[1024,512]{1,0:T(8,128)(2,1)}, bf16[1024,512]{1,0:T(8,128)(2,1)}, u32[]{:S(2)}, u32[]{:S(2)}) collective-permute-start(bf16[1024,512]{1,0:T(8,128)(2,1)} %add_convert_fusion.8), channel_id=1, source_target_pairs={{0,1},{1,0},{2,3},{3,2},{4,5},{5,4},{6,7},{7,6},{8,9},{9,8},{10,11... | collective-permute-start | bytes 3145736 | tf_op jit(solution)/shard_map/ppermute | solution.py:686
  671.6 49.4 %collective-permute-start.84 = (bf16[1024,512]{1,0:T(8,128)(2,1)}, bf16[1024,512]{1,0:T(8,128)(2,1)}, u32[]{:S(2)}, u32[]{:S(2)}) collective-permute-start(bf16[1024,512]{1,0:T(8,128)(2,1)} %add_convert_fusion.17), channel_id=1, source_target_pairs={{0,4},{12,8},{1,5},{13,9},{2,6},{14,10},{3,7},{15,11},{16,20},{28,... | collective-permute-start | bytes 3145736 | tf_op jit(solution)/shard_map/ppermute | solution.py:724
  702.5 116.1 %collective-permute-start.65 = (bf16[1024,256]{1,0:T(8,128)(2,1)}, bf16[1024,256]{1,0:T(8,128)(2,1)}, u32[]{:S(2)}, u32[]{:S(2)}) collective-permute-start(bf16[1024,256]{1,0:T(8,128)(2,1)} %broadcast_select_fusion.19), channel_id=1, source_target_pairs={{0,16},{1,17},{2,18},{3,19},{4,20},{5,21},{6,22},{7,23},{8,24},{9,... | collective-permute-start | bytes 1572872 | tf_op jit(solution)/shard_map/ppermute | solution.py:986
  715.2 33.6 %collective-permute-start.66 = (bf16[1024,256]{1,0:T(8,128)(2,1)S(1)}, bf16[1024,256]{1,0:T(8,128)(2,1)S(1)}, u32[]{:S(2)}, u32[]{:S(2)}) collective-permute-start(bf16[1024,256]{1,0:T(8,128)(2,1)S(1)} %copy-done.97), channel_id=1, source_target_pairs={{0,2},{1,3},{2,0},{3,1},{4,6},{5,7},{6,4},{7,5},{8,10},{9,11},{10,... | collective-permute-start | bytes 1572872 | tf_op jit(solution)/shard_map/ppermute | solution.py:686
  740.8 118.9 %collective-permute-start.78 = (bf16[1024,256]{1,0:T(8,128)(2,1)}, bf16[1024,256]{1,0:T(8,128)(2,1)}, u32[]{:S(2)}, u32[]{:S(2)}) collective-permute-start(bf16[1024,256]{1,0:T(8,128)(2,1)} %broadcast_select_fusion.17), channel_id=1, source_target_pairs={{0,16},{1,17},{2,18},{3,19},{4,20},{5,21},{6,22},{7,23},{8,24},{9,... | collective-permute-start | bytes 1572872 | tf_op jit(solution)/shard_map/ppermute | solution.py:986
  747.1 61.2 %collective-permute-start.85 = (bf16[1024,512]{1,0:T(8,128)(2,1)}, bf16[1024,512]{1,0:T(8,128)(2,1)}, u32[]{:S(2)}, u32[]{:S(2)}) collective-permute-start(bf16[1024,512]{1,0:T(8,128)(2,1)} %add_convert_fusion.16), channel_id=1, source_target_pairs={{4,8},{8,4},{5,9},{9,5},{6,10},{10,6},{7,11},{11,7},{20,24},{24,20... | collective-permute-start | bytes 3145736 | tf_op jit(solution)/shard_map/ppermute | solution.py:725
  748.8 36.9 %collective-permute-start.56 = (bf16[1024,256]{1,0:T(8,128)(2,1)}, bf16[1024,256]{1,0:T(8,128)(2,1)S(1)}, u32[]{:S(2)}, u32[]{:S(2)}) collective-permute-start(bf16[1024,256]{1,0:T(8,128)(2,1)} %add_convert_fusion.39), channel_id=1, source_target_pairs={{0,4},{12,8},{1,5},{13,9},{2,6},{14,10},{3,7},{15,11},{16,20},{28,... | collective-permute-start | bytes 1572872 | tf_op jit(solution)/shard_map/ppermute | solution.py:724
  808.3 97.8 %collective-permute-start.93 = (bf16[1024,512]{1,0:T(8,128)(2,1)S(1)}, bf16[1024,512]{1,0:T(8,128)(2,1)}, u32[]{:S(2)}, u32[]{:S(2)}) collective-permute-start(bf16[1024,512]{1,0:T(8,128)(2,1)S(1)} %copy-done.131), channel_id=1, source_target_pairs={{0,16},{1,17},{2,18},{3,19},{4,20},{5,21},{6,22},{7,23},{8,24},{9,... | collective-permute-start | bytes 3145736 | tf_op jit(solution)/shard_map/ppermute | solution.py:986
  813.5 43.2 %collective-permute-start.58 = (bf16[1024,256]{1,0:T(8,128)(2,1)S(1)}, bf16[1024,256]{1,0:T(8,128)(2,1)S(1)}, u32[]{:S(2)}, u32[]{:S(2)}) collective-permute-start(bf16[1024,256]{1,0:T(8,128)(2,1)S(1)} %add_convert_fusion.37), channel_id=1, source_target_pairs={{4,0},{8,12},{5,1},{9,13},{6,2},{10,14},{7,3},{11,15},{20,16},{24,... | collective-permute-start | bytes 1572872 | tf_op jit(solution)/shard_map/ppermute | solution.py:726
  815.0 94.8 %collective-permute-start.106 = (bf16[1024,512]{1,0:T(8,128)(2,1)S(1)}, bf16[1024,512]{1,0:T(8,128)(2,1)}, u32[]{:S(2)}, u32[]{:S(2)}) collective-permute-start(bf16[1024,512]{1,0:T(8,128)(2,1)S(1)} %copy-done.130), channel_id=1, source_target_pairs={{0,16},{1,17},{2,18},{3,19},{4,20},{5,21},{6,22},{7,23},{8,24},{9,... | collective-permute-start | bytes 3145736 | tf_op jit(solution)/shard_map/ppermute | solution.py:986
  818.6 88.8 %collective-permute-start.86 = (bf16[1024,512]{1,0:T(8,128)(2,1)}, bf16[1024,512]{1,0:T(8,128)(2,1)}, u32[]{:S(2)}, u32[]{:S(2)}) collective-permute-start(bf16[1024,512]{1,0:T(8,128)(2,1)} %add_convert_fusion.15), channel_id=1, source_target_pairs={{4,0},{8,12},{5,1},{9,13},{6,2},{10,14},{7,3},{11,15},{20,16},{24,... | collective-permute-start | bytes 3145736 | tf_op jit(solution)/shard_map/ppermute | solution.py:726
  856.8 33.7 %collective-permute-start.71 = (bf16[1024,256]{1,0:T(8,128)(2,1)S(1)}, bf16[1024,256]{1,0:T(8,128)(2,1)S(1)}, u32[]{:S(2)}, u32[]{:S(2)}) collective-permute-start(bf16[1024,256]{1,0:T(8,128)(2,1)S(1)} %add_convert_fusion.27), channel_id=1, source_target_pairs={{4,0},{8,12},{5,1},{9,13},{6,2},{10,14},{7,3},{11,15},{20,16},{24,... | collective-permute-start | bytes 1572872 | tf_op jit(solution)/shard_map/ppermute | solution.py:726
  859.7 50.1 %collective-permute-start.99 = (bf16[1024,512]{1,0:T(8,128)(2,1)}, bf16[1024,512]{1,0:T(8,128)(2,1)}, u32[]{:S(2)}, u32[]{:S(2)}) collective-permute-start(bf16[1024,512]{1,0:T(8,128)(2,1)} %add_convert_fusion.5), channel_id=1, source_target_pairs={{4,0},{8,12},{5,1},{9,13},{6,2},{10,14},{7,3},{11,15},{20,16},{24,... | collective-permute-start | bytes 3145736 | tf_op jit(solution)/shard_map/ppermute | solution.py:726
  913.9 37.2 %collective-permute-start.107 = (bf16[1024,512]{1,0:T(8,128)(2,1)}, bf16[1024,512]{1,0:T(8,128)(2,1)}, u32[]{:S(2)}, u32[]{:S(2)}) collective-permute-start(bf16[1024,512]{1,0:T(8,128)(2,1)} %get-tuple-element.303), channel_id=1, source_target_pairs={{16,0},{17,1},{18,2},{19,3},{20,4},{21,5},{22,6},{23,7},{24,8},{25... | collective-permute-start | bytes 3145736 | tf_op jit(solution)/shard_map/ppermute | solution.py:987
  915.2 38.2 %collective-permute-start.108 = (bf16[1024,512]{1,0:T(8,128)(2,1)}, bf16[1024,512]{1,0:T(8,128)(2,1)}, u32[]{:S(2)}, u32[]{:S(2)}) collective-permute-start(bf16[1024,512]{1,0:T(8,128)(2,1)} %get-tuple-element.305), channel_id=1, source_target_pairs={{16,0},{17,1},{18,2},{19,3},{20,4},{21,5},{22,6},{23,7},{24,8},{25... | collective-permute-start | bytes 3145736 | tf_op jit(solution)/shard_map/ppermute | solution.py:987
  (240 other events, 3548.6 us)

commit v2 on v1

--- a/solution.py
+++ b/solution.py
@@ -35,10 +35,16 @@
     return math.prod(shape) * jnp.dtype(dtype).itemsize
 
 
-def run_kernel(body, name, ins, outs, scratch, flops, exps=0):
+def run_kernel(kernel, name, ins, outs, scratch, flops, exps=0, deps=()):
+    deps = list(deps)
+
+    def body(*refs):
+        kernel(*refs[len(deps) :])
+
     spaces = {"v": pltpu.VMEM, "a": pl.ANY, "s": pltpu.SMEM}
     moved = sum(size_of(a.shape, a.dtype) for a, _ in ins) + sum(size_of(s, d) for s, d, _ in outs)
     held = sum(size_of(a.shape, a.dtype) for a, k in ins if k == "v")
+    ins = [(a, "a") for a in deps] + ins
     held += sum(size_of(s, d) for s, d, k in outs if k == "v")
     held += sum(size_of(s.shape, s.dtype) for s in scratch if s.memory_space == pltpu.VMEM)
     return pl.pallas_call(
@@ -68,6 +74,32 @@
 
 def block_rows(scal, k, rows):
     return pl.ds(pl.multiple_of((scal[0] ^ k) * rows, rows), rows)
+
+
+def scatter_groups(count, h):
+    places = [1 << i for i in range(count.bit_length() - 1)]
+    groups = [[0]]
+    for place in places[::-1] if h == 0 else places:
+        groups.insert(0, [k ^ place for group in groups for k in group])
+    return groups
+
+
+def group_shapes(shape, count):
+    return [
+        ((len(group) * shape[0], shape[1]), BF16, "a")
+        for h in range(2)
+        for group in scatter_groups(count, h)
+    ]
+
+
+def group_views(refs, size, count):
+    views, refs = {}, list(refs)
+    for h in range(2):
+        for group in scatter_groups(count, h):
+            ref = refs.pop(0)
+            for place, k in enumerate(group):
+                views[2 * k + h] = ref.at[place * size : (place + 1) * size, :]
+    return [views[i] for i in range(2 * count)]
 
 
 def mix_pairs(scal, pieces, full, rows, count):
@@ -151,12 +183,12 @@
     return values * below, below + values * energy * 0.3989422804014327
 
 
-def mix_forward(params, hidden, gain, shift, bias, scal, pieces):
+def mix_forward(params, hidden, vectors, bias, scal, pieces, deps):
     rows, count = params
     tokens, width = hidden.shape
     span = 3 * GROUP
 
-    def body(scal, hidden, gain, shift, bias, *rest):
+    def body(scal, hidden, vectors, bias, *rest):
         pieces, (normed, keep, send, full, sems) = rest[: 2 * count], rest[2 * count :]
         copies = start_all(mix_pairs(scal, pieces, full, rows, count), sems)
 
@@ -164,7 +196,7 @@
         def _(i):
             part = pl.ds(pl.multiple_of(i * ROWS, ROWS), ROWS)
             unit, _ = norm_parts(hidden[part, :].astype(F32))
-            normed[part, :] = (unit * gain[...] + shift[...]).astype(BF16)
+            normed[part, :] = (unit * vectors[0:1, :] + vectors[1:2, :]).astype(BF16)
 
         wait_all(copies)
         for target, group in ((send, 1 - scal[1]), (keep, scal[1])):
@@ -176,11 +208,11 @@
     return run_kernel(
         body,
         "mix_forward",
-        [(scal, "s"), (hidden, "v"), (gain, "v"), (shift, "v"), (bias, "v")]
-        + [(p, "a") for p in pieces],
+        [(scal, "s"), (hidden, "v"), (vectors, "v"), (bias, "v")] + [(p, "a") for p in pieces],
         [((tokens, width), BF16, "v"), ((tokens, span), BF16, "v"), ((tokens, span), BF16, "v")],
         [pltpu.VMEM((width, 2 * span), BF16), pltpu.SemaphoreType.DMA((6 * count,))],
         4 * tokens * width * span,
+        deps=deps,
     )
 
 
@@ -205,7 +237,7 @@
     return scores[:start, :], jnp.where(position < length, tail, NEGATIVE)
 
 
-def attend_forward(keep, other, scal):
+def attend_forward(keep, other, scal, deps):
     tokens = keep.shape[0]
     total = 2 * tokens
     heads = GROUP // HEAD_DIM
@@ -255,6 +287,7 @@
         ],
         heads * total * total * HEAD_DIM * 4,
         heads * total * total,
+        deps,
     )
 
 
@@ -265,7 +298,7 @@
     return start_all([(keep, full.at[:, own]), (other, full.at[:, far])], sems, first)
 
 
-def out_forward(params, keep, other, scal, pieces, width):
+def out_forward(params, keep, other, scal, pieces, width, deps):
     rows, count = params
     tokens = keep.shape[0]
     inner = 2 * GROUP
@@ -288,10 +321,11 @@
         [((tokens, inner), BF16, "v"), ((tokens, width), F32, "v"), ((tokens, width), BF16, "v")],
         [pltpu.VMEM((inner, width), BF16), pltpu.SemaphoreType.DMA((4 * count + 2,))],
         2 * tokens * inner * width,
-    )
-
-
-def feed_forward(params, hidden, own, other, vectors, upbias, scal, pieces):
+        deps=deps,
+    )
+
+
+def feed_forward(params, hidden, own, other, vectors, upbias, scal, pieces, deps):
     rows, count = params
     tokens, width = hidden.shape
     inner = upbias.shape[1]
@@ -308,12 +342,12 @@
         @pl.loop(0, tokens // ROWS)
         def _(i):
             part = pl.ds(pl.multiple_of(i * ROWS, ROWS), ROWS)
-            made = own[part, :] + other[part, :].astype(F32) + vectors[0:1, :]
+            made = own[part, :] + other[part, :].astype(F32) + vectors[4:5, :]
             branch[part, :] = made
-            made = hidden[part, :].astype(F32) + vectors[1:2, :] * made
+            made = hidden[part, :].astype(F32) + vectors[5:6, :] * made
             residual[part, :] = made
             unit, _ = norm_parts(made)
-            normed[part, :] = (unit * vectors[2:3, :] + vectors[3:4, :]).astype(BF16)
+            normed[part, :] = (unit * vectors[6:7, :] + vectors[7:8, :]).astype(BF16)
 
         wait_all(up_copies)
 
@@ -357,16 +391,38 @@
         ],
         4 * tokens * width * inner,
         2 * tokens * inner,
-    )
-
-
-def feed_backward(params, incoming, feedscale, slope, scal, pieces):
+        deps,
+    )
+
+
+def layer_result(residual, own, other, vectors, deps):
+    tokens, width = residual.shape
+
+    def body(residual, own, other, vectors, made):
+        @pl.loop(0, tokens // ROWS)
+        def _(i):
+            part = pl.ds(pl.multiple_of(i * ROWS, ROWS), ROWS)
+            branch = own[part, :] + other[part, :].astype(F32) + vectors[8:9, :]
+            made[part, :] = (residual[part, :] + vectors[9:10, :] * branch).astype(BF16)
+
+    return run_kernel(
+        body,
+        "layer_result",
+        [(residual, "v"), (own, "v"), (other, "v"), (vectors, "v")],
+        [((tokens, width), BF16, "v")],
+        [],
+        4 * tokens * width,
+        deps=deps,
+    )[0]
+
+
+def feed_backward(params, incoming, vectors, slope, scal, pieces, deps):
     rows, count = params
     tokens, width = incoming.shape
     inner = slope.shape[1]
     tile = 512
 
-    def body(scal, incoming, feedscale, slope, *rest):
+    def body(scal, incoming, vectors, slope, *rest):
         pieces = rest[: 2 * count]
         lower, up_grad, bias_grad, made_own, made_send, up, down, sems = rest[2 * count :]
         down_copies = start_all(down_pairs(scal, pieces, down, rows, count), sems)
@@ -375,7 +431,7 @@
         @pl.loop(0, tokens // ROWS)
         def _(i):
             part = pl.ds(pl.multiple_of(i * ROWS, ROWS), ROWS)
-            lower[part, :] = (incoming[part, :].astype(F32) * feedscale[...]).astype(BF16)
+            lower[part, :] = (incoming[part, :].astype(F32) * vectors[9:10, :]).astype(BF16)
 
         wait_all(down_copies)
 
@@ -399,7 +455,7 @@
     return run_kernel(
         body,
         "feed_backward",
-        [(scal, "s"), (incoming, "v"), (feedscale, "v"), (slope, "v")]
+        [(scal, "s"), (incoming, "v"), (vectors, "v"), (slope, "v")]
         + [(p, "a") for p in pieces],
         [
             ((tokens, width), BF16, "v"),
@@ -414,10 +470,11 @@
             pltpu.SemaphoreType.DMA((6 * count,)),
         ],
         4 * tokens * width * inner,
-    )
-
-
-def feed_weights(params, active, lower, normed, up_grad, scal):
+        deps=deps,
+    )
+
+
+def feed_weights(params, active, lower, normed, up_grad, scal, deps):
     rows, count = params
     tokens, width = lower.shape
     inner = active.shape[1]
@@ -425,7 +482,7 @@
     tile = 512
 
     def body(scal, active, lower, normed, up_grad, *rest):
-        pieces, (up, down, sems) = rest[: 2 * count], rest[2 * count :]
+        pieces, (up, down, sems) = group_views(rest[:-3], 4 * rows, count), rest[-3:]
 
         @pl.loop(0, inner // tile)
         def _(i):
@@ -447,40 +504,41 @@
         body,
         "feed_weights",
         [(scal, "s"), (active, "v"), (lower, "v"), (normed, "v"), (up_grad, "v")],
-        [(shape, BF16, "a")] * (2 * count),
+        group_shapes(shape, count),
         [
             pltpu.VMEM((width, inner), BF16),
             pltpu.VMEM((inner, width), BF16),
             pltpu.SemaphoreType.DMA((6 * count,)),
         ],
         4 * tokens * width * inner,
-    )
-
-
-def feed_sums(incoming, own, other, downbias, lower):
+        deps=deps,
+    )
+
+
+def feed_sums(incoming, own, other, vectors, lower):
     tokens, width = incoming.shape
 
-    def body(incoming, own, other, downbias, lower, sums):
+    def body(incoming, own, other, vectors, lower, sums):
         sums[...] = jnp.zeros_like(sums)
 
         @pl.loop(0, tokens // ROWS)
         def _(i):
             part = pl.ds(pl.multiple_of(i * ROWS, ROWS), ROWS)
-            branch = own[part, :] + other[part, :].astype(F32) + downbias[...]
+            branch = own[part, :] + other[part, :].astype(F32) + vectors[8:9, :]
             sums[0:1, :] += column_sum(branch * incoming[part, :].astype(F32))
             sums[1:2, :] += column_sum(lower[part, :].astype(F32))
 
     return run_kernel(
         body,
         "feed_sums",
-        [(incoming, "v"), (own, "v"), (other, "v"), (downbias, "v"), (lower, "v")],
+        [(incoming, "v"), (own, "v"), (other, "v"), (vectors, "v"), (lower, "v")],
         [((8, width), F32, "v")],
         [],
         4 * tokens * width,
     )[0]
 
 
-def out_backward(params, incoming, residual, own, other, branch, vectors, scal, pieces):
+def out_backward(params, incoming, residual, own, other, branch, vectors, scal, pieces, deps):
     rows, count = params
     tokens, width = incoming.shape
     inner = 2 * GROUP
@@ -495,13 +553,13 @@
         def _(i):
             part = pl.ds(pl.multiple_of(i * ROWS, ROWS), ROWS)
             grad = own[part, :] + other[part, :].astype(F32)
-            back, unit = norm_back(residual[part, :], vectors[2:3, :], grad)
+            back, unit = norm_back(residual[part, :], vectors[6:7, :], grad)
             sums[0:1, :] += column_sum(grad * unit)
             sums[1:2, :] += column_sum(grad)
             back = incoming[part, :].astype(F32) + back
             residual_grad[part, :] = back
             sums[2:3, :] += column_sum(back * branch[part, :])
-            low = (back * vectors[1:2, :]).astype(BF16)
+            low = (back * vectors[5:6, :]).astype(BF16)
             branch_grad[part, :] = low
             sums[3:4, :] += column_sum(low.astype(F32))
 
@@ -525,10 +583,11 @@
         ],
         [pltpu.VMEM((inner, width), BF16), pltpu.SemaphoreType.DMA((4 * count,))],
         2 * tokens * inner * width,
-    )
-
-
-def attend_backward(keep, other, grad_keep, grad_other, peaks, scal):
+        deps=deps,
+    )
+
+
+def attend_backward(keep, other, grad_keep, grad_other, peaks, scal, deps):
     tokens = keep.shape[0]
     total = 2 * tokens
     heads = GROUP // HEAD_DIM
@@ -588,10 +647,11 @@
         ],
         heads * total * total * HEAD_DIM * 10,
         heads * total * total,
-    )
-
-
-def mix_backward(params, keep, other, scal, pieces, width):
+        deps,
+    )
+
+
+def mix_backward(params, keep, other, scal, pieces, width, deps):
     rows, count = params
     tokens = keep.shape[0]
     inner = 6 * GROUP
@@ -617,16 +677,20 @@
         [((tokens, inner), BF16, "v"), ((tokens, width), F32, "v"), ((tokens, width), BF16, "v")],
         [pltpu.VMEM((width, inner), BF16), pltpu.SemaphoreType.DMA((6 * count + 2,))],
         2 * tokens * inner * width,
-    )
-
-
-def mix_weights(params, normed, triple, mixed, branch_grad, scal):
+        deps=deps,
+    )
+
+
+def mix_weights(params, normed, triple, mixed, branch_grad, sums, scal, deps):
     rows, count = params
     tokens, width = normed.shape
     inner = triple.shape[1]
 
-    def body(scal, normed, triple, mixed, branch_grad, *rest):
-        pieces, (sums, full, out, sems) = rest[: 2 * count], rest[2 * count :]
+    extra, half = 16, rows // 2
+
+    def body(scal, normed, triple, mixed, branch_grad, in_sum, out_sum, feed_sum, up_sum, *rest):
+        refs, (full, out, vectors, low, bias, sems) = rest[:-6], rest[-6:]
+        pieces = group_views(refs, 4 * rows + extra, count)
         out[...] = dot_tn(mixed[...], branch_grad[...]).astype(BF16)
         pairs = [(b, a) for a, b in out_pairs(scal, pieces, out, rows, count)]
         copies = start_all(pairs, sems)
@@ -635,36 +699,78 @@
         def _(i):
             part = pl.ds(pl.multiple_of(i * GROUP, GROUP), GROUP)
             full[:, part] = dot_tn(normed[...], triple[:, part]).astype(BF16)
-            sums[:, part] = column_sum(triple[:, part].astype(F32))
+            bias[0:1, part] = column_sum(triple[:, part].astype(F32))
 
         pairs = [(b, a) for a, b in mix_pairs(scal, pieces, full, rows, count)]
-        wait_all(copies + start_all(pairs, sems, 4 * count))
+        copies += start_all(pairs, sems, 4 * count)
+        vectors[...] = jnp.zeros_like(vectors)
+        vectors[0:2, :] = in_sum[0:2, :]
+        vectors[2:6, :] = out_sum[0:4, :]
+        vectors[6:8, :] = feed_sum[0:2, :]
+        for j in range(2):
+            for b in range(count):
+                at = (2 * b + j) * rows
+                vectors[8 + j : 9 + j, b * rows : (b + 1) * rows] = up_sum[:, at : at + rows]
+        for side, t in enumerate((0, 2)):
+            row = jnp.concatenate(
+                [bias[0:1, (3 * h + t) * GROUP : (3 * h + t + 1) * GROUP] for h in range(2)], axis=1
+            )
+            for b in range(count):
+                at = b * rows + side * half
+                vectors[10:11, at : at + half] = row[:, b * half : (b + 1) * half]
+        low[...] = vectors[...].astype(BF16)
+        pairs = [
+            (low.at[:, block_rows(scal, k, rows)], pieces[2 * k + h].at[4 * rows :, 0:rows])
+            for k in range(count)
+            for h in range(2)
+        ]
+        wait_all(copies + start_all(pairs, sems, 10 * count))
 
     return run_kernel(
         body,
         "mix_weights",
-        [(scal, "s"), (normed, "v"), (triple, "v"), (mixed, "v"), (branch_grad, "v")],
-        [((4 * rows, GROUP), BF16, "a")] * (2 * count) + [((1, inner), F32, "v")],
+        [(scal, "s"), (normed, "v"), (triple, "v"), (mixed, "v"), (branch_grad, "v")]
+        + [(v, "v") for v in sums],
+        group_shapes((4 * rows + extra, GROUP), count),
         [
             pltpu.VMEM((width, inner), BF16),
             pltpu.VMEM((2 * GROUP, width), BF16),
-            pltpu.SemaphoreType.DMA((10 * count,)),
+            pltpu.VMEM((extra, width), F32),
+            pltpu.VMEM((extra, width), BF16),
+            pltpu.VMEM((8, inner), F32),
+            pltpu.SemaphoreType.DMA((12 * count,)),
         ],
         2 * tokens * width * (inner + 2 * GROUP),
-    )
-
-
-def input_backward(hidden, own, other, residual_grad, gain):
+        deps=deps,
+    )
+
+
+def add_kernel(left, right, deps):
+    def body(left, right, made):
+        made[...] = add_low(left[...], right[...])
+
+    return run_kernel(
+        body,
+        "add_kernel",
+        [(left, "v"), (right, "v")],
+        [(left.shape, BF16, "v")],
+        [],
+        left.size,
+        deps=deps,
+    )[0]
+
+
+def input_backward(hidden, own, other, residual_grad, vectors):
     tokens, width = hidden.shape
 
-    def body(hidden, own, other, residual_grad, gain, input_grad, low_grad, sums):
+    def body(hidden, own, other, residual_grad, vectors, input_grad, low_grad, sums):
         sums[...] = jnp.zeros_like(sums)
 
         @pl.loop(0, tokens // ROWS)
         def _(i):
             part = pl.ds(pl.multiple_of(i * ROWS, ROWS), ROWS)
             grad = own[part, :] + other[part, :].astype(F32)
-            back, unit = norm_back(hidden[part, :].astype(F32), gain[...], grad)
+            back, unit = norm_back(hidden[part, :].astype(F32), vectors[0:1, :], grad)
             sums[0:1, :] += column_sum(grad * unit)
             sums[1:2, :] += column_sum(grad)
             back = residual_grad[part, :] + back
@@ -674,7 +780,7 @@
     return run_kernel(
         body,
         "input_backward",
-        [(hidden, "v"), (own, "v"), (other, "v"), (residual_grad, "v"), (gain, "v")],
+        [(hidden, "v"), (own, "v"), (other, "v"), (residual_grad, "v"), (vectors, "v")],
         [((tokens, width), F32, "v"), ((tokens, width), BF16, "v"), ((8, width), F32, "v")],
         [],
         20 * tokens * width,
@@ -692,110 +798,257 @@
 
 def gather_blocks(halves, bits):
     places = [1 << i for i in range(len(bits))]
-    held = {}
+    held, stages = {}, ([], [], [])
     for h, value in enumerate(halves):
         order = list(zip(bits, places))
         order = order if h == 0 else order[::-1]
         blocks = {0: value}
-        for bit, place in order:
+        for hop, (bit, place) in enumerate(order):
             for k in list(blocks):
                 blocks[k ^ place] = swap(blocks[k], "fsdp", bit)
+                stages[0 if hop == 0 else 1 if k == 0 else 2].append(blocks[k ^ place])
         for k in blocks:
             held[k, h] = blocks[k]
-    return [held[k, h] for k in range(1 << len(bits)) for h in range(2)]
-
-
-def scatter_blocks(pieces, bits):
-    places = [1 << i for i in range(len(bits))]
-    results = []
+    return [held[k, h] for k in range(1 << len(bits)) for h in range(2)], stages
+
+
+def scatter_blocks(groups, bits, deps=()):
+    results, stages, groups = [], [[] for _ in bits], list(groups)
     for h in range(2):
-        blocks = {k: pieces[2 * k + h] for k in range(1 << len(bits))}
-        order = list(zip(bits, places))
-        order = order if h == 0 else order[::-1]
-        for bit, place in order:
-            for k in [k for k in blocks if k & place]:
-                blocks[k ^ place] = add_low(blocks[k ^ place], swap(blocks.pop(k), "fsdp", bit))
-        results.append(blocks[0])
-    return results
+        held = [groups.pop(0) for _ in range(len(bits) + 1)]
+        for hop, bit in enumerate(bits if h == 0 else bits[::-1]):
+            far = swap(held.pop(0), "fsdp", bit)
+            stages[hop].append(far)
+            at = 0
+            for i, value in enumerate(held):
+                if deps and hop == len(bits) - 1:
+                    held[i] = add_kernel(value, far, deps)
+                else:
+                    held[i] = add_low(value, far[at : at + value.shape[0]])
+                at += value.shape[0]
+        results.append(held[0])
+    return results, stages
 
 
 def sum_line(value):
     place = lax.axis_index("seq")
-    near = add_low(value, lax.ppermute(value, "seq", [(0, 1), (3, 2)]))
-    both = add_low(near, lax.ppermute(near, "seq", [(1, 2), (2, 1)]))
+    inward = lax.ppermute(value, "seq", [(0, 1), (3, 2)])
+    near = add_low(value, inward)
+    across = lax.ppermute(near, "seq", [(1, 2), (2, 1)])
+    both = add_low(near, across)
     back = lax.ppermute(both, "seq", [(1, 0), (2, 3)])
-    return jnp.where((place == 1) | (place == 2), both, back)
+    return jnp.where((place == 1) | (place == 2), both, back), (inward, across, back)
+
+
+def sum_shares(shares, layer):
+    if layer == 0:
+        lines = [sum_line(v) for v in shares]
+        return [v for v, _ in lines], [moved for _, moved in lines]
+    total, moved = sum_line(jnp.concatenate(shares, axis=0))
+    size = shares[0].shape[0]
+    return [total[:size], total[size:]], [moved]
 
 
 def pick(flag, first, second):
     return jnp.where(flag, first, second)
 
 
-def pack_mix(mix, out, side, count):
-    rows, width = mix.shape[0], out.shape[1]
-    split = mix.reshape(rows, 3, count, 2, width // (2 * count))[:, :, :, side]
-    split = split.reshape(rows, 3, width // 2)
-    half = out[side * rows // 2 : (side + 1) * rows // 2]
-    return [
-        jnp.concatenate(
-            [split[:, t, h * GROUP : (h + 1) * GROUP] for t in range(3)]
-            + [half[:, (2 * h + j) * GROUP : (2 * h + j + 1) * GROUP] for j in range(2)],
-            axis=0,
-        )
-        for h in range(2)
-    ]
-
-
-def unpack_mix(sides, count):
-    rows = sides[0][0].shape[0] // 4
-    width = 4 * GROUP
-    mixes, outs = [], []
-    for halves in sides:
-        parts = [
-            jnp.concatenate([halves[h][t * rows : (t + 1) * rows] for h in range(2)], axis=1)
-            for t in range(3)
+def side_pick(core, low, high):
+    return jnp.where(core == 0, low, high), jnp.where(core == 0, high, low)
+
+
+def pack_mix(params, mix, out, vectors, scal):
+    rows, count = params
+    width = out.shape[1]
+    lanes = width // (2 * count)
+    half = rows // 2
+    extra = vectors.shape[0]
+
+    def body(scal, mix, out, vectors, *made):
+        core = scal[3]
+        for h in range(2):
+            kept, sent = made[h], made[2 + h]
+            for t in range(3):
+                sides = []
+                for s in range(2):
+                    blocks = range(h * count // 2, (h + 1) * count // 2)
+                    at = [t * width + (2 * b + s) * lanes for b in blocks]
+                    sides.append(jnp.concatenate([mix[:, i : i + lanes] for i in at], axis=1))
+                part = slice(t * rows, (t + 1) * rows)
+                kept[part, :], sent[part, :] = side_pick(core, *sides)
+            for j in range(2):
+                columns = slice((2 * h + j) * GROUP, (2 * h + j + 1) * GROUP)
+                part = slice(3 * rows + j * half, 3 * rows + (j + 1) * half)
+                kept[part, :], sent[part, :] = side_pick(
+                    core, out[:half, columns], out[half:, columns]
+                )
+            for target in (kept, sent):
+                target[4 * rows :, :] = vectors[...]
+
+    return run_kernel(
+        body,
+        "pack_mix",
+        [(scal, "s"), (mix, "v"), (out, "v"), (vectors, "v")],
+        [((4 * rows + extra, GROUP), BF16, "v")] * 4,
+        [],
+        8 * rows * width,
+    )
+
+
+def pack_feed(params, up, down, scal, deps):
+    rows, count = params
+    inner, width = up.shape[1], down.shape[1]
+    lanes = inner // (2 * count)
+    wide, narrow = inner // 8, width // 2
+
+    def body(scal, up, down, *made):
+        core = scal[3]
+        for h in range(2):
+            kept, sent = made[h], made[2 + h]
+            for j in range(2):
+                sides = []
+                for s in range(2):
+                    first = (2 * h + j) * wide // lanes
+                    at = [(2 * (first + q) + s) * lanes for q in range(wide // lanes)]
+                    sides.append(jnp.concatenate([up[:, i : i + lanes] for i in at], axis=1))
+                part = slice(j * rows, (j + 1) * rows)
+                kept[part, :], sent[part, :] = side_pick(core, *sides)
+            columns = slice(h * narrow, (h + 1) * narrow)
+            part = slice(2 * rows, 4 * rows)
+            kept[part, :], sent[part, :] = side_pick(
+                core, down[: 2 * rows, columns], down[2 * rows :, columns]
+            )
+
+    return run_kernel(
+        body,
+        "pack_feed",
+        [(scal, "s"), (up, "v"), (down, "v")],
+        [((4 * rows, wide), BF16, "v")] * 4,
+        [],
+        8 * rows * inner,
+        deps=deps,
+    )
+
+
+def take_vectors(params, pieces, scal):
+    rows, count = params
+    width = rows * count
+    first = 4 * rows
+    extra = pieces[0].shape[0] - first
+
+    def body(scal, *rest):
+        pieces, (made, up_bias, mix_bias, held, sems) = rest[:count], rest[count:]
+        pairs = [
+            (pieces[k].at[first : first + extra, 0:rows], held.at[:, block_rows(scal, k, rows)])
+            for k in range(count)
         ]
-        mixes.append(jnp.stack(parts, axis=1).reshape(rows, 3, count, width // (2 * count)))
+        wait_all(start_all(pairs, sems))
+        made[...] = held[...].astype(F32)
+        low = scal[3] == 0
         half = rows // 2
-        outs.append(
-            jnp.concatenate(
-                [
-                    halves[h][3 * rows + j * half : 3 * rows + (j + 1) * half]
-                    for h in range(2)
-                    for j in range(2)
-                ],
-                axis=1,
-            )
-        )
-    return jnp.stack(mixes, axis=3).reshape(rows, 3 * width), jnp.concatenate(outs, axis=0)
-
-
-def pack_feed(up, down, side, count):
-    rows, inner = up.shape
-    split = up.reshape(rows, count, 2, inner // (2 * count))[:, :, side].reshape(rows, inner // 2)
-    half = down[side * 2 * rows : (side + 1) * 2 * rows]
-    wide, narrow = inner // 8, down.shape[1] // 2
-    return [
-        jnp.concatenate(
-            [split[:, (2 * h + j) * wide : (2 * h + j + 1) * wide] for j in range(2)]
-            + [half[:, h * narrow : (h + 1) * narrow]],
-            axis=0,
-        )
-        for h in range(2)
-    ]
-
-
-def unpack_feed(sides, count):
-    rows = sides[0][0].shape[0] // 4
-    ups, downs = [], []
-    for halves in sides:
-        up = jnp.concatenate(
-            [halves[h][j * rows : (j + 1) * rows] for h in range(2) for j in range(2)], axis=1
-        )
-        ups.append(up.reshape(rows, count, up.shape[1] // count))
-        downs.append(jnp.concatenate([halves[h][2 * rows :] for h in range(2)], axis=1))
-    up = jnp.stack(ups, axis=2)
-    return up.reshape(rows, -1), jnp.concatenate(downs, axis=0)
+        for b in range(count):
+            at = b * rows
+            for j in range(2):
+                columns = slice((2 * b + j) * rows, (2 * b + j + 1) * rows)
+                up_bias[:, columns] = jnp.where(
+                    low, made[10 + j : 11 + j, at : at + rows], made[12 + j : 13 + j, at : at + rows]
+                )
+        for index, t in ((2, 0), (3, 2)):
+            row = made[index : index + 1, :]
+            parts = [
+                jnp.where(
+                    low,
+                    row[:, b * rows : b * rows + half],
+                    row[:, b * rows + half : (b + 1) * rows],
+                )
+                for b in range(count)
+            ]
+            joint = jnp.concatenate(parts, axis=1)
+            for h in range(2):
+                at = (3 * h + t) * GROUP
+                mix_bias[:, at : at + GROUP] = joint[:, h * GROUP : (h + 1) * GROUP]
+        for h in range(2):
+            at = (3 * h + 1) * GROUP
+            mix_bias[:, at : at + GROUP] = jnp.zeros((1, GROUP), F32)
+
+    return run_kernel(
+        body,
+        "take_vectors",
+        [(scal, "s")] + [(pieces[2 * k], "a") for k in range(count)],
+        [((extra, width), F32, "v"), ((1, 2 * width), F32, "v"), ((1, 6 * GROUP), F32, "v")],
+        [pltpu.VMEM((extra, width), BF16), pltpu.SemaphoreType.DMA((count,))],
+        width,
+    )
+
+
+def unpack_mix(params, own, far, scal, dtype):
+    rows, count = params
+    width = rows * count
+    lanes = width // (2 * count)
+    half = rows // 2
+    extra = own[0].shape[0] - 4 * rows
+
+    def body(scal, own0, own1, far0, far1, mix, out, vectors):
+        for h, (mine, other) in enumerate(((own0, far0), (own1, far1))):
+            for t in range(3):
+                part = slice(t * rows, (t + 1) * rows)
+                for s, value in enumerate(side_pick(scal[3], mine[part, :], other[part, :])):
+                    value = value.astype(dtype)
+                    for q in range(count // 2):
+                        at = t * width + (2 * (h * count // 2 + q) + s) * lanes
+                        mix[:, at : at + lanes] = value[:, q * lanes : (q + 1) * lanes]
+            for j in range(2):
+                part = slice(3 * rows + j * half, 3 * rows + (j + 1) * half)
+                columns = slice((2 * h + j) * GROUP, (2 * h + j + 1) * GROUP)
+                for s, value in enumerate(side_pick(scal[3], mine[part, :], other[part, :])):
+                    out[s * half : (s + 1) * half, columns] = value.astype(dtype)
+        sides = side_pick(scal[3], own0[4 * rows :, :], far0[4 * rows :, :])
+        for s, value in enumerate(sides):
+            vectors[s * extra : (s + 1) * extra, :] = value.astype(F32)
+
+    return run_kernel(
+        body,
+        "unpack_mix",
+        [(scal, "s")] + [(v, "v") for v in own + far],
+        [
+            ((rows, 3 * width), dtype, "v"),
+            ((rows, width), dtype, "v"),
+            ((2 * extra, GROUP), F32, "v"),
+        ],
+        [],
+        8 * rows * width,
+    )
+
+
+def unpack_feed(params, own, far, scal, dtype):
+    rows, count = params
+    width = rows * count
+    wide = own[0].shape[1]
+    inner = 8 * wide
+    lanes = inner // (2 * count)
+
+    def body(scal, own0, own1, far0, far1, up, down):
+        for h, (mine, other) in enumerate(((own0, far0), (own1, far1))):
+            for j in range(2):
+                part = slice(j * rows, (j + 1) * rows)
+                for s, value in enumerate(side_pick(scal[3], mine[part, :], other[part, :])):
+                    value = value.astype(dtype)
+                    for q in range(wide // lanes):
+                        at = (2 * ((2 * h + j) * wide // lanes + q) + s) * lanes
+                        up[:, at : at + lanes] = value[:, q * lanes : (q + 1) * lanes]
+            part = slice(2 * rows, 4 * rows)
+            for s, value in enumerate(side_pick(scal[3], mine[part, :], other[part, :])):
+                at = s * 2 * rows
+                down[at : at + 2 * rows, h * wide : (h + 1) * wide] = value.astype(dtype)
+
+    return run_kernel(
+        body,
+        "unpack_feed",
+        [(scal, "s")] + [(v, "v") for v in own + far],
+        [((rows, inner), dtype, "v"), ((4 * rows, width), dtype, "v")],
+        [],
+        8 * rows * inner,
+    )
 
 
 def body(activations, cotangent, lengths, *weights):
@@ -817,13 +1070,11 @@
     params = (rows, count)
     block = spot >> joined
 
-    def join(value):
+    def join(value, axis=0):
         for i in range(joined):
             far = swap(value, "fsdp", 1 << i)
             upper = ((spot >> i) & 1) == 1
-            value = jnp.concatenate(
-                [pick(upper, far, value), pick(upper, value, far)], axis=0
-            )
+            value = jnp.concatenate([pick(upper, far, value), pick(upper, value, far)], axis=axis)
         return value
 
     def unjoin(value):
@@ -832,48 +1083,39 @@
             upper = ((spot >> i) & 1) == 1
             low, high = value[:half], value[half:]
             value = add_low(pick(upper, high, low), swap(pick(upper, low, high), "fsdp", 1 << i))
-        return value
+        return value.astype(F32)[None]
+
+    low_micro = micro == 0
+    length = pick(low_micro, lengths[0, 0], lengths[1, 0])
+    scal = jnp.stack([block, parity, length, core]).astype(jnp.int32)
 
     def spread(packs):
-        sides = [packs(0), packs(1)]
         layers = [[], []]
         for h in range(2):
-            keep = pick(first, sides[0][h], sides[1][h])
-            far = swap(pick(first, sides[1][h], sides[0][h]), "section", 1)
+            keep, far = packs[h], swap(packs[2 + h], "section", 1)
             layers[0].append(pick(first, keep, far))
             layers[1].append(pick(first, far, keep))
         return layers
 
-    mix_shard, out_shard = join(mixweight[0]), join(outweight[0])
-    up_shard, down_shard = join(upweight[0]), join(downweight[0])
-    mix_halves = spread(lambda side: pack_mix(mix_shard, out_shard, side, count))
-    feed_halves = spread(lambda side: pack_feed(up_shard, down_shard, side, count))
-    mix_pieces, feed_pieces = [], []
-    for layer in range(2):
-        mix_pieces.append(gather_blocks(mix_halves[layer], bits))
-        feed_pieces.append(gather_blocks(feed_halves[layer], bits))
-
-    packed = jnp.concatenate(
+    vectors = jnp.stack(
         [mixgain[0], mixshift[0], mixbias[0, 0], mixbias[0, 1], outbias[0], mixscale[0]]
-        + [feedgain[0], feedshift[0], downbias[0], feedscale[0], upbias[0]]
-    )
-    packed = lax.all_gather(packed, ("section", "fsdp"), axis=0)
-    packed = packed.reshape(2, shards, -1).astype(F32)
-
-    def vector(layer, index):
-        taken = packed[layer, :, index * base_rows : (index + 1) * base_rows]
-        return taken.reshape(1, width)
-
-    def half_vector(value):
-        value = value.reshape(count, 2, -1)
-        return pick(first, value[:, 0], value[:, 1]).reshape(1, -1)
-
-    def mix_bias(layer):
-        query = half_vector(vector(layer, 2)).reshape(2, 1, GROUP)
-        value = half_vector(vector(layer, 3)).reshape(2, 1, GROUP)
-        return jnp.concatenate([query, jnp.zeros_like(query), value], axis=1).reshape(1, -1)
-
-    low_micro = micro == 0
+        + [feedgain[0], feedshift[0], downbias[0], feedscale[0]]
+    )
+    vectors = jnp.concatenate(
+        [join(vectors, 1), join(upbias[0]).reshape(4, rows), jnp.zeros((2, rows), BF16)], axis=0
+    )
+    if rows < GROUP:
+        vectors = jnp.concatenate([vectors, jnp.zeros((16, GROUP - rows), BF16)], axis=1)
+    mix_halves = spread(pack_mix(params, join(mixweight[0]), join(outweight[0]), vectors, scal))
+    mix_parts = [gather_blocks(halves, bits) for halves in mix_halves]
+    mix_pieces, mix_stages = zip(*mix_parts)
+    ready = mix_stages[0][0] + mix_stages[0][1]
+    feed_halves = spread(
+        pack_feed(params, join(upweight[0]), join(downweight[0]), scal, ready)
+    )
+    feed_parts = [gather_blocks(halves, bits) for halves in feed_halves]
+    feed_pieces, feed_stages = zip(*feed_parts)
+
     tokens = activations.shape[2]
 
     def to_pair(value):
@@ -883,41 +1125,46 @@
 
     def from_pair(value):
         low, high = value[:tokens], value[tokens:]
-        far = swap(pick(low_micro, high, low).astype(BF16), "seq", 2).astype(value.dtype)
+        far = swap(pick(low_micro, high, low).astype(BF16), "seq", 2)
+        wide = far.astype(value.dtype)
         keep = pick(low_micro, low, high)
-        return jnp.stack([pick(low_micro, keep, far), pick(low_micro, far, keep)])[None, :, None]
-
-    length = pick(low_micro, lengths[0, 0], lengths[1, 0])
-    scal = jnp.stack([block, parity, length]).astype(jnp.int32)
+        made = jnp.stack([pick(low_micro, keep, wide), pick(low_micro, wide, keep)])
+        return made[None, :, None], far
 
     hidden = to_pair(activations)
     incoming = to_pair(cotangent)
     kept, results = [], []
     for layer in range(2):
         pieces, feeds = mix_pieces[layer], feed_pieces[layer]
-        normed, keep, send = mix_forward(
-            params, hidden, vector(layer, 0), vector(layer, 1), mix_bias(layer), scal, pieces
-        )
+        vectors, up_bias, mix_bias = take_vectors(params, pieces, scal)
+        normed, keep, send = mix_forward(params, hidden, vectors, mix_bias, scal, pieces, [])
         other = swap(send, "seq", 1)
-        out_keep, out_send, peaks = attend_forward(keep, other, scal)
+        out_keep, out_send, peaks = attend_forward(
+            keep, other, scal, feed_stages[layer][0] + feed_stages[layer][1] + [incoming]
+        )
         out_other = swap(out_send, "seq", 1)
-        mixed, own, send = out_forward(params, out_keep, out_other, scal, pieces, width)
+        mixed, own, send = out_forward(
+            params, out_keep, out_other, scal, pieces, width, feed_stages[layer][2]
+        )
         far = swap(send, "section", 1)
-        vectors = jnp.concatenate([vector(layer, i) for i in (4, 5, 6, 7)], axis=0)
-        up_bias = half_vector(packed[layer, :, 10 * base_rows :].reshape(1, inner))
         branch, residual, normed_two, active, slope, own, send = feed_forward(
-            params, hidden, own, far, vectors, up_bias, scal, feeds
+            params, hidden, own, far, vectors, up_bias, scal, feeds,
+            mix_stages[1][0] + mix_stages[1][1] if layer == 0 else [],
         )
         far = swap(send, "section", 1)
         kept.append(
             (hidden, normed, keep, other, peaks, mixed, branch, residual, normed_two, active)
             + (slope, own, far, vectors)
         )
-        made = own + far.astype(F32) + vector(layer, 8)
-        hidden = (residual + vector(layer, 9) * made).astype(BF16)
+        hidden = layer_result(
+            residual, own, far, vectors,
+            mix_stages[1][2] + feed_stages[1][0] if layer == 0 else [],
+        )
         results.append(hidden)
 
-    gradients, sums, mix_shares, feed_shares = [None] * 2, [None] * 2, [None] * 2, [None] * 2
+    section_output, sent = from_pair(pick(first, results[0], results[1]))
+    gradients, mix_shares, feed_shares = [None] * 2, [None] * 2, [None] * 2
+    waits = {"attend": [sent]}
     for layer in (1, 0):
         pieces, feeds = mix_pieces[layer], feed_pieces[layer]
         hidden, normed, keep, other, peaks, mixed, branch, residual, normed_two, active = kept[
@@ -925,91 +1172,82 @@
         ][:10]
         slope, branch_own, branch_far, vectors = kept[layer][10:]
         lower, up_grad, up_sum, own, send = feed_backward(
-            params, incoming, vector(layer, 9), slope, scal, feeds
+            params, incoming, vectors, slope, scal, feeds, waits.get("feed", [])
         )
         far = swap(send, "section", 1)
-        grads = feed_weights(params, active, lower, normed_two, up_grad, scal)
-        feed_shares[layer] = [sum_line(v) for v in scatter_blocks(grads, bits)]
-        feed_sum = feed_sums(incoming, branch_own, branch_far, vector(layer, 8), lower)
+        grads = feed_weights(params, active, lower, normed_two, up_grad, scal, [branch_far])
+        feed_share, feed_hops = scatter_blocks(grads, bits)
+        feed_shares[layer], feed_lines = sum_shares(feed_share, layer)
+        feed_sum = feed_sums(incoming, branch_own, branch_far, vectors, lower)
         residual_grad, branch_grad, grad_keep, grad_send, out_sum = out_backward(
-            params, incoming, residual, own, far, branch, vectors, scal, pieces
+            params, incoming, residual, own, far, branch, vectors, scal, pieces, waits.get("out", [])
         )
         grad_other = swap(grad_send, "seq", 1)
         triple_keep, triple_send = attend_backward(
-            keep, other, grad_keep, grad_other, peaks, scal
+            keep, other, grad_keep, grad_other, peaks, scal, waits.get("attend", [])
         )
         triple_other = swap(triple_send, "seq", 1)
-        triple, own, send = mix_backward(params, triple_keep, triple_other, scal, pieces, width)
+        triple, own, send = mix_backward(
+            params, triple_keep, triple_other, scal, pieces, width, waits.get("mix", []) + feed_hops[0]
+        )
         far = swap(send, "section", 1)
-        *grads, mix_sum = mix_weights(params, normed, triple, mixed, branch_grad, scal)
-        mix_shares[layer] = [sum_line(v) for v in scatter_blocks(grads, bits)]
-        input_grad, incoming, in_sum = input_backward(
-            hidden, own, far, residual_grad, vector(layer, 0)
-        )
+        input_grad, incoming, in_sum = input_backward(hidden, own, far, residual_grad, vectors)
         gradients[layer] = input_grad
-        mix_sum = mix_sum.reshape(2, 3, GROUP)
-        sums[layer] = (
-            jnp.concatenate([in_sum[:2], out_sum[:4], feed_sum[:2]], axis=0).reshape(-1),
-            jnp.concatenate([up_sum.reshape(-1), mix_sum[:, 0].reshape(-1), mix_sum[:, 2].reshape(-1)]),
-        )
-
-    whole = pick(first, sums[0][0], sums[1][0])
-    own_half = pick(first, sums[0][1], sums[1][1])
-    far_half = swap(pick(first, sums[1][1], sums[0][1]), "section", 1)
-    totals = jnp.concatenate(
-        [whole, pick(first, own_half, far_half), pick(first, far_half, own_half)]
-    ).reshape(-1, 128)
-    for axis in ("fsdp", "seq"):
-        bit = 1
-        while bit < lax.axis_size(axis):
-            totals = totals + swap(totals, axis, bit)
-            bit *= 2
-    totals = totals.reshape(-1)
-    whole = totals[: 8 * width].reshape(8, width)
-    halves = totals[8 * width :].reshape(2, -1)
-    half = inner // 2
-    up_total = jnp.stack([halves[s, :half].reshape(count, -1) for s in range(2)], axis=1)
-    bias_total = jnp.stack(
-        [halves[s, half:].reshape(2, count, -1) for s in range(2)], axis=2
-    ).reshape(2, width)
-
-    def own_part(value, size):
-        return lax.dynamic_slice_in_dim(value, spot * size, size, axis=value.ndim - 1)
-
-    whole = own_part(whole, base_rows)[:, None]
-    up_total = own_part(up_total.reshape(inner), inner // shards)[None]
-    bias_total = own_part(bias_total, base_rows)[None]
-
-    def collect(shares):
-        sides = [[], []]
-        for h in range(2):
-            early = lax.ppermute(shares[1][h], "section", [(0, 1)])
-            late = lax.ppermute(shares[0][h], "section", [(1, 0)])
-            sides[0].append(pick(first, shares[0][h], early))
-            sides[1].append(pick(first, late, shares[1][h]))
-        return sides
-
-    mix_total, out_total = unpack_mix(collect(mix_shares), count)
-    up_weight, down_weight = unpack_feed(collect(feed_shares), count)
-
-    def final(value):
-        return unjoin(value).astype(F32)[None]
+        after = []
+        if layer == 0:
+            input_gradient, sent = from_pair(pick(first, gradients[0], gradients[1]))
+            after = [sent]
+        grads = mix_weights(
+            params, normed, triple, mixed, branch_grad, [in_sum, out_sum, feed_sum, up_sum], scal,
+            waits.get("weights", []) + (feed_hops[1] if layer == 0 else []),
+        )
+        mix_share, mix_hops = scatter_blocks(grads, bits, after)
+        mix_shares[layer], mix_lines = sum_shares(mix_share, layer)
+        waits = {
+            "feed": sum(feed_hops[1:], []),
+            "out": mix_hops[0],
+            "attend": sum(mix_hops[1:], []),
+            "mix": [moved[0] for moved in feed_lines],
+            "weights": [moved[1] for moved in feed_lines] + [moved[0] for moved in mix_lines],
+        }
+
+    def collect(unpack, shares):
+        own = [pick(first, low, high) for low, high in zip(*shares)]
+        far = [swap(pick(first, high, low), "section", 1) for low, high in zip(*shares)]
+        return unpack(params, own, far, scal, BF16 if joined else F32)
+
+    up_weight, down_weight = (unjoin(v) for v in collect(unpack_feed, feed_shares))
+    *made, sums = collect(unpack_mix, mix_shares)
+    mix_total, out_total = (unjoin(v) for v in made)
+
+    extra = sums.shape[0] // 2
+    sums = sums[:, :rows].reshape(2, extra, rows)
+    place = spot & ((1 << joined) - 1)
+
+    def own_part(value):
+        size = value.shape[-1] >> joined
+        return lax.dynamic_slice_in_dim(value, place * size, size, axis=value.ndim - 1)
+
+    whole = own_part(sums[0, :8])[:, None]
+    up_total = own_part(sums[:, 8:10].reshape(1, 4 * rows))
+    bias_total = sums[:, 10].reshape(2, 2, rows // 2).transpose(1, 0, 2).reshape(2, rows)
+    bias_total = own_part(bias_total)[None]
 
     return (
-        from_pair(pick(first, results[0], results[1])),
-        from_pair(pick(first, gradients[0], gradients[1])),
+        section_output,
+        input_gradient,
         whole[0],
         whole[1],
-        final(mix_total),
+        mix_total,
         bias_total,
-        final(out_total),
+        out_total,
         whole[5],
         whole[4],
         whole[2],
         whole[3],
-        final(up_weight),
+        up_weight,
         up_total,
-        final(down_weight),
+        down_weight,
         whole[7],
         whole[6],
     )

time: 985 us -> 747 us (0.76)
  local copies, waits for them, and re-layouts: 139 us -> 38.1 us
  other arithmetic: 90.9 us -> 23.5 us
  starting transfers between devices: 139 us -> 97.8 us
  blocking collectives: 23.5 us -> 0 us
    unnamed x401 -> x270, local copies, waits for them, and re-layouts: 72 us -> 32.7 us
    another operation x20 -> x4, local copies, waits for them, and re-layouts: 32.4 us -> 1.37 us  [the longest x1 0.76 us: body(): jnp.stack([mixgain[0], mixshift[0], mixbias[0, 0], mixbias[0, 1], outbias...]
    select_n x27 -> x13, other arithmetic: 29.1 us -> 1.86 us  [pick(): return jnp.where(flag, first, second)]
    all_gather x1 -> x0, blocking collectives: 23.5 us -> none  [body(): packed = lax.all_gather(packed, ('section', 'fsdp'), axis=0)]
    slice x41 -> x2, local copies, waits for them, and re-layouts: 21.6 us -> 0.01 us  [the longest x1 0.01 us: body(): sums[:, 10].reshape(2, 2, rows // 2).transpose(1, 0, 2).reshape(2, rows)]
    ppermute x77 -> x68, starting transfers between devices: 76.6 us -> 56.3 us  [swap(): return lax.ppermute(value, axis, [(i, i ^ bit) for i in range(count)])]
    ppermute x24 -> x12, starting transfers between devices: 51.9 us -> 33.4 us  [the longest x6 29.1 us: sum_line(): inward = lax.ppermute(value, 'seq', [(0, 1), (3, 2)])]
    convert_element_type x32 -> x26, other arithmetic: 31.6 us -> 14.9 us  [add_low(): return (left.astype(F32) + right.astype(F32)).astype(BF16)]
  transfers between devices with their start and end apart: 109 -> 86, of which waited for: 42 -> 41; matrix products, arithmetic and copies ran while one was open for 15% -> 3% of each run, Pallas kernels for 14% -> 22%
where the time goes in v2:
time: 747 us; the launch traced here: 743 us
  waiting for transfers between devices  386 us (52%)
  Pallas kernels  193 us (26%)
  starting transfers between devices  97.8 us (13%)
  local copies, waits for them, and re-layouts  38.1 us (5%)
  other arithmetic  23.5 us (3%)
    ppermute x68, waiting for transfers between devices, swap(): return lax.ppermute(value, axis, [(i, i ^ bit) for i in range(count)])  271 us
    pallas_call x34, Pallas kernels, run_kernel(): pl.pallas_call(body, name=name, out_shape=[jax.ShapeDtypeStruct(s, d) for...  193 us
    ppermute x6, waiting for transfers between devices, sum_line(): back = lax.ppermute(both, 'seq', [(1, 0), (2, 3)])  73.7 us
    ppermute x68, starting transfers between devices, swap(): return lax.ppermute(value, axis, [(i, i ^ bit) for i in range(count)])  56.3 us
    ppermute x6, waiting for transfers between devices, sum_line(): inward = lax.ppermute(value, 'seq', [(0, 1), (3, 2)])  41 us
    unnamed x270, local copies, waits for them, and re-layouts  32.7 us
    ppermute x6, starting transfers between devices, sum_line(): inward = lax.ppermute(value, 'seq', [(0, 1), (3, 2)])  29.1 us
  transfers between devices with their start and end apart: 86, of which 41 were waited for; matrix products, arithmetic and copies ran while one was open for 3% of the time, Pallas kernels for 22%

profile of v2, /device:TPU:0, one launch (start us, length us, event | category | flops | bytes accessed | tf_op | source)
XLA Modules:
  0.0 742.6 jit_solution(2367133420578514040)
XLA Ops:
  16.9 10.6 %collective-permute-done.8.refs_2_.refs_3_.refs_8_.refs_9_.refs_13_.refs_10_ = bf16[1040,256]{1,0:T(8,128)(2,1)S(1)} collective-permute-done((bf16[1040,256]{1,0:T(8,128)(2,1)S(1)}, bf16[1040,256]{1,0:T(8,128)(2,1)S(1)}, u32[]{:S(2)}, u32[]{:S(2)}) %collective-permute-start.8) | collective-permute-done | bytes 532512 | tf_op jit(solution)/shard_map/ppermute | solution.py:792
  29.7 10.3 %collective-permute-done.9.refs_3_.refs_7_.refs_8_.refs_12_.refs_9_ = bf16[1040,256]{1,0:T(8,128)(2,1)S(1)} collective-permute-done((bf16[1040,256]{1,0:T(8,128)(2,1)S(1)}, bf16[1040,256]{1,0:T(8,128)(2,1)S(1)}, u32[]{:S(2)}, u32[]{:S(2)}) %collective-permute-start.9) | collective-permute-done | bytes 532512 | tf_op jit(solution)/shard_map/ppermute | solution.py:792
  48.9 18.7 %collective-permute-done.16 = bf16[256,1024]{1,0:T(8,128)(2,1)S(1)} collective-permute-done((bf16[256,1024]{1,0:T(8,128)(2,1)S(1)}, bf16[256,1024]{1,0:T(8,128)(2,1)S(1)}, u32[]{:S(2)}, u32[]{:S(2)}) %collective-permute-start.16) | collective-permute-done | bytes 524320 | tf_op jit(solution)/shard_map/ppermute | solution.py:792
  67.7 14.4 %collective-permute-done.24.refs_4_.refs_10_.refs_11_.refs_15_.refs_12_ = bf16[1040,256]{1,0:T(8,128)(2,1)S(1)} collective-permute-done((bf16[1040,256]{1,0:T(8,128)(2,1)S(1)}, bf16[1040,256]{1,0:T(8,128)(2,1)S(1)}, u32[]{:S(2)}, u32[]{:S(2)}) %collective-permute-start.24) | collective-permute-done | bytes 532512 | tf_op jit(solution)/shard_map/ppermute | solution.py:792
  84.8 4.6 mix_forward.2
  94.8 15.3 %collective-permute-done.26.refs_7_.refs_4_ = bf16[512,768]{1,0:T(8,128)(2,1)S(1)} collective-permute-done((bf16[512,768]{1,0:T(8,128)(2,1)S(1)}, bf16[512,768]{1,0:T(8,128)(2,1)S(1)}, u32[]{:S(2)}, u32[]{:S(2)}) %collective-permute-start.26) | collective-permute-done | bytes 786464 | tf_op jit(solution)/shard_map/ppermute | solution.py:792
  110.2 13.7 %attend_forward.2 = (bf16[512,256]{1,0:T(8,128)(2,1)S(1)}, bf16[512,256]{1,0:T(8,128)(2,1)S(1)}, f32[8,1024]{1,0:T(8,128)S(1)}) custom-call(bf16[1024,512]{1,0:T(8,128)(2,1)S(1)} %collective-permute-done.17.refs_0_.refs_12_.refs_8_, bf16[1024,512]{1,0:T(8,128)(2,1)S(1)} %collective-permute-done.19.refs_1_.refs_15_.refs_11_, ...), custom_call_target="tpu_custom_call" | custom-call | flops 1073741824 | bytes 2129936 | tf_op jit(solution)/shard_map/attend_forward/pallas_call | solution.py:50
  124.3 6.1 collective-permute-done.27.refs_4_
  138.4 10.8 %collective-permute-done.14.refs_2_.refs_3_.refs_8_.refs_9_.refs_11_ = bf16[1040,256]{1,0:T(8,128)(2,1)S(1)} collective-permute-done((bf16[1040,256]{1,0:T(8,128)(2,1)S(1)}, bf16[1040,256]{1,0:T(8,128)(2,1)S(1)}, u32[]{:S(2)}, u32[]{:S(2)}) %collective-permute-start.14) | collective-permute-done | bytes 532512 | tf_op jit(solution)/shard_map/ppermute | solution.py:792
  151.3 10.0 %collective-permute-done.15.refs_3_.refs_7_.refs_8_.refs_10_ = bf16[1040,256]{1,0:T(8,128)(2,1)S(1)} collective-permute-done((bf16[1040,256]{1,0:T(8,128)(2,1)S(1)}, bf16[1040,256]{1,0:T(8,128)(2,1)S(1)}, u32[]{:S(2)}, u32[]{:S(2)}) %collective-permute-start.15) | collective-permute-done | bytes 532512 | tf_op jit(solution)/shard_map/ppermute | solution.py:792
  164.1 17.1 %feed_forward.2 = (f32[512,1024]{1,0:T(8,128)}, f32[512,1024]{1,0:T(8,128)}, bf16[512,1024]{1,0:T(8,128)(2,1)S(1)}, bf16[512,2048]{1,0:T(8,128)(2,1)}, bf16[512,...) custom-call(bf16[1040,256]{1,0:T(8,128)(2,1)S(1)} %collective-permute-done.1.refs_0_.refs_2_.refs_6_.refs_7_.ref, ...), custom_call_target="tpu_custom_call" | custom-call | flops 4294967296 | bytes 25239568 | tf_op jit(solution)/shard_map/feed_forward/pallas_call | solution.py:50
  184.3 11.6 %collective-permute-done.2.refs_0_.refs_4_.refs_10_.refs_11_.refs_13_ = bf16[1040,256]{1,0:T(8,128)(2,1)S(1)} collective-permute-done((bf16[1040,256]{1,0:T(8,128)(2,1)S(1)}, bf16[1040,256]{1,0:T(8,128)(2,1)S(1)}, u32[]{:S(2)}, u32[]{:S(2)}) %collective-permute-start.2) | collective-permute-done | bytes 532512 | tf_op jit(solution)/shard_map/ppermute | solution.py:792
  202.3 4.6 mix_forward.3
  209.1 12.9 %collective-permute-done.32.refs_2_.refs_10_.refs_8_ = bf16[1024,512]{1,0:T(8,128)(2,1)S(1)} collective-permute-done((bf16[1024,512]{1,0:T(8,128)(2,1)S(1)}, bf16[1024,512]{1,0:T(8,128)(2,1)S(1)}, u32[]{:S(2)}, u32[]{:S(2)}) %collective-permute-start.32) | collective-permute-done | bytes 1048608 | tf_op jit(solution)/shard_map/ppermute | solution.py:792
  225.5 14.1 %attend_forward.3 = (bf16[512,256]{1,0:T(8,128)(2,1)S(1)}, bf16[512,256]{1,0:T(8,128)(2,1)S(1)}, f32[8,1024]{1,0:T(8,128)S(1)}) custom-call(bf16[1024,512]{1,0:T(8,128)(2,1)S(1)} %collective-permute-done.11.refs_2_.refs_0_.refs_8_.refs_6_, bf16[1024,512]{1,0:T(8,128)(2,1)S(1)} %collective-permute-done.13.refs_3_.refs_1_.refs_11_.refs_9_, ...), custom_call_target="tpu_custom_call" | custom-call | flops 1073741824 | bytes 2129936 | tf_op jit(solution)/shard_map/attend_forward/pallas_call | solution.py:50
  251.8 16.9 %feed_forward.3 = (f32[512,1024]{1,0:T(8,128)S(1)}, f32[512,1024]{1,0:T(8,128)}, bf16[512,1024]{1,0:T(8,128)(2,1)S(1)}, bf16[512,2048]{1,0:T(8,128)(2,1)}, bf16[...) custom-call(s32[4]{0:T(128)S(1)} %pad_add_fusion.refs_0_.refs_4_.refs_5_.refs_2_.refs_1_.refs_3_, ...), custom_call_target="tpu_custom_call" | custom-call | flops 4294967296 | bytes 25239568 | tf_op jit(solution)/shard_map/feed_forward/pallas_call | solution.py:50
  275.5 9.1 %feed_backward.2 = (bf16[512,1024]{1,0:T(8,128)(2,1)S(1)}, bf16[512,2048]{1,0:T(8,128)(2,1)S(1)}, f32[1,2048]{1,0:T(1,128)S(1)}, f32[512,1024]{1,0:T(8,128)S(1)}, bf16[512,1024]{1,0:T(8,128)(2,1)}) custom-call(s32[4]{0:T(128)S(1)} %pad_add_fusion.refs_0_.refs_4_.refs_5_.refs_2_.refs_1_.refs_3_, ...), custom_call_target="tpu_custom_call" | custom-call | flops 4294967296 | bytes 17899536 | tf_op jit(solution)/shard_map/feed_backward/pallas_call | solution.py:50
  287.0 8.4 %feed_weights.2 = (bf16[2048,512]{1,0:T(8,128)(2,1)}, bf16[1024,512]{1,0:T(8,128)(2,1)S(1)}, bf16[1024,512]{1,0:T(8,128)(2,1)S(1)}, bf16[2048,512]{1,0:T(8,128)(...) custom-call(bf16[512,1024]{1,0:T(8,128)(2,1)S(1)} %collective-permute-done.37.refs_2_.refs_0_, ...), custom_call_target="tpu_custom_call" | custom-call | flops 4294967296 | bytes 14680080 | tf_op jit(solution)/shard_map/feed_weights/pallas_call | solution.py:50
  301.8 4.7 out_backward.2
  307.9 10.6 %collective-permute-done.45.refs_5_ = bf16[512,256]{1,0:T(8,128)(2,1)S(1)} collective-permute-done((bf16[512,256]{1,0:T(8,128)(2,1)S(1)}, bf16[512,256]{1,0:T(8,128)(2,1)S(1)}, u32[]{:S(2)}, u32[]{:S(2)}) %collective-permute-start.45) | collective-permute-done | bytes 262176 | tf_op jit(solution)/shard_map/ppermute | solution.py:792
  318.5 6.3 collective-permute-done.38.refs_0_
  324.8 16.9 %attend_backward.2 = (bf16[512,768]{1,0:T(8,128)(2,1)S(1)}, bf16[512,768]{1,0:T(8,128)(2,1)S(1)}) custom-call(bf16[256,1024]{1,0:T(8,128)(2,1)S(1)} %collective-permute-done.38.refs_0_, s32[4]{0:T(128)S(1)} %pad_add_fusion.refs_0_.refs_4_.refs_5_.refs_2_.refs_1_.refs_3_, bf16[512,768]{1,0:T(8,128)(2,1)S(1)} %copy-done.116, bf16[512,768]{1,0:T(8,128)(2,1)S(1)} %copy-done.108, ...), custom_call_target="tpu_custom_call" | custom-call | flops 2684354560 | bytes 3702800 | tf_op jit(solution)/shard_map/attend_backward/pallas_call | solution.py:50
  342.3 18.3 %collective-permute-done.46.refs_4_ = bf16[512,768]{1,0:T(8,128)(2,1)S(1)} collective-permute-done((bf16[512,768]{1,0:T(8,128)(2,1)S(1)}, bf16[512,768]{1,0:T(8,128)(2,1)S(1)}, u32[]{:S(2)}, u32[]{:S(2)}) %collective-permute-start.46) | collective-permute-done | bytes 786464 | tf_op jit(solution)/shard_map/ppermute | solution.py:792
  360.6 4.6 mix_backward.2
  382.5 6.0 mix_weights.2
  395.9 9.1 %feed_backward.3 = (bf16[512,1024]{1,0:T(8,128)(2,1)S(1)}, bf16[512,2048]{1,0:T(8,128)(2,1)S(1)}, f32[1,2048]{1,0:T(1,128)S(1)}, f32[512,1024]{1,0:T(8,128)S(1)}, bf16[512,1024]{1,0:T(8,128)(2,1)}) custom-call(bf16[1024,512]{1,0:T(8,128)(2,1)} %collective-permute-done.40.refs_0_, bf16[1024,512]{1,0:T(8,128)(2,1)} %collective-permute-done.42.refs_1_, ...), custom_call_target="tpu_custom_call" | custom-call | flops 4294967296 | bytes 17899536 | tf_op jit(solution)/shard_map/feed_backward/pallas_call | solution.py:50
  411.5 5.9 collective-permute-done.50.refs_0_
  418.4 14.5 %collective-permute-done.52.refs_1_ = bf16[2080,256]{1,0:T(8,128)(2,1)S(1)} collective-permute-done((bf16[2080,256]{1,0:T(8,128)(2,1)}, bf16[2080,256]{1,0:T(8,128)(2,1)S(1)}, u32[]{:S(2)}, u32[]{:S(2)}) %collective-permute-start.52) | collective-permute-done | bytes 1064992 | tf_op jit(solution)/shard_map/ppermute | solution.py:792
  439.7 5.0 out_backward.3
  446.7 7.7 %feed_weights.3 = (bf16[2048,512]{1,0:T(8,128)(2,1)S(1)}, bf16[1024,512]{1,0:T(8,128)(2,1)S(1)}, bf16[1024,512]{1,0:T(8,128)(2,1)S(1)}, bf16[2048,512]{1,0:T(8,1...) custom-call(bf16[512,1024]{1,0:T(8,128)(2,1)S(1)} %copy-done.28, ...), custom_call_target="tpu_custom_call" | custom-call | flops 4294967296 | bytes 14680080 | tf_op jit(solution)/shard_map/feed_weights/pallas_call | solution.py:50
  457.2 32.2 %collective-permute-done.55.refs_6_ = bf16[512,256]{1,0:T(8,128)(2,1)S(1)} collective-permute-done((bf16[512,256]{1,0:T(8,128)(2,1)S(1)}, bf16[512,256]{1,0:T(8,128)(2,1)S(1)}, u32[]{:S(2)}, u32[]{:S(2)}) %collective-permute-start.55) | collective-permute-done | bytes 262176 | tf_op jit(solution)/shard_map/ppermute | solution.py:792
  489.9 16.7 %attend_backward.3 = (bf16[512,768]{1,0:T(8,128)(2,1)S(1)}, bf16[512,768]{1,0:T(8,128)(2,1)S(1)}) custom-call(bf16[1040,256]{1,0:T(8,128)(2,1)S(1)} %collective-permute-done.51.refs_0_, bf16[1040,256]{1,0:T(8,128)(2,1)} %collective-permute-done.53.refs_1_, s32[4]{0:T(128)S(1)} %pad_add_fusion.refs_0_.refs_4_.refs_5_.refs_2_.refs_1_.refs_3_, ...), custom_call_target="tpu_custom_call" | custom-call | flops 2684354560 | bytes 3702800 | tf_op jit(solution)/shard_map/attend_backward/pallas_call | solution.py:50
  517.1 20.8 %collective-permute-done.49.refs_2_ = bf16[2048,512]{1,0:T(8,128)(2,1)S(1)} collective-permute-done((bf16[2048,512]{1,0:T(8,128)(2,1)S(1)}, bf16[2048,512]{1,0:T(8,128)(2,1)S(1)}, u32[]{:S(2)}, u32[]{:S(2)}) %collective-permute-start.49) | collective-permute-done | bytes 2097184 | tf_op jit(solution)/shard_map/ppermute | solution.py:792
  542.7 4.1 collective-permute-done.60.refs_1_
  547.8 9.7 %collective-permute-done.61.refs_2_ = bf16[1024,512]{1,0:T(8,128)(2,1)S(1)} collective-permute-done((bf16[1024,512]{1,0:T(8,128)(2,1)S(1)}, bf16[1024,512]{1,0:T(8,128)(2,1)S(1)}, u32[]{:S(2)}, u32[]{:S(2)}) %collective-permute-start.61) | collective-permute-done | bytes 1048608 | tf_op jit(solution)/shard_map/ppermute | solution.py:792
  558.0 4.7 collective-permute-start.77
  571.3 5.4 mix_weights.3
  578.2 7.8 %collective-permute-done.77 = bf16[1024,512]{1,0:T(8,128)(2,1)S(1)} collective-permute-done((bf16[1024,512]{1,0:T(8,128)(2,1)S(1)}, bf16[1024,512]{1,0:T(8,128)(2,1)S(1)}, u32[]{:S(2)}, u32[]{:S(2)}) %collective-permute-start.77) | collective-permute-done | bytes 1048608 | tf_op jit(solution)/shard_map/ppermute | solution.py:835
  586.8 21.6 %collective-permute-done.81 = bf16[1024,512]{1,0:T(8,128)(2,1)S(1)} collective-permute-done((bf16[1024,512]{1,0:T(8,128)(2,1)S(1)}, bf16[1024,512]{1,0:T(8,128)(2,1)S(1)}, u32[]{:S(2)}, u32[]{:S(2)}) %collective-permute-start.81) | collective-permute-done | bytes 1048608 | tf_op jit(solution)/shard_map/ppermute | solution.py:835
  621.4 9.0 %collective-permute-start.65 = (bf16[1040,256]{1,0:T(8,128)(2,1)S(1)}, bf16[1040,256]{1,0:T(8,128)(2,1)S(1)}, u32[]{:S(2)}, u32[]{:S(2)}) collective-permute-start(bf16[1040,256]{1,0:T(8,128)(2,1)S(1)} %add_kernel.2), channel_id=1, source_target_pairs={{0,4},{12,8},{1,5},{13,9},{2,6},{14,10},{3,7},{15,11},{16,20},{28,... | collective-permute-start | bytes 1597448 | tf_op jit(solution)/shard_map/ppermute | solution.py:835
  630.6 7.9 %collective-permute-start.72 = (bf16[1040,256]{1,0:T(8,128)(2,1)S(1)}, bf16[1040,256]{1,0:T(8,128)(2,1)S(1)}, u32[]{:S(2)}, u32[]{:S(2)}) collective-permute-start(bf16[1040,256]{1,0:T(8,128)(2,1)S(1)} %add_kernel.3), channel_id=1, source_target_pairs={{0,4},{12,8},{1,5},{13,9},{2,6},{14,10},{3,7},{15,11},{16,20},{28,... | collective-permute-start | bytes 1597448 | tf_op jit(solution)/shard_map/ppermute | solution.py:835
  643.4 5.2 collective-permute-done.72
  654.3 8.6 %collective-permute-done.80 = bf16[2048,512]{1,0:T(8,128)(2,1)S(1)} collective-permute-done((bf16[2048,512]{1,0:T(8,128)(2,1)S(1)}, bf16[2048,512]{1,0:T(8,128)(2,1)S(1)}, u32[]{:S(2)}, u32[]{:S(2)}) %collective-permute-start.80) | collective-permute-done | bytes 2097184 | tf_op jit(solution)/shard_map/ppermute | solution.py:839
  663.1 22.2 %collective-permute-done.79 = bf16[1024,512]{1,0:T(8,128)(2,1)S(1)} collective-permute-done((bf16[1024,512]{1,0:T(8,128)(2,1)S(1)}, bf16[1024,512]{1,0:T(8,128)(2,1)S(1)}, u32[]{:S(2)}, u32[]{:S(2)}) %collective-permute-start.79) | collective-permute-done | bytes 1048608 | tf_op jit(solution)/shard_map/ppermute | solution.py:839
  685.3 22.5 %collective-permute-done.83 = bf16[1024,512]{1,0:T(8,128)(2,1)S(1)} collective-permute-done((bf16[1024,512]{1,0:T(8,128)(2,1)S(1)}, bf16[1024,512]{1,0:T(8,128)(2,1)S(1)}, u32[]{:S(2)}, u32[]{:S(2)}) %collective-permute-start.83) | collective-permute-done | bytes 1048608 | tf_op jit(solution)/shard_map/ppermute | solution.py:839
  708.8 10.5 %collective-permute-done.67 = bf16[1040,256]{1,0:T(8,128)(2,1)S(1)} collective-permute-done((bf16[1040,256]{1,0:T(8,128)(2,1)S(1)}, bf16[1040,256]{1,0:T(8,128)(2,1)S(1)}, u32[]{:S(2)}, u32[]{:S(2)}) %collective-permute-start.67) | collective-permute-done | bytes 532512 | tf_op jit(solution)/shard_map/ppermute | solution.py:839
  719.2 9.9 %collective-permute-done.74 = bf16[1040,256]{1,0:T(8,128)(2,1)S(1)} collective-permute-done((bf16[1040,256]{1,0:T(8,128)(2,1)S(1)}, bf16[1040,256]{1,0:T(8,128)(2,1)S(1)}, u32[]{:S(2)}, u32[]{:S(2)}) %collective-permute-start.74) | collective-permute-done | bytes 532512 | tf_op jit(solution)/shard_map/ppermute | solution.py:839
  732.7 4.5 unpack_feed.1
  (491 shorter events, 195.8 us)
Async XLA Ops:
  41.6 25.9 %collective-permute-start.16 = (bf16[256,1024]{1,0:T(8,128)(2,1)S(1)}, bf16[256,1024]{1,0:T(8,128)(2,1)S(1)}, u32[]{:S(2)}, u32[]{:S(2)}) collective-permute-start(bf16[256,1024]{1,0:T(8,128)(2,1)S(1)} %select_bitcast_fusion.3), channel_id=1, source_target_pairs={{0,8},{4,12},{8,0},{12,4},{1,9},{5,13},{9,1},{13,5},{2,10},{6,14},... | collective-permute-start | bytes 1572872 | tf_op jit(solution)/shard_map/ppermute | solution.py:792
  44.5 48.1 %collective-permute-start.17 = (bf16[1024,512]{1,0:T(8,128)(2,1)S(1)}, bf16[1024,512]{1,0:T(8,128)(2,1)S(1)}, u32[]{:S(2)}, u32[]{:S(2)}) collective-permute-start(bf16[1024,512]{1,0:T(8,128)(2,1)S(1)} %get-tuple-element.266.refs_10_.refs_6_), channel_id=1, source_target_pairs={{0,1},{1,0},{2,3},{3,2},{4,5},{5,4},{6,7},{7,6},{8,9},{9,8},{10,11... | collective-permute-start | bytes 3145736 | tf_op jit(solution)/shard_map/ppermute | solution.py:792
  46.2 47.0 %collective-permute-start.19 = (bf16[1024,512]{1,0:T(8,128)(2,1)S(1)}, bf16[1024,512]{1,0:T(8,128)(2,1)S(1)}, u32[]{:S(2)}, u32[]{:S(2)}) collective-permute-start(bf16[1024,512]{1,0:T(8,128)(2,1)S(1)} %get-tuple-element.264.refs_11_.refs_7_), channel_id=1, source_target_pairs={{0,2},{1,3},{2,0},{3,1},{4,6},{5,7},{6,4},{7,5},{8,10},{9,11},{10,... | collective-permute-start | bytes 3145736 | tf_op jit(solution)/shard_map/ppermute | solution.py:792
  46.8 35.3 %collective-permute-start.24 = (bf16[1040,256]{1,0:T(8,128)(2,1)S(1)}, bf16[1040,256]{1,0:T(8,128)(2,1)S(1)}, u32[]{:S(2)}, u32[]{:S(2)}) collective-permute-start(bf16[1040,256]{1,0:T(8,128)(2,1)S(1)} %collective-permute-done.6.refs_0_.refs_2_.refs_6_.refs_7_.refs_11_.refs_8_), channel_id=1, source_target_pairs={{0,2},{1,3},{2,0},{3,1},{4,6},{5,7},{6,4},{7,5},{8,10},{9,11},{10,... | collective-permute-start | bytes 1597448 | tf_op jit(solution)/shard_map/ppermute | solution.py:792
  48.3 34.3 %collective-permute-start.25 = (bf16[1040,256]{1,0:T(8,128)(2,1)S(1)}, bf16[1040,256]{1,0:T(8,128)(2,1)S(1)}, u32[]{:S(2)}, u32[]{:S(2)}) collective-permute-start(bf16[1040,256]{1,0:T(8,128)(2,1)S(1)} %collective-permute-done.7.refs_1_.refs_9_.refs_10_.refs_14_.refs_11_), channel_id=1, source_target_pairs={{0,1},{1,0},{2,3},{3,2},{4,5},{5,4},{6,7},{7,6},{8,9},{9,8},{10,11... | collective-permute-start | bytes 1597448 | tf_op jit(solution)/shard_map/ppermute | solution.py:792
  82.1 28.1 %collective-permute-start.21 = (bf16[1024,512]{1,0:T(8,128)(2,1)S(1)}, bf16[1024,512]{1,0:T(8,128)(2,1)S(1)}, u32[]{:S(2)}, u32[]{:S(2)}) collective-permute-start(bf16[1024,512]{1,0:T(8,128)(2,1)S(1)} %get-tuple-element.266.refs_10_.refs_6_), channel_id=1, source_target_pairs={{0,2},{1,3},{2,0},{3,1},{4,6},{5,7},{6,4},{7,5},{8,10},{9,11},{10,... | collective-permute-start | bytes 3145736 | tf_op jit(solution)/shard_map/ppermute | solution.py:792
  82.6 27.6 %collective-permute-start.22 = (bf16[1024,512]{1,0:T(8,128)(2,1)S(1)}, bf16[1024,512]{1,0:T(8,128)(2,1)S(1)}, u32[]{:S(2)}, u32[]{:S(2)}) collective-permute-start(bf16[1024,512]{1,0:T(8,128)(2,1)S(1)} %get-tuple-element.264.refs_11_.refs_7_), channel_id=1, source_target_pairs={{0,1},{1,0},{2,3},{3,2},{4,5},{5,4},{6,7},{7,6},{8,9},{9,8},{10,11... | collective-permute-start | bytes 3145736 | tf_op jit(solution)/shard_map/ppermute | solution.py:792
  92.6 37.8 %collective-permute-start.18 = (bf16[1024,512]{1,0:T(8,128)(2,1)S(1)}, bf16[1024,512]{1,0:T(8,128)(2,1)S(1)}, u32[]{:S(2)}, u32[]{:S(2)}) collective-permute-start(bf16[1024,512]{1,0:T(8,128)(2,1)S(1)} %collective-permute-done.17.refs_0_.refs_12_.refs_8_), channel_id=1, source_target_pairs={{0,2},{1,3},{2,0},{3,1},{4,6},{5,7},{6,4},{7,5},{8,10},{9,11},{10,... | collective-permute-start | bytes 3145736 | tf_op jit(solution)/shard_map/ppermute | solution.py:792
  93.2 37.2 %collective-permute-start.20 = (bf16[1024,512]{1,0:T(8,128)(2,1)S(1)}, bf16[1024,512]{1,0:T(8,128)(2,1)S(1)}, u32[]{:S(2)}, u32[]{:S(2)}) collective-permute-start(bf16[1024,512]{1,0:T(8,128)(2,1)S(1)} %collective-permute-done.19.refs_1_.refs_15_.refs_11_), channel_id=1, source_target_pairs={{0,1},{1,0},{2,3},{3,2},{4,5},{5,4},{6,7},{7,6},{8,9},{9,8},{10,11... | collective-permute-start | bytes 3145736 | tf_op jit(solution)/shard_map/ppermute | solution.py:792
  134.3 27.0 %collective-permute-start.28 = (bf16[512,1024]{1,0:T(8,128)(2,1)S(1)}, bf16[512,1024]{1,0:T(8,128)(2,1)S(1)}, u32[]{:S(2)}, u32[]{:S(2)}) collective-permute-start(bf16[512,1024]{1,0:T(8,128)(2,1)S(1)} %get-tuple-element.141), channel_id=1, source_target_pairs={{0,16},{16,0},{1,17},{17,1},{2,18},{18,2},{3,19},{19,3},{4,20},{20... | collective-permute-start | bytes 3145736 | tf_op jit(solution)/shard_map/ppermute | solution.py:792
  136.3 25.0 %collective-permute-start.15 = (bf16[1040,256]{1,0:T(8,128)(2,1)S(1)}, bf16[1040,256]{1,0:T(8,128)(2,1)S(1)}, u32[]{:S(2)}, u32[]{:S(2)}) collective-permute-start(bf16[1040,256]{1,0:T(8,128)(2,1)S(1)} %get-tuple-element.281.refs_5_.refs_6_.refs_8_), channel_id=1, source_target_pairs={{0,1},{1,0},{2,3},{3,2},{4,5},{5,4},{6,7},{7,6},{8,9},{9,8},{10,11... | collective-permute-start | bytes 1597448 | tf_op jit(solution)/shard_map/ppermute | solution.py:792
  149.2 50.2 %collective-permute-start.11 = (bf16[1024,512]{1,0:T(8,128)(2,1)S(1)}, bf16[1024,512]{1,0:T(8,128)(2,1)S(1)}, u32[]{:S(2)}, u32[]{:S(2)}) collective-permute-start(bf16[1024,512]{1,0:T(8,128)(2,1)S(1)} %get-tuple-element.267.refs_6_.refs_4_), channel_id=1, source_target_pairs={{0,1},{1,0},{2,3},{3,2},{4,5},{5,4},{6,7},{7,6},{8,9},{9,8},{10,11... | collective-permute-start | bytes 3145736 | tf_op jit(solution)/shard_map/ppermute | solution.py:792
  150.7 48.7 %collective-permute-start.13 = (bf16[1024,512]{1,0:T(8,128)(2,1)S(1)}, bf16[1024,512]{1,0:T(8,128)(2,1)S(1)}, u32[]{:S(2)}, u32[]{:S(2)}) collective-permute-start(bf16[1024,512]{1,0:T(8,128)(2,1)S(1)} %get-tuple-element.265.refs_7_.refs_5_), channel_id=1, source_target_pairs={{0,2},{1,3},{2,0},{3,1},{4,6},{5,7},{6,4},{7,5},{8,10},{9,11},{10,... | collective-permute-start | bytes 3145736 | tf_op jit(solution)/shard_map/ppermute | solution.py:792
  195.9 26.1 %collective-permute-start.32 = (bf16[1024,512]{1,0:T(8,128)(2,1)S(1)}, bf16[1024,512]{1,0:T(8,128)(2,1)S(1)}, u32[]{:S(2)}, u32[]{:S(2)}) collective-permute-start(bf16[1024,512]{1,0:T(8,128)(2,1)S(1)} %get-tuple-element.267.refs_6_.refs_4_), channel_id=1, source_target_pairs={{0,2},{1,3},{2,0},{3,1},{4,6},{5,7},{6,4},{7,5},{8,10},{9,11},{10,... | collective-permute-start | bytes 3145736 | tf_op jit(solution)/shard_map/ppermute | solution.py:792
  197.3 26.1 %collective-permute-start.33 = (bf16[1024,512]{1,0:T(8,128)(2,1)S(1)}, bf16[1024,512]{1,0:T(8,128)(2,1)S(1)}, u32[]{:S(2)}, u32[]{:S(2)}) collective-permute-start(bf16[1024,512]{1,0:T(8,128)(2,1)S(1)} %get-tuple-element.265.refs_7_.refs_5_), channel_id=1, source_target_pairs={{0,1},{1,0},{2,3},{3,2},{4,5},{5,4},{6,7},{7,6},{8,9},{9,8},{10,11... | collective-permute-start | bytes 3145736 | tf_op jit(solution)/shard_map/ppermute | solution.py:792
  207.3 35.8 %collective-permute-start.30 = (bf16[1024,512]{1,0:T(8,128)(2,1)S(1)}, bf16[1024,512]{1,0:T(8,128)(2,1)S(1)}, u32[]{:S(2)}, u32[]{:S(2)}) collective-permute-start(bf16[1024,512]{1,0:T(8,128)(2,1)S(1)} %collective-permute-done.11.refs_2_.refs_0_.refs_8_.refs_6_), channel_id=1, source_target_pairs={{0,2},{1,3},{2,0},{3,1},{4,6},{5,7},{6,4},{7,5},{8,10},{9,11},{10,... | collective-permute-start | bytes 3145736 | tf_op jit(solution)/shard_map/ppermute | solution.py:792
  208.6 35.6 %collective-permute-start.31 = (bf16[1024,512]{1,0:T(8,128)(2,1)S(1)}, bf16[1024,512]{1,0:T(8,128)(2,1)S(1)}, u32[]{:S(2)}, u32[]{:S(2)}) collective-permute-start(bf16[1024,512]{1,0:T(8,128)(2,1)S(1)} %collective-permute-done.13.refs_3_.refs_1_.refs_11_.refs_9_), channel_id=1, source_target_pairs={{0,1},{1,0},{2,3},{3,2},{4,5},{5,4},{6,7},{7,6},{8,9},{9,8},{10,11... | collective-permute-start | bytes 3145736 | tf_op jit(solution)/shard_map/ppermute | solution.py:792
  296.5 64.1 %collective-permute-start.39 = (bf16[2048,512]{1,0:T(8,128)(2,1)}, bf16[2048,512]{1,0:T(8,128)(2,1)S(1)}, u32[]{:S(2)}, u32[]{:S(2)}) collective-permute-start(bf16[2048,512]{1,0:T(8,128)(2,1)} %get-tuple-element.164), channel_id=1, source_target_pairs={{0,1},{1,0},{2,3},{3,2},{4,5},{5,4},{6,7},{7,6},{8,9},{9,8},{10,11... | collective-permute-start | bytes 6291464 | tf_op jit(solution)/shard_map/ppermute | solution.py:792
  297.0 63.6 %collective-permute-start.41 = (bf16[2048,512]{1,0:T(8,128)(2,1)}, bf16[2048,512]{1,0:T(8,128)(2,1)S(1)}, u32[]{:S(2)}, u32[]{:S(2)}) collective-permute-start(bf16[2048,512]{1,0:T(8,128)(2,1)} %get-tuple-element.167), channel_id=1, source_target_pairs={{0,2},{1,3},{2,0},{3,1},{4,6},{5,7},{6,4},{7,5},{8,10},{9,11},{10,... | collective-permute-start | bytes 6291464 | tf_op jit(solution)/shard_map/ppermute | solution.py:792
  298.3 26.4 %collective-permute-start.38 = (bf16[256,1024]{1,0:T(8,128)(2,1)S(1)}, bf16[256,1024]{1,0:T(8,128)(2,1)S(1)}, u32[]{:S(2)}, u32[]{:S(2)}) collective-permute-start(bf16[256,1024]{1,0:T(8,128)(2,1)S(1)} %broadcast_select_fusion.26), channel_id=1, source_target_pairs={{0,8},{4,12},{8,0},{12,4},{1,9},{5,13},{9,1},{13,5},{2,10},{6,14},... | collective-permute-start | bytes 1572872 | tf_op jit(solution)/shard_map/ppermute | solution.py:792
  366.9 25.5 %collective-permute-start.40 = (bf16[1024,512]{1,0:T(8,128)(2,1)}, bf16[1024,512]{1,0:T(8,128)(2,1)}, u32[]{:S(2)}, u32[]{:S(2)}) collective-permute-start(bf16[1024,512]{1,0:T(8,128)(2,1)} %add_convert_fusion.18), channel_id=1, source_target_pairs={{0,2},{1,3},{2,0},{3,1},{4,6},{5,7},{6,4},{7,5},{8,10},{9,11},{10,... | collective-permute-start | bytes 3145736 | tf_op jit(solution)/shard_map/ppermute | solution.py:792
  369.4 26.4 %collective-permute-start.42 = (bf16[1024,512]{1,0:T(8,128)(2,1)}, bf16[1024,512]{1,0:T(8,128)(2,1)}, u32[]{:S(2)}, u32[]{:S(2)}) collective-permute-start(bf16[1024,512]{1,0:T(8,128)(2,1)} %add_convert_fusion.15), channel_id=1, source_target_pairs={{0,1},{1,0},{2,3},{3,2},{4,5},{5,4},{6,7},{7,6},{8,9},{9,8},{10,11... | collective-permute-start | bytes 3145736 | tf_op jit(solution)/shard_map/ppermute | solution.py:792
  388.5 28.8 %collective-permute-start.50 = (bf16[2080,256]{1,0:T(8,128)(2,1)}, bf16[2080,256]{1,0:T(8,128)(2,1)S(1)}, u32[]{:S(2)}, u32[]{:S(2)}) collective-permute-start(bf16[2080,256]{1,0:T(8,128)(2,1)} %get-tuple-element.196), channel_id=1, source_target_pairs={{0,1},{1,0},{2,3},{3,2},{4,5},{5,4},{6,7},{7,6},{8,9},{9,8},{10,11... | collective-permute-start | bytes 3194888 | tf_op jit(solution)/shard_map/ppermute | solution.py:792
  406.4 33.2 %collective-permute-start.54 = (bf16[512,1024]{1,0:T(8,128)(2,1)}, bf16[512,1024]{1,0:T(8,128)(2,1)S(1)}, u32[]{:S(2)}, u32[]{:S(2)}) collective-permute-start(bf16[512,1024]{1,0:T(8,128)(2,1)} %get-tuple-element.200), channel_id=1, source_target_pairs={{0,16},{16,0},{1,17},{17,1},{2,18},{18,2},{3,19},{19,3},{4,20},{20... | collective-permute-start | bytes 3145736 | tf_op jit(solution)/shard_map/ppermute | solution.py:792
  406.4 26.5 %collective-permute-start.52 = (bf16[2080,256]{1,0:T(8,128)(2,1)}, bf16[2080,256]{1,0:T(8,128)(2,1)S(1)}, u32[]{:S(2)}, u32[]{:S(2)}) collective-permute-start(bf16[2080,256]{1,0:T(8,128)(2,1)} %copy-done.86), channel_id=1, source_target_pairs={{0,2},{1,3},{2,0},{3,1},{4,6},{5,7},{6,4},{7,5},{8,10},{9,11},{10,... | collective-permute-start | bytes 3194888 | tf_op jit(solution)/shard_map/ppermute | solution.py:792
  417.6 72.3 %collective-permute-start.51 = (bf16[1040,256]{1,0:T(8,128)(2,1)S(1)}, bf16[1040,256]{1,0:T(8,128)(2,1)S(1)}, u32[]{:S(2)}, u32[]{:S(2)}) collective-permute-start(bf16[1040,256]{1,0:T(8,128)(2,1)S(1)} %add_convert_fusion.33), channel_id=1, source_target_pairs={{0,2},{1,3},{2,0},{3,1},{4,6},{5,7},{6,4},{7,5},{8,10},{9,11},{10,... | collective-permute-start | bytes 1597448 | tf_op jit(solution)/shard_map/ppermute | solution.py:792
  433.1 56.8 %collective-permute-start.53 = (bf16[1040,256]{1,0:T(8,128)(2,1)S(1)}, bf16[1040,256]{1,0:T(8,128)(2,1)}, u32[]{:S(2)}, u32[]{:S(2)}) collective-permute-start(bf16[1040,256]{1,0:T(8,128)(2,1)S(1)} %add_convert_fusion.32), channel_id=1, source_target_pairs={{0,1},{1,0},{2,3},{3,2},{4,5},{5,4},{6,7},{7,6},{8,9},{9,8},{10,11... | collective-permute-start | bytes 1597448 | tf_op jit(solution)/shard_map/ppermute | solution.py:792
  436.1 77.6 %collective-permute-start.43 = (bf16[2048,512]{1,0:T(8,128)(2,1)}, bf16[2048,512]{1,0:T(8,128)(2,1)S(1)}, u32[]{:S(2)}, u32[]{:S(2)}) collective-permute-start(bf16[2048,512]{1,0:T(8,128)(2,1)} %pad_maximum_fusion), channel_id=1, source_target_pairs={{0,4},{12,8},{1,5},{13,9},{2,6},{14,10},{3,7},{15,11},{16,20},{28,... | collective-permute-start | bytes 6291464 | tf_op jit(solution)/shard_map/ppermute | solution.py:835
  444.7 44.7 %collective-permute-start.55 = (bf16[512,256]{1,0:T(8,128)(2,1)S(1)}, bf16[512,256]{1,0:T(8,128)(2,1)S(1)}, u32[]{:S(2)}, u32[]{:S(2)}) collective-permute-start(bf16[512,256]{1,0:T(8,128)(2,1)S(1)} %get-tuple-element.203), channel_id=1, source_target_pairs={{0,4},{4,0},{8,12},{12,8},{1,5},{5,1},{9,13},{13,9},{2,6},{6,2},{1... | collective-permute-start | bytes 786440 | tf_op jit(solution)/shard_map/ppermute | solution.py:792
  455.7 59.5 %collective-permute-start.48 = (bf16[2048,512]{1,0:T(8,128)(2,1)S(1)}, bf16[2048,512]{1,0:T(8,128)(2,1)S(1)}, u32[]{:S(2)}, u32[]{:S(2)}) collective-permute-start(bf16[2048,512]{1,0:T(8,128)(2,1)S(1)} %get-tuple-element.186), channel_id=1, source_target_pairs={{0,1},{1,0},{2,3},{3,2},{4,5},{5,4},{6,7},{7,6},{8,9},{9,8},{10,11... | collective-permute-start | bytes 6291464 | tf_op jit(solution)/shard_map/ppermute | solution.py:792
  489.4 48.6 %collective-permute-start.49 = (bf16[2048,512]{1,0:T(8,128)(2,1)S(1)}, bf16[2048,512]{1,0:T(8,128)(2,1)S(1)}, u32[]{:S(2)}, u32[]{:S(2)}) collective-permute-start(bf16[2048,512]{1,0:T(8,128)(2,1)S(1)} %copy-done.81), channel_id=1, source_target_pairs={{0,2},{1,3},{2,0},{3,1},{4,6},{5,7},{6,4},{7,5},{8,10},{9,11},{10,... | collective-permute-start | bytes 6291464 | tf_op jit(solution)/shard_map/ppermute | solution.py:792
  506.6 32.4 %collective-permute-start.56 = (bf16[512,768]{1,0:T(8,128)(2,1)S(1)}, bf16[512,768]{1,0:T(8,128)(2,1)S(1)}, u32[]{:S(2)}, u32[]{:S(2)}) collective-permute-start(bf16[512,768]{1,0:T(8,128)(2,1)S(1)} %get-tuple-element.206), channel_id=1, source_target_pairs={{0,4},{4,0},{8,12},{12,8},{1,5},{5,1},{9,13},{13,9},{2,6},{6,2},{1... | collective-permute-start | bytes 2359304 | tf_op jit(solution)/shard_map/ppermute | solution.py:792
  511.0 35.8 %collective-permute-start.60 = (bf16[2080,256]{1,0:T(8,128)(2,1)S(1)}, bf16[2080,256]{1,0:T(8,128)(2,1)S(1)}, u32[]{:S(2)}, u32[]{:S(2)}) collective-permute-start(bf16[2080,256]{1,0:T(8,128)(2,1)S(1)} %pad_maximum_fusion.1), channel_id=1, source_target_pairs={{0,4},{12,8},{1,5},{13,9},{2,6},{14,10},{3,7},{15,11},{16,20},{28,... | collective-permute-start | bytes 3194888 | tf_op jit(solution)/shard_map/ppermute | solution.py:835
  514.4 56.9 %collective-permute-start.59 = (bf16[2048,512]{1,0:T(8,128)(2,1)S(1)}, bf16[2048,512]{1,0:T(8,128)(2,1)S(1)}, u32[]{:S(2)}, u32[]{:S(2)}) collective-permute-start(bf16[2048,512]{1,0:T(8,128)(2,1)S(1)} %add_convert_fusion.1), channel_id=1, source_target_pairs={{4,8},{8,4},{5,9},{9,5},{6,10},{10,6},{7,11},{11,7},{20,24},{24,20... | collective-permute-start | bytes 6291464 | tf_op jit(solution)/shard_map/ppermute | solution.py:837
  515.5 42.0 %collective-permute-start.61 = (bf16[1024,512]{1,0:T(8,128)(2,1)S(1)}, bf16[1024,512]{1,0:T(8,128)(2,1)S(1)}, u32[]{:S(2)}, u32[]{:S(2)}) collective-permute-start(bf16[1024,512]{1,0:T(8,128)(2,1)S(1)} %add_convert_fusion.13), channel_id=1, source_target_pairs={{0,2},{1,3},{2,0},{3,1},{4,6},{5,7},{6,4},{7,5},{8,10},{9,11},{10,... | collective-permute-start | bytes 3145736 | tf_op jit(solution)/shard_map/ppermute | solution.py:792
  558.0 28.0 %collective-permute-start.77 = (bf16[1024,512]{1,0:T(8,128)(2,1)S(1)}, bf16[1024,512]{1,0:T(8,128)(2,1)S(1)}, u32[]{:S(2)}, u32[]{:S(2)}) collective-permute-start(bf16[1024,512]{1,0:T(8,128)(2,1)S(1)} %add_convert_fusion.10), channel_id=1, source_target_pairs={{0,4},{12,8},{1,5},{13,9},{2,6},{14,10},{3,7},{15,11},{16,20},{28,... | collective-permute-start | bytes 3145736 | tf_op jit(solution)/shard_map/ppermute | solution.py:835
  563.2 45.3 %collective-permute-start.81 = (bf16[1024,512]{1,0:T(8,128)(2,1)S(1)}, bf16[1024,512]{1,0:T(8,128)(2,1)S(1)}, u32[]{:S(2)}, u32[]{:S(2)}) collective-permute-start(bf16[1024,512]{1,0:T(8,128)(2,1)S(1)} %add_convert_fusion.6), channel_id=1, source_target_pairs={{0,4},{12,8},{1,5},{13,9},{2,6},{14,10},{3,7},{15,11},{16,20},{28,... | collective-permute-start | bytes 3145736 | tf_op jit(solution)/shard_map/ppermute | solution.py:835
  568.6 47.3 %collective-permute-start.58 = (bf16[256,1024]{1,0:T(8,128)(2,1)S(1)}, bf16[256,1024]{1,0:T(8,128)(2,1)S(1)}, u32[]{:S(2)}, u32[]{:S(2)}) collective-permute-start(bf16[256,1024]{1,0:T(8,128)(2,1)S(1)} %select_convert_fusion), channel_id=1, source_target_pairs={{0,8},{4,12},{8,0},{12,4},{1,9},{5,13},{9,1},{13,5},{2,10},{6,14},... | collective-permute-start | bytes 1572872 | tf_op jit(solution)/shard_map/ppermute | solution.py:792
  569.9 51.5 %collective-permute-start.69 = (bf16[2080,256]{1,0:T(8,128)(2,1)S(1)}, bf16[2080,256]{1,0:T(8,128)(2,1)S(1)}, u32[]{:S(2)}, u32[]{:S(2)}) collective-permute-start(bf16[2080,256]{1,0:T(8,128)(2,1)S(1)} %add_convert_fusion.2), channel_id=1, source_target_pairs={{4,0},{8,12},{5,1},{9,13},{6,2},{10,14},{7,3},{11,15},{20,16},{24,... | collective-permute-start | bytes 3194888 | tf_op jit(solution)/shard_map/ppermute | solution.py:839
  576.7 33.3 %collective-permute-start.63 = (bf16[2080,256]{1,0:T(8,128)(2,1)S(1)}, bf16[2080,256]{1,0:T(8,128)(2,1)S(1)}, u32[]{:S(2)}, u32[]{:S(2)}) collective-permute-start(bf16[2080,256]{1,0:T(8,128)(2,1)S(1)} %get-tuple-element.224), channel_id=1, source_target_pairs={{0,1},{1,0},{2,3},{3,2},{4,5},{5,4},{6,7},{7,6},{8,9},{9,8},{10,11... | collective-permute-start | bytes 3194888 | tf_op jit(solution)/shard_map/ppermute | solution.py:792
  586.0 25.2 %collective-permute-start.70 = (bf16[2080,256]{1,0:T(8,128)(2,1)S(1)}, bf16[2080,256]{1,0:T(8,128)(2,1)S(1)}, u32[]{:S(2)}, u32[]{:S(2)}) collective-permute-start(bf16[2080,256]{1,0:T(8,128)(2,1)S(1)} %get-tuple-element.227), channel_id=1, source_target_pairs={{0,2},{1,3},{2,0},{3,1},{4,6},{5,7},{6,4},{7,5},{8,10},{9,11},{10,... | collective-permute-start | bytes 3194888 | tf_op jit(solution)/shard_map/ppermute | solution.py:792
  608.4 54.4 %collective-permute-start.80 = (bf16[2048,512]{1,0:T(8,128)(2,1)S(1)}, bf16[2048,512]{1,0:T(8,128)(2,1)S(1)}, u32[]{:S(2)}, u32[]{:S(2)}) collective-permute-start(bf16[2048,512]{1,0:T(8,128)(2,1)S(1)} %add_convert_fusion), channel_id=1, source_target_pairs={{4,0},{8,12},{5,1},{9,13},{6,2},{10,14},{7,3},{11,15},{20,16},{24,... | collective-permute-start | bytes 6291464 | tf_op jit(solution)/shard_map/ppermute | solution.py:839
  610.1 28.5 %collective-permute-start.78 = (bf16[1024,512]{1,0:T(8,128)(2,1)S(1)}, bf16[1024,512]{1,0:T(8,128)(2,1)S(1)}, u32[]{:S(2)}, u32[]{:S(2)}) collective-permute-start(bf16[1024,512]{1,0:T(8,128)(2,1)S(1)} %add_convert_fusion.9), channel_id=1, source_target_pairs={{4,8},{8,4},{5,9},{9,5},{6,10},{10,6},{7,11},{11,7},{20,24},{24,20... | collective-permute-start | bytes 3145736 | tf_op jit(solution)/shard_map/ppermute | solution.py:837
  615.9 33.5 %collective-permute-start.82 = (bf16[1024,512]{1,0:T(8,128)(2,1)S(1)}, bf16[1024,512]{1,0:T(8,128)(2,1)S(1)}, u32[]{:S(2)}, u32[]{:S(2)}) collective-permute-start(bf16[1024,512]{1,0:T(8,128)(2,1)S(1)} %add_convert_fusion.5), channel_id=1, source_target_pairs={{4,8},{8,4},{5,9},{9,5},{6,10},{10,6},{7,11},{11,7},{20,24},{24,20... | collective-permute-start | bytes 3145736 | tf_op jit(solution)/shard_map/ppermute | solution.py:837
  638.9 46.4 %collective-permute-start.79 = (bf16[1024,512]{1,0:T(8,128)(2,1)S(1)}, bf16[1024,512]{1,0:T(8,128)(2,1)S(1)}, u32[]{:S(2)}, u32[]{:S(2)}) collective-permute-start(bf16[1024,512]{1,0:T(8,128)(2,1)S(1)} %add_convert_fusion.8), channel_id=1, source_target_pairs={{4,0},{8,12},{5,1},{9,13},{6,2},{10,14},{7,3},{11,15},{20,16},{24,... | collective-permute-start | bytes 3145736 | tf_op jit(solution)/shard_map/ppermute | solution.py:839
  649.7 58.1 %collective-permute-start.83 = (bf16[1024,512]{1,0:T(8,128)(2,1)S(1)}, bf16[1024,512]{1,0:T(8,128)(2,1)S(1)}, u32[]{:S(2)}, u32[]{:S(2)}) collective-permute-start(bf16[1024,512]{1,0:T(8,128)(2,1)S(1)} %add_convert_fusion.4), channel_id=1, source_target_pairs={{4,0},{8,12},{5,1},{9,13},{6,2},{10,14},{7,3},{11,15},{20,16},{24,... | collective-permute-start | bytes 3145736 | tf_op jit(solution)/shard_map/ppermute | solution.py:839
  651.2 68.0 %collective-permute-start.67 = (bf16[1040,256]{1,0:T(8,128)(2,1)S(1)}, bf16[1040,256]{1,0:T(8,128)(2,1)S(1)}, u32[]{:S(2)}, u32[]{:S(2)}) collective-permute-start(bf16[1040,256]{1,0:T(8,128)(2,1)S(1)} %add_convert_fusion.24), channel_id=1, source_target_pairs={{4,0},{8,12},{5,1},{9,13},{6,2},{10,14},{7,3},{11,15},{20,16},{24,... | collective-permute-start | bytes 1597448 | tf_op jit(solution)/shard_map/ppermute | solution.py:839
  652.7 76.5 %collective-permute-start.74 = (bf16[1040,256]{1,0:T(8,128)(2,1)S(1)}, bf16[1040,256]{1,0:T(8,128)(2,1)S(1)}, u32[]{:S(2)}, u32[]{:S(2)}) collective-permute-start(bf16[1040,256]{1,0:T(8,128)(2,1)S(1)} %add_convert_fusion.20), channel_id=1, source_target_pairs={{4,0},{8,12},{5,1},{9,13},{6,2},{10,14},{7,3},{11,15},{20,16},{24,... | collective-permute-start | bytes 1597448 | tf_op jit(solution)/shard_map/ppermute | solution.py:839
  (173 other events, 2874.3 us)

commit v3 on v2

--- a/solution.py
+++ b/solution.py
@@ -55,7 +55,7 @@
         out_specs=[pl.BlockSpec(memory_space=spaces[k]) for _, _, k in outs],
         scratch_shapes=scratch,
         compiler_params=pltpu.CompilerParams(vmem_limit_bytes=min(held + 14 * MIB, 58 * MIB)),
-        cost_estimate=pl.CostEstimate(flops=flops, bytes_accessed=moved, transcendentals=exps),
+        cost_estimate=pl.CostEstimate(flops=flops // 16, bytes_accessed=moved // 16, transcendentals=0),
     )(*[a for a, _ in ins])
 
 
@@ -688,8 +688,9 @@
 
     extra, half = 16, rows // 2
 
-    def body(scal, normed, triple, mixed, branch_grad, in_sum, out_sum, feed_sum, up_sum, *rest):
-        refs, (full, out, vectors, low, bias, sems) = rest[:-6], rest[-6:]
+    def body(scal, normed, triple, mixed, branch_grad, *rest):
+        *in_sums, out_sum, feed_sum, up_sum = rest[: len(sums)]
+        refs, (full, out, vectors, low, bias, sems) = rest[len(sums) : -6], rest[-6:]
         pieces = group_views(refs, 4 * rows + extra, count)
         out[...] = dot_tn(mixed[...], branch_grad[...]).astype(BF16)
         pairs = [(b, a) for a, b in out_pairs(scal, pieces, out, rows, count)]
@@ -704,7 +705,9 @@
         pairs = [(b, a) for a, b in mix_pairs(scal, pieces, full, rows, count)]
         copies += start_all(pairs, sems, 4 * count)
         vectors[...] = jnp.zeros_like(vectors)
-        vectors[0:2, :] = in_sum[0:2, :]
+        for i, in_sum in enumerate(in_sums):
+            at = 11 if i == 0 else 0
+            vectors[at : at + 2, :] = in_sum[0:2, :]
         vectors[2:6, :] = out_sum[0:4, :]
         vectors[6:8, :] = feed_sum[0:2, :]
         for j in range(2):
@@ -760,7 +763,7 @@
     )[0]
 
 
-def input_backward(hidden, own, other, residual_grad, vectors):
+def input_backward(hidden, own, other, residual_grad, vectors, deps):
     tokens, width = hidden.shape
 
     def body(hidden, own, other, residual_grad, vectors, input_grad, low_grad, sums):
@@ -784,6 +787,7 @@
         [((tokens, width), F32, "v"), ((tokens, width), BF16, "v"), ((8, width), F32, "v")],
         [],
         20 * tokens * width,
+        deps=deps,
     )
 
 
@@ -821,8 +825,8 @@
             stages[hop].append(far)
             at = 0
             for i, value in enumerate(held):
-                if deps and hop == len(bits) - 1:
-                    held[i] = add_kernel(value, far, deps)
+                if deps and hop < len(deps) and i == len(held) - 1:
+                    held[i] = add_kernel(value, far[at : at + value.shape[0]], deps[hop])
                 else:
                     held[i] = add_low(value, far[at : at + value.shape[0]])
                 at += value.shape[0]
@@ -830,23 +834,17 @@
     return results, stages
 
 
-def sum_line(value):
-    place = lax.axis_index("seq")
-    inward = lax.ppermute(value, "seq", [(0, 1), (3, 2)])
-    near = add_low(value, inward)
-    across = lax.ppermute(near, "seq", [(1, 2), (2, 1)])
-    both = add_low(near, across)
-    back = lax.ppermute(both, "seq", [(1, 0), (2, 3)])
-    return jnp.where((place == 1) | (place == 2), both, back), (inward, across, back)
-
-
-def sum_shares(shares, layer):
-    if layer == 0:
-        lines = [sum_line(v) for v in shares]
-        return [v for v, _ in lines], [moved for _, moved in lines]
-    total, moved = sum_line(jnp.concatenate(shares, axis=0))
-    size = shares[0].shape[0]
-    return [total[:size], total[size:]], [moved]
+def sum_line(shares, parts=1):
+    even = lax.axis_index("seq") % 2 == 0
+    low, high = shares
+    near = swap(pick(even, high, low), "seq", 1)
+    value = add_low(pick(even, low, high), near)
+    size = value.shape[0] // parts
+    cut = [value[i * size : (i + 1) * size] for i in range(parts)]
+    across = [swap(v, "seq", 2) for v in cut]
+    value = jnp.concatenate([add_low(v, far) for v, far in zip(cut, across)], axis=0)
+    back = swap(value, "seq", 1)
+    return [pick(even, value, back), pick(even, back, value)], (near, across, back)
 
 
 def pick(flag, first, second):
@@ -928,6 +926,23 @@
         8 * rows * inner,
         deps=deps,
     )
+
+
+def sort_layers(keep, far, scal, deps):
+    def body(scal, keep0, keep1, far0, far1, *made):
+        for h, (mine, other) in enumerate(((keep0, far0), (keep1, far1))):
+            made[h][...], made[2 + h][...] = side_pick(scal[3], mine[...], other[...])
+
+    made = run_kernel(
+        body,
+        "sort_layers",
+        [(scal, "s")] + [(v, "v") for v in keep + far],
+        [(v.shape, BF16, "v") for v in keep + far],
+        [],
+        4 * keep[0].size,
+        deps=deps,
+    )
+    return [made[:2], made[2:]]
 
 
 def take_vectors(params, pieces, scal):
@@ -1089,13 +1104,20 @@
     length = pick(low_micro, lengths[0, 0], lengths[1, 0])
     scal = jnp.stack([block, parity, length, core]).astype(jnp.int32)
 
-    def spread(packs):
-        layers = [[], []]
-        for h in range(2):
-            keep, far = packs[h], swap(packs[2 + h], "section", 1)
-            layers[0].append(pick(first, keep, far))
-            layers[1].append(pick(first, far, keep))
-        return layers
+    def spread(packs, deps):
+        far = [swap(v, "section", 1) for v in packs[2:]]
+        return sort_layers(list(packs[:2]), far, scal, deps)
+
+    tokens = activations.shape[2]
+
+    def to_pair(value):
+        keep = pick(low_micro, value[0, 0], value[1, 0])
+        far = swap(pick(low_micro, value[1, 0], value[0, 0]), "seq", 2)
+        made = jnp.concatenate([pick(low_micro, keep, far), pick(low_micro, far, keep)], axis=0)
+        return made, far
+
+    hidden, arrived = to_pair(activations)
+    incoming, _ = to_pair(cotangent)
 
     vectors = jnp.stack(
         [mixgain[0], mixshift[0], mixbias[0, 0], mixbias[0, 1], outbias[0], mixscale[0]]
@@ -1106,50 +1128,49 @@
     )
     if rows < GROUP:
         vectors = jnp.concatenate([vectors, jnp.zeros((16, GROUP - rows), BF16)], axis=1)
-    mix_halves = spread(pack_mix(params, join(mixweight[0]), join(outweight[0]), vectors, scal))
-    mix_parts = [gather_blocks(halves, bits) for halves in mix_halves]
+    packs = pack_mix(params, join(mixweight[0]), join(outweight[0]), vectors, scal)
+    mix_parts = [gather_blocks(halves, bits) for halves in spread(packs, [])]
     mix_pieces, mix_stages = zip(*mix_parts)
-    ready = mix_stages[0][0] + mix_stages[0][1]
-    feed_halves = spread(
-        pack_feed(params, join(upweight[0]), join(downweight[0]), scal, ready)
-    )
-    feed_parts = [gather_blocks(halves, bits) for halves in feed_halves]
+    packs = pack_feed(params, join(upweight[0]), join(downweight[0]), scal, [])
+    ready = sum(mix_stages[0], []) + [arrived]
+    feed_parts = [gather_blocks(halves, bits) for halves in spread(packs, ready)]
     feed_pieces, feed_stages = zip(*feed_parts)
 
-    tokens = activations.shape[2]
-
-    def to_pair(value):
-        keep = pick(low_micro, value[0, 0], value[1, 0])
-        far = swap(pick(low_micro, value[1, 0], value[0, 0]), "seq", 2)
-        return jnp.concatenate([pick(low_micro, keep, far), pick(low_micro, far, keep)], axis=0)
-
-    def from_pair(value):
-        low, high = value[:tokens], value[tokens:]
-        far = swap(pick(low_micro, high, low).astype(BF16), "seq", 2)
-        wide = far.astype(value.dtype)
-        keep = pick(low_micro, low, high)
-        made = jnp.stack([pick(low_micro, keep, wide), pick(low_micro, wide, keep)])
-        return made[None, :, None], far
-
-    hidden = to_pair(activations)
-    incoming = to_pair(cotangent)
+    def send_rows(value):
+        return pick(low_micro, value[tokens:], value[:tokens]).astype(BF16)
+
+    def send_layer(sent, layer):
+        count = lax.axis_size("seq")
+        moves = [(layer * count + i, layer * count + (i ^ 2)) for i in range(count)]
+        return lax.ppermute(sent, ("section", "seq"), moves)
+
+    def from_pair(value, far):
+        far = far.astype(value.dtype)
+        keep = pick(low_micro, value[:tokens], value[tokens:])
+        return jnp.stack([pick(low_micro, keep, far), pick(low_micro, far, keep)])[None, :, None]
+
+    result_far = []
     kept, results = [], []
     for layer in range(2):
         pieces, feeds = mix_pieces[layer], feed_pieces[layer]
         vectors, up_bias, mix_bias = take_vectors(params, pieces, scal)
-        normed, keep, send = mix_forward(params, hidden, vectors, mix_bias, scal, pieces, [])
+        normed, keep, send = mix_forward(
+            params, hidden, vectors, mix_bias, scal, pieces, result_far
+        )
         other = swap(send, "seq", 1)
         out_keep, out_send, peaks = attend_forward(
-            keep, other, scal, feed_stages[layer][0] + feed_stages[layer][1] + [incoming]
+            keep, other, scal,
+            feed_stages[layer][0] + feed_stages[layer][1],
         )
         out_other = swap(out_send, "seq", 1)
         mixed, own, send = out_forward(
-            params, out_keep, out_other, scal, pieces, width, feed_stages[layer][2]
+            params, out_keep, out_other, scal, pieces, width,
+            feed_stages[layer][2] + ([incoming] if layer == 0 else []),
         )
         far = swap(send, "section", 1)
         branch, residual, normed_two, active, slope, own, send = feed_forward(
             params, hidden, own, far, vectors, up_bias, scal, feeds,
-            mix_stages[1][0] + mix_stages[1][1] if layer == 0 else [],
+            [],
         )
         far = swap(send, "section", 1)
         kept.append(
@@ -1158,13 +1179,16 @@
         )
         hidden = layer_result(
             residual, own, far, vectors,
-            mix_stages[1][2] + feed_stages[1][0] if layer == 0 else [],
+            sum(mix_stages[1], []) if layer == 0 else [],
         )
         results.append(hidden)
-
-    section_output, sent = from_pair(pick(first, results[0], results[1]))
+        if layer == 0:
+            result_far = [send_layer(send_rows(hidden), 0)]
+
+    result_far.append(send_layer(send_rows(results[1]), 1))
+    section_output = from_pair(pick(first, *results), pick(first, *result_far))
     gradients, mix_shares, feed_shares = [None] * 2, [None] * 2, [None] * 2
-    waits = {"attend": [sent]}
+    in_sums, waits = [], {"out": [result_far[1]]}
     for layer in (1, 0):
         pieces, feeds = mix_pieces[layer], feed_pieces[layer]
         hidden, normed, keep, other, peaks, mixed, branch, residual, normed_two, active = kept[
@@ -1172,15 +1196,18 @@
         ][:10]
         slope, branch_own, branch_far, vectors = kept[layer][10:]
         lower, up_grad, up_sum, own, send = feed_backward(
-            params, incoming, vectors, slope, scal, feeds, waits.get("feed", [])
+            params, incoming, vectors, slope, scal, feeds, waits.get("lower", [])
         )
         far = swap(send, "section", 1)
-        grads = feed_weights(params, active, lower, normed_two, up_grad, scal, [branch_far])
-        feed_share, feed_hops = scatter_blocks(grads, bits)
-        feed_shares[layer], feed_lines = sum_shares(feed_share, layer)
+        feed_grads = feed_weights(
+            params, active, lower, normed_two, up_grad, scal, waits.get("feed", [branch_far]) + [far],
+        )
+        feed_share, feed_hops = scatter_blocks(feed_grads, bits)
+        feed_shares[layer], feed_moved = sum_line(feed_share)
         feed_sum = feed_sums(incoming, branch_own, branch_far, vectors, lower)
         residual_grad, branch_grad, grad_keep, grad_send, out_sum = out_backward(
-            params, incoming, residual, own, far, branch, vectors, scal, pieces, waits.get("out", [])
+            params, incoming, residual, own, far, branch, vectors, scal, pieces,
+            [feed_grads[0]] + waits.get("out", []),
         )
         grad_other = swap(grad_send, "seq", 1)
         triple_keep, triple_send = attend_backward(
@@ -1188,28 +1215,36 @@
         )
         triple_other = swap(triple_send, "seq", 1)
         triple, own, send = mix_backward(
-            params, triple_keep, triple_other, scal, pieces, width, waits.get("mix", []) + feed_hops[0]
+            params, triple_keep, triple_other, scal, pieces, width,
+            waits.get("mix", []) + feed_hops[0],
         )
         far = swap(send, "section", 1)
-        input_grad, incoming, in_sum = input_backward(hidden, own, far, residual_grad, vectors)
+        input_grad, incoming, in_sum = input_backward(
+            hidden, own, far, residual_grad, vectors, waits.get("input", [])
+        )
         gradients[layer] = input_grad
+        in_sums.append(in_sum)
         after = []
         if layer == 0:
-            input_gradient, sent = from_pair(pick(first, gradients[0], gradients[1]))
-            after = [sent]
+            gradient_far.append(send_layer(send_rows(input_grad), 0))
+            after = [[feed_moved[0]], feed_moved[1]]
+        if layer == 1:
+            gradient_far = [send_layer(send_rows(input_grad), 1)]
         grads = mix_weights(
-            params, normed, triple, mixed, branch_grad, [in_sum, out_sum, feed_sum, up_sum], scal,
+            params, normed, triple, mixed, branch_grad,
+            (in_sums if layer == 0 else []) + [out_sum, feed_sum, up_sum], scal,
             waits.get("weights", []) + (feed_hops[1] if layer == 0 else []),
         )
         mix_share, mix_hops = scatter_blocks(grads, bits, after)
-        mix_shares[layer], mix_lines = sum_shares(mix_share, layer)
+        mix_shares[layer], mix_moved = sum_line(mix_share)
         waits = {
-            "feed": sum(feed_hops[1:], []),
-            "out": mix_hops[0],
-            "attend": sum(mix_hops[1:], []),
-            "mix": [moved[0] for moved in feed_lines],
-            "weights": [moved[1] for moved in feed_lines] + [moved[0] for moved in mix_lines],
+            "feed": gradient_far + feed_hops[-1] + sum(mix_hops, []) + [feed_moved[0]],
+            "out": [mix_moved[0]],
+            "mix": feed_moved[1],
+            "weights": [feed_moved[2]] + mix_moved[1],
         }
+
+    first_rows = mix_shares[0][0][4 * rows :]
 
     def collect(unpack, shares):
         own = [pick(first, low, high) for low, high in zip(*shares)]
@@ -1228,14 +1263,17 @@
         size = value.shape[-1] >> joined
         return lax.dynamic_slice_in_dim(value, place * size, size, axis=value.ndim - 1)
 
-    whole = own_part(sums[0, :8])[:, None]
+    own_sums = pick(first, sums[0], sums[1])
+    later = first_rows[11:13, :rows].astype(F32)
+    whole = jnp.concatenate([pick(first, own_sums[:2], later), own_sums[2:8]], axis=0)
+    whole = own_part(whole)[:, None]
     up_total = own_part(sums[:, 8:10].reshape(1, 4 * rows))
     bias_total = sums[:, 10].reshape(2, 2, rows // 2).transpose(1, 0, 2).reshape(2, rows)
     bias_total = own_part(bias_total)[None]
 
     return (
         section_output,
-        input_gradient,
+        from_pair(pick(first, *gradients), pick(first, *gradient_far[::-1])),
         whole[0],
         whole[1],
         mix_total,

time: 747 us -> 708 us (0.948)
  waiting for transfers between devices: 386 us -> 313 us
  starting transfers between devices: 97.8 us -> 111 us
  other arithmetic: 23.5 us -> 33.5 us
  local copies, waits for them, and re-layouts: 38.1 us -> 47.7 us
    ppermute x18 -> x4, waiting for transfers between devices: 115 us -> 12 us  [send_layer(): return lax.ppermute(sent, ('section', 'seq'), moves)]
    ppermute x68 -> x78, starting transfers between devices: 56.3 us -> 100 us  [swap(): return lax.ppermute(value, axis, [(i, i ^ bit) for i in range(count)])]
    ppermute x18 -> x4, starting transfers between devices: 41.5 us -> 10.9 us  [send_layer(): return lax.ppermute(sent, ('section', 'seq'), moves)]
    ppermute x68 -> x78, waiting for transfers between devices: 271 us -> 301 us  [swap(): return lax.ppermute(value, axis, [(i, i ^ bit) for i in range(count)])]
    unnamed x270 -> x268, local copies, waits for them, and re-layouts: 32.7 us -> 42.2 us
    select_n x13 -> x17, other arithmetic: 1.86 us -> 10.6 us  [pick(): return jnp.where(flag, first, second)]
    convert_element_type x26 -> x16, other arithmetic: 14.9 us -> 18.8 us  [add_low(): return (left.astype(F32) + right.astype(F32)).astype(BF16)]
    pallas_call x34 -> x38, Pallas kernels: 193 us -> 195 us  [run_kernel(): pl.pallas_call(body, name=name, out_shape=[jax.ShapeDtypeStruct(s, d) for...]
  transfers between devices with their start and end apart: 86 -> 82, of which waited for: 41 -> 38; matrix products, arithmetic and copies ran while one was open for 3% -> 5% of each run, Pallas kernels for 22% -> 21%
where the time goes in v3:
time: 708 us; the launch traced here: 704 us
  waiting for transfers between devices  313 us (44%)
  Pallas kernels  195 us (28%)
  starting transfers between devices  111 us (16%)
  local copies, waits for them, and re-layouts  47.7 us (7%)
  other arithmetic  33.5 us (5%)
    ppermute x78, waiting for transfers between devices, swap(): return lax.ppermute(value, axis, [(i, i ^ bit) for i in range(count)])  301 us
    pallas_call x38, Pallas kernels, run_kernel(): pl.pallas_call(body, name=name, out_shape=[jax.ShapeDtypeStruct(s, d) for...  195 us
    ppermute x78, starting transfers between devices, swap(): return lax.ppermute(value, axis, [(i, i ^ bit) for i in range(count)])  100 us
    unnamed x268, local copies, waits for them, and re-layouts  42.2 us
    convert_element_type x16, other arithmetic, add_low(): return (left.astype(F32) + right.astype(F32)).astype(BF16)  18.8 us
  transfers between devices with their start and end apart: 82, of which 38 were waited for; matrix products, arithmetic and copies ran while one was open for 5% of the time, Pallas kernels for 21%

profile of v3, /device:TPU:0, one launch (start us, length us, event | category | flops | bytes accessed | tf_op | source)
XLA Modules:
  0.0 704.1 jit_solution(4356407897107458559)
XLA Ops:
  20.8 23.3 %collective-permute-done.8.refs_6_ = bf16[256,1024]{1,0:T(8,128)(2,1)S(1)} collective-permute-done((bf16[256,1024]{1,0:T(8,128)(2,1)S(1)}, bf16[256,1024]{1,0:T(8,128)(2,1)S(1)}, u32[]{:S(2)}, u32[]{:S(2)}) %collective-permute-start.8) | collective-permute-done | bytes 524320 | tf_op jit(solution)/shard_map/ppermute | solution.py:796
  48.1 11.0 %collective-permute-done.12.refs_3_.refs_7_.refs_9_.refs_12_ = bf16[1040,256]{1,0:T(8,128)(2,1)S(1)} collective-permute-done((bf16[1040,256]{1,0:T(8,128)(2,1)S(1)}, bf16[1040,256]{1,0:T(8,128)(2,1)S(1)}, u32[]{:S(2)}, u32[]{:S(2)}) %collective-permute-start.12) | collective-permute-done | bytes 532512 | tf_op jit(solution)/shard_map/ppermute | solution.py:796
  59.6 8.9 %collective-permute-done.14.refs_5_.refs_11_.refs_13_.refs_16_ = bf16[1040,256]{1,0:T(8,128)(2,1)S(1)} collective-permute-done((bf16[1040,256]{1,0:T(8,128)(2,1)S(1)}, bf16[1040,256]{1,0:T(8,128)(2,1)S(1)}, u32[]{:S(2)}, u32[]{:S(2)}) %collective-permute-start.14) | collective-permute-done | bytes 532512 | tf_op jit(solution)/shard_map/ppermute | solution.py:796
  74.1 4.6 mix_forward.2
  83.4 13.7 %collective-permute-done.17.refs_0_.refs_8_.refs_6_ = bf16[1024,512]{1,0:T(8,128)(2,1)S(1)} collective-permute-done((bf16[1024,512]{1,0:T(8,128)(2,1)S(1)}, bf16[1024,512]{1,0:T(8,128)(2,1)S(1)}, u32[]{:S(2)}, u32[]{:S(2)}) %collective-permute-start.17) | collective-permute-done | bytes 1048608 | tf_op jit(solution)/shard_map/ppermute | solution.py:796
  100.8 20.3 %collective-permute-done.22.refs_2_.refs_10_.refs_8_ = bf16[1024,512]{1,0:T(8,128)(2,1)S(1)} collective-permute-done((bf16[1024,512]{1,0:T(8,128)(2,1)S(1)}, bf16[1024,512]{1,0:T(8,128)(2,1)S(1)}, u32[]{:S(2)}, u32[]{:S(2)}) %collective-permute-start.22) | collective-permute-done | bytes 1048608 | tf_op jit(solution)/shard_map/ppermute | solution.py:796
  121.1 13.7 %attend_forward.2 = (bf16[512,256]{1,0:T(8,128)(2,1)S(1)}, bf16[512,256]{1,0:T(8,128)(2,1)S(1)}, f32[8,1024]{1,0:T(8,128)S(1)}) custom-call(bf16[1024,512]{1,0:T(8,128)(2,1)S(1)} %collective-permute-done.17.refs_0_.refs_8_.refs_6_, bf16[1024,512]{1,0:T(8,128)(2,1)S(1)} %collective-permute-done.19.refs_1_.refs_11_.refs_9_, ...), custom_call_target="tpu_custom_call" | custom-call | flops 67108864 | bytes 133121 | tf_op jit(solution)/shard_map/attend_forward/pallas_call | solution.py:50
  136.7 4.5 collective-permute-done.25.refs_5_
  147.8 16.5 %feed_forward.2 = (f32[512,1024]{1,0:T(8,128)S(1)}, f32[512,1024]{1,0:T(8,128)}, bf16[512,1024]{1,0:T(8,128)(2,1)S(1)}, bf16[512,2048]{1,0:T(8,128)(2,1)}, bf16[...) custom-call(s32[4]{0:T(128)S(1)} %pad_add_fusion.refs_0_.refs_7_.refs_4_.refs_3_.refs_1_.refs_2_.refs_9_, ...), custom_call_target="tpu_custom_call" | custom-call | flops 268435456 | bytes 1577473 | tf_op jit(solution)/shard_map/feed_forward/pallas_call | solution.py:50
  169.8 10.9 %collective-permute-done.5.refs_3_.refs_8_.refs_12_ = bf16[1040,256]{1,0:T(8,128)(2,1)S(1)} collective-permute-done((bf16[1040,256]{1,0:T(8,128)(2,1)S(1)}, bf16[1040,256]{1,0:T(8,128)(2,1)S(1)}, u32[]{:S(2)}, u32[]{:S(2)}) %collective-permute-start.5) | collective-permute-done | bytes 532512 | tf_op jit(solution)/shard_map/ppermute | solution.py:796
  182.0 10.1 %collective-permute-done.7.refs_5_.refs_12_.refs_16_ = bf16[1040,256]{1,0:T(8,128)(2,1)S(1)} collective-permute-done((bf16[1040,256]{1,0:T(8,128)(2,1)S(1)}, bf16[1040,256]{1,0:T(8,128)(2,1)S(1)}, u32[]{:S(2)}, u32[]{:S(2)}) %collective-permute-start.7) | collective-permute-done | bytes 532512 | tf_op jit(solution)/shard_map/ppermute | solution.py:796
  196.8 4.9 collective-permute-start.34
  204.8 9.8 %collective-permute-done.34.refs_0_ = bf16[256,1024]{1,0:T(8,128)(2,1)S(1)} collective-permute-done((bf16[256,1024]{1,0:T(8,128)(2,1)S(1)}, bf16[256,1024]{1,0:T(8,128)(2,1)S(1)}, u32[]{:S(2)}, u32[]{:S(2)}) %collective-permute-start.34) | collective-permute-done | bytes 524320 | tf_op jit(solution)/shard_map/ppermute | solution.py:1145
  214.5 4.6 mix_forward.3
  223.1 14.5 %collective-permute-done.32.refs_2_.refs_10_.refs_8_ = bf16[1024,512]{1,0:T(8,128)(2,1)S(1)} collective-permute-done((bf16[1024,512]{1,0:T(8,128)(2,1)}, bf16[1024,512]{1,0:T(8,128)(2,1)S(1)}, u32[]{:S(2)}, u32[]{:S(2)}) %collective-permute-start.32) | collective-permute-done | bytes 1048608 | tf_op jit(solution)/shard_map/ppermute | solution.py:796
  237.6 13.7 %attend_forward.3 = (bf16[512,256]{1,0:T(8,128)(2,1)S(1)}, bf16[512,256]{1,0:T(8,128)(2,1)S(1)}, f32[8,1024]{1,0:T(8,128)S(1)}) custom-call(bf16[1024,512]{1,0:T(8,128)(2,1)S(1)} %collective-permute-done.28.refs_0_.refs_8_.refs_6_, bf16[1024,512]{1,0:T(8,128)(2,1)S(1)} %collective-permute-done.30.refs_1_.refs_11_.refs_9_, ...), custom_call_target="tpu_custom_call" | custom-call | flops 67108864 | bytes 133121 | tf_op jit(solution)/shard_map/attend_forward/pallas_call | solution.py:50
  253.0 6.2 collective-permute-done.29.refs_0_.refs_12_.refs_10_
  265.7 16.2 %feed_forward.3 = (f32[512,1024]{1,0:T(8,128)S(1)}, f32[512,1024]{1,0:T(8,128)}, bf16[512,1024]{1,0:T(8,128)(2,1)S(1)}, bf16[512,2048]{1,0:T(8,128)(2,1)}, bf16[...) custom-call(s32[4]{0:T(128)S(1)} %pad_add_fusion.refs_0_.refs_7_.refs_4_.refs_3_.refs_1_.refs_2_.refs_9_, ...), custom_call_target="tpu_custom_call" | custom-call | flops 268435456 | bytes 1577473 | tf_op jit(solution)/shard_map/feed_forward/pallas_call | solution.py:50
  286.9 8.2 %feed_backward.2 = (bf16[512,1024]{1,0:T(8,128)(2,1)S(1)}, bf16[512,2048]{1,0:T(8,128)(2,1)S(1)}, f32[1,2048]{1,0:T(1,128)S(1)}, f32[512,1024]{1,0:T(8,128)S(1)}, bf16[512,1024]{1,0:T(8,128)(2,1)S(1)}) custom-call(s32[4]{0:T(128)S(1)} %pad_add_fusion.refs_0_.refs_7_.refs_4_.refs_3_.refs_1_.refs_2_.refs_9_, ...), custom_call_target="tpu_custom_call" | custom-call | flops 268435456 | bytes 1118721 | tf_op jit(solution)/shard_map/feed_backward/pallas_call | solution.py:50
  306.3 7.7 %feed_weights.2 = (bf16[2048,512]{1,0:T(8,128)(2,1)S(1)}, bf16[1024,512]{1,0:T(8,128)(2,1)S(1)}, bf16[1024,512]{1,0:T(8,128)(2,1)S(1)}, bf16[2048,512]{1,0:T(8,1...) custom-call(bf16[512,1024]{1,0:T(8,128)(2,1)S(1)} %collective-permute-done.38.refs_2_.refs_0_, ...), custom_call_target="tpu_custom_call" | custom-call | flops 268435456 | bytes 917505 | tf_op jit(solution)/shard_map/feed_weights/pallas_call | solution.py:50
  318.5 4.8 out_backward.2
  325.0 5.9 collective-permute-done.47.refs_4_
  330.9 16.6 %attend_backward.2 = (bf16[512,768]{1,0:T(8,128)(2,1)S(1)}, bf16[512,768]{1,0:T(8,128)(2,1)S(1)}) custom-call(s32[4]{0:T(128)S(1)} %pad_add_fusion.refs_0_.refs_7_.refs_4_.refs_3_.refs_1_.refs_2_.refs_9_, bf16[512,768]{1,0:T(8,128)(2,1)S(1)} %get-tuple-element.164.refs_5_.refs_1_, bf16[512,768]{1,0:T(8,128)(2,1)S(1)} %collective-permute-done.35.refs_6_.refs_2_, ...), custom_call_target="tpu_custom_call" | custom-call | flops 167772160 | bytes 231425 | tf_op jit(solution)/shard_map/attend_backward/pallas_call | solution.py:50
  350.1 11.7 %collective-permute-done.43.refs_1_ = bf16[2048,512]{1,0:T(8,128)(2,1)S(1)} collective-permute-done((bf16[2048,512]{1,0:T(8,128)(2,1)S(1)}, bf16[2048,512]{1,0:T(8,128)(2,1)S(1)}, u32[]{:S(2)}, u32[]{:S(2)}) %collective-permute-start.43) | collective-permute-done | bytes 2097184 | tf_op jit(solution)/shard_map/ppermute | solution.py:796
  367.7 4.6 mix_backward.2
  372.3 5.0 collective-permute-start.49
  377.2 6.2 mix_weights.2
  404.1 8.3 %feed_backward.3 = (bf16[512,1024]{1,0:T(8,128)(2,1)S(1)}, bf16[512,2048]{1,0:T(8,128)(2,1)S(1)}, f32[1,2048]{1,0:T(1,128)S(1)}, f32[512,1024]{1,0:T(8,128)S(1)}, bf16[512,1024]{1,0:T(8,128)(2,1)S(1)}) custom-call(s32[4]{0:T(128)S(1)} %pad_add_fusion.refs_0_.refs_7_.refs_4_.refs_3_.refs_1_.refs_2_.refs_9_, ...), custom_call_target="tpu_custom_call" | custom-call | flops 268435456 | bytes 1118721 | tf_op jit(solution)/shard_map/feed_backward/pallas_call | solution.py:50
  418.4 10.0 %collective-permute-done.53.refs_5_ = bf16[1040,256]{1,0:T(8,128)(2,1)S(1)} collective-permute-done((bf16[1040,256]{1,0:T(8,128)(2,1)S(1)}, bf16[1040,256]{1,0:T(8,128)(2,1)S(1)}, u32[]{:S(2)}, u32[]{:S(2)}) %collective-permute-start.53) | collective-permute-done | bytes 532512 | tf_op jit(solution)/shard_map/ppermute | solution.py:796
  429.8 8.4 %feed_weights.3 = (bf16[2048,512]{1,0:T(8,128)(2,1)}, bf16[1024,512]{1,0:T(8,128)(2,1)S(1)}, bf16[1024,512]{1,0:T(8,128)(2,1)S(1)}, bf16[2048,512]{1,0:T(8,128)(...) custom-call(bf16[256,1024]{1,0:T(8,128)(2,1)S(1)} %collective-permute-done.50.refs_0_, ...), custom_call_target="tpu_custom_call" | custom-call | flops 268435456 | bytes 917505 | tf_op jit(solution)/shard_map/feed_weights/pallas_call | solution.py:50
  451.7 11.4 %collective-permute-done.58.refs_1_ = bf16[1040,256]{1,0:T(8,128)(2,1)S(1)} collective-permute-done((bf16[1040,256]{1,0:T(8,128)(2,1)S(1)}, bf16[1040,256]{1,0:T(8,128)(2,1)S(1)}, u32[]{:S(2)}, u32[]{:S(2)}) %collective-permute-start.58) | collective-permute-done | bytes 532512 | tf_op jit(solution)/shard_map/ppermute | solution.py:796
  463.1 4.8 out_backward.3
  469.0 14.1 %collective-permute-done.59.refs_4_ = bf16[512,256]{1,0:T(8,128)(2,1)S(1)} collective-permute-done((bf16[512,256]{1,0:T(8,128)(2,1)S(1)}, bf16[512,256]{1,0:T(8,128)(2,1)S(1)}, u32[]{:S(2)}, u32[]{:S(2)}) %collective-permute-start.59) | collective-permute-done | bytes 262176 | tf_op jit(solution)/shard_map/ppermute | solution.py:796
  483.1 16.7 %attend_backward.3 = (bf16[512,768]{1,0:T(8,128)(2,1)S(1)}, bf16[512,768]{1,0:T(8,128)(2,1)S(1)}) custom-call(s32[4]{0:T(128)S(1)} %pad_add_fusion.refs_0_.refs_7_.refs_4_.refs_3_.refs_1_.refs_2_.refs_9_, bf16[512,768]{1,0:T(8,128)(2,1)S(1)} %copy-done.69, bf16[512,768]{1,0:T(8,128)(2,1)S(1)} %copy-done.71, bf16[512,256]{1,0:T(8,128)(2,1)S(1)} %get-tuple-element.220.refs_3_, ...), custom_call_target="tpu_custom_call" | custom-call | flops 167772160 | bytes 231425 | tf_op jit(solution)/shard_map/attend_backward/pallas_call | solution.py:50
  507.6 11.5 %collective-permute-done.60.refs_5_ = bf16[512,768]{1,0:T(8,128)(2,1)S(1)} collective-permute-done((bf16[512,768]{1,0:T(8,128)(2,1)S(1)}, bf16[512,768]{1,0:T(8,128)(2,1)S(1)}, u32[]{:S(2)}, u32[]{:S(2)}) %collective-permute-start.60) | collective-permute-done | bytes 786464 | tf_op jit(solution)/shard_map/ppermute | solution.py:796
  519.1 4.8 mix_backward.3
  542.4 4.9 input_backward.3
  547.2 5.7 collective-permute-done.68.refs_1_
  553.2 5.4 mix_weights.3
  559.0 5.8 collective-permute-start.71
  564.9 10.5 %collective-permute-done.65.refs_0_ = bf16[1024,512]{1,0:T(8,128)(2,1)S(1)} collective-permute-done((bf16[1024,512]{1,0:T(8,128)(2,1)}, bf16[1024,512]{1,0:T(8,128)(2,1)S(1)}, u32[]{:S(2)}, u32[]{:S(2)}) %collective-permute-start.65) | collective-permute-done | bytes 1048608 | tf_op jit(solution)/shard_map/ppermute | solution.py:796
  576.4 5.2 collective-permute-start.66
  582.8 5.8 collective-permute-start.70
  595.7 4.8 collective-permute-done.70.refs_2_
  600.4 27.3 %collective-permute-done.66.refs_0_ = bf16[1024,512]{1,0:T(8,128)(2,1)S(1)} collective-permute-done((bf16[1024,512]{1,0:T(8,128)(2,1)S(1)}, bf16[1024,512]{1,0:T(8,128)(2,1)S(1)}, u32[]{:S(2)}, u32[]{:S(2)}) %collective-permute-start.66) | collective-permute-done | bytes 1048608 | tf_op jit(solution)/shard_map/ppermute | solution.py:796
  628.3 4.6 collective-permute-start.62
  633.4 15.4 %collective-permute-done.73 = bf16[1040,256]{1,0:T(8,128)(2,1)S(1)} collective-permute-done((bf16[1040,256]{1,0:T(8,128)(2,1)S(1)}, bf16[1040,256]{1,0:T(8,128)(2,1)S(1)}, u32[]{:S(2)}, u32[]{:S(2)}) %collective-permute-start.73) | collective-permute-done | bytes 532512 | tf_op jit(solution)/shard_map/ppermute | solution.py:796
  652.2 30.2 %collective-permute-done.74 = bf16[1040,256]{1,0:T(8,128)(2,1)S(1)} collective-permute-done((bf16[1040,256]{1,0:T(8,128)(2,1)S(1)}, bf16[1040,256]{1,0:T(8,128)(2,1)S(1)}, u32[]{:S(2)}, u32[]{:S(2)}) %collective-permute-start.74) | collective-permute-done | bytes 532512 | tf_op jit(solution)/shard_map/ppermute | solution.py:796
  (478 shorter events, 206.5 us)
Async XLA Ops:
  12.7 31.9 %collective-permute-start.15 = (bf16[1024,512]{1,0:T(8,128)(2,1)S(1)}, bf16[1024,512]{1,0:T(8,128)(2,1)S(1)}, u32[]{:S(2)}, u32[]{:S(2)}) collective-permute-start(bf16[1024,512]{1,0:T(8,128)(2,1)S(1)} %get-tuple-element.144), channel_id=1, source_target_pairs={{0,16},{16,0},{1,17},{17,1},{2,18},{18,2},{3,19},{19,3},{4,20},{20... | collective-permute-start | bytes 3145736 | tf_op jit(solution)/shard_map/ppermute | solution.py:796
  13.9 31.1 %collective-permute-start.10 = (bf16[1040,256]{1,0:T(8,128)(2,1)S(1)}, bf16[1040,256]{1,0:T(8,128)(2,1)S(1)}, u32[]{:S(2)}, u32[]{:S(2)}) collective-permute-start(bf16[1040,256]{1,0:T(8,128)(2,1)S(1)} %get-tuple-element.141.refs_5_.refs_7_.refs_10_), channel_id=1, source_target_pairs={{0,2},{1,3},{2,0},{3,1},{4,6},{5,7},{6,4},{7,5},{8,10},{9,11},{10,... | collective-permute-start | bytes 1597448 | tf_op jit(solution)/shard_map/ppermute | solution.py:796
  16.6 30.0 %collective-permute-start.9 = (bf16[1040,256]{1,0:T(8,128)(2,1)S(1)}, bf16[1040,256]{1,0:T(8,128)(2,1)S(1)}, u32[]{:S(2)}, u32[]{:S(2)}) collective-permute-start(bf16[1040,256]{1,0:T(8,128)(2,1)S(1)} %get-tuple-element.140.refs_1_.refs_4_.refs_6_.refs_9_), channel_id=1, source_target_pairs={{0,1},{1,0},{2,3},{3,2},{4,5},{5,4},{6,7},{7,6},{8,9},{9,8},{10,11... | collective-permute-start | bytes 1597448 | tf_op jit(solution)/shard_map/ppermute | solution.py:796
  18.1 25.9 %collective-permute-start.8 = (bf16[256,1024]{1,0:T(8,128)(2,1)S(1)}, bf16[256,1024]{1,0:T(8,128)(2,1)S(1)}, u32[]{:S(2)}, u32[]{:S(2)}) collective-permute-start(bf16[256,1024]{1,0:T(8,128)(2,1)S(1)} %select_bitcast_fusion.3), channel_id=1, source_target_pairs={{0,8},{4,12},{8,0},{12,4},{1,9},{5,13},{9,1},{13,5},{2,10},{6,14},... | collective-permute-start | bytes 1572872 | tf_op jit(solution)/shard_map/ppermute | solution.py:796
  20.8 27.3 %collective-permute-start.16 = (bf16[1024,512]{1,0:T(8,128)(2,1)S(1)}, bf16[1024,512]{1,0:T(8,128)(2,1)S(1)}, u32[]{:S(2)}, u32[]{:S(2)}) collective-permute-start(bf16[1024,512]{1,0:T(8,128)(2,1)S(1)} %get-tuple-element.145), channel_id=1, source_target_pairs={{0,16},{16,0},{1,17},{17,1},{2,18},{18,2},{3,19},{19,3},{4,20},{20... | collective-permute-start | bytes 3145736 | tf_op jit(solution)/shard_map/ppermute | solution.py:796
  45.0 23.4 %collective-permute-start.14 = (bf16[1040,256]{1,0:T(8,128)(2,1)S(1)}, bf16[1040,256]{1,0:T(8,128)(2,1)S(1)}, u32[]{:S(2)}, u32[]{:S(2)}) collective-permute-start(bf16[1040,256]{1,0:T(8,128)(2,1)S(1)} %collective-permute-done.10.refs_1_.refs_9_.refs_11_.refs_14_), channel_id=1, source_target_pairs={{0,1},{1,0},{2,3},{3,2},{4,5},{5,4},{6,7},{7,6},{8,9},{9,8},{10,11... | collective-permute-start | bytes 1597448 | tf_op jit(solution)/shard_map/ppermute | solution.py:796
  46.6 22.2 %collective-permute-start.13 = (bf16[1040,256]{1,0:T(8,128)(2,1)S(1)}, bf16[1040,256]{1,0:T(8,128)(2,1)S(1)}, u32[]{:S(2)}, u32[]{:S(2)}) collective-permute-start(bf16[1040,256]{1,0:T(8,128)(2,1)S(1)} %collective-permute-done.9.refs_0_.refs_2_.refs_6_.refs_8_.refs_11_), channel_id=1, source_target_pairs={{0,2},{1,3},{2,0},{3,1},{4,6},{5,7},{6,4},{7,5},{8,10},{9,11},{10,... | collective-permute-start | bytes 1597448 | tf_op jit(solution)/shard_map/ppermute | solution.py:796
  71.0 26.1 %collective-permute-start.17 = (bf16[1024,512]{1,0:T(8,128)(2,1)S(1)}, bf16[1024,512]{1,0:T(8,128)(2,1)S(1)}, u32[]{:S(2)}, u32[]{:S(2)}) collective-permute-start(bf16[1024,512]{1,0:T(8,128)(2,1)S(1)} %get-tuple-element.146.refs_6_.refs_4_), channel_id=1, source_target_pairs={{0,1},{1,0},{2,3},{3,2},{4,5},{5,4},{6,7},{7,6},{8,9},{9,8},{10,11... | collective-permute-start | bytes 3145736 | tf_op jit(solution)/shard_map/ppermute | solution.py:796
  72.5 26.1 %collective-permute-start.19 = (bf16[1024,512]{1,0:T(8,128)(2,1)S(1)}, bf16[1024,512]{1,0:T(8,128)(2,1)S(1)}, u32[]{:S(2)}, u32[]{:S(2)}) collective-permute-start(bf16[1024,512]{1,0:T(8,128)(2,1)S(1)} %get-tuple-element.147.refs_7_.refs_5_), channel_id=1, source_target_pairs={{0,2},{1,3},{2,0},{3,1},{4,6},{5,7},{6,4},{7,5},{8,10},{9,11},{10,... | collective-permute-start | bytes 3145736 | tf_op jit(solution)/shard_map/ppermute | solution.py:796
  81.4 39.7 %collective-permute-start.22 = (bf16[1024,512]{1,0:T(8,128)(2,1)S(1)}, bf16[1024,512]{1,0:T(8,128)(2,1)S(1)}, u32[]{:S(2)}, u32[]{:S(2)}) collective-permute-start(bf16[1024,512]{1,0:T(8,128)(2,1)S(1)} %get-tuple-element.146.refs_6_.refs_4_), channel_id=1, source_target_pairs={{0,2},{1,3},{2,0},{3,1},{4,6},{5,7},{6,4},{7,5},{8,10},{9,11},{10,... | collective-permute-start | bytes 3145736 | tf_op jit(solution)/shard_map/ppermute | solution.py:796
  82.9 38.2 %collective-permute-start.23 = (bf16[1024,512]{1,0:T(8,128)(2,1)S(1)}, bf16[1024,512]{1,0:T(8,128)(2,1)S(1)}, u32[]{:S(2)}, u32[]{:S(2)}) collective-permute-start(bf16[1024,512]{1,0:T(8,128)(2,1)S(1)} %get-tuple-element.147.refs_7_.refs_5_), channel_id=1, source_target_pairs={{0,1},{1,0},{2,3},{3,2},{4,5},{5,4},{6,7},{7,6},{8,9},{9,8},{10,11... | collective-permute-start | bytes 3145736 | tf_op jit(solution)/shard_map/ppermute | solution.py:796
  97.1 44.1 %collective-permute-start.18 = (bf16[1024,512]{1,0:T(8,128)(2,1)S(1)}, bf16[1024,512]{1,0:T(8,128)(2,1)S(1)}, u32[]{:S(2)}, u32[]{:S(2)}) collective-permute-start(bf16[1024,512]{1,0:T(8,128)(2,1)S(1)} %collective-permute-done.17.refs_0_.refs_8_.refs_6_), channel_id=1, source_target_pairs={{0,2},{1,3},{2,0},{3,1},{4,6},{5,7},{6,4},{7,5},{8,10},{9,11},{10,... | collective-permute-start | bytes 3145736 | tf_op jit(solution)/shard_map/ppermute | solution.py:796
  98.6 42.7 %collective-permute-start.20 = (bf16[1024,512]{1,0:T(8,128)(2,1)S(1)}, bf16[1024,512]{1,0:T(8,128)(2,1)S(1)}, u32[]{:S(2)}, u32[]{:S(2)}) collective-permute-start(bf16[1024,512]{1,0:T(8,128)(2,1)S(1)} %collective-permute-done.19.refs_1_.refs_11_.refs_9_), channel_id=1, source_target_pairs={{0,1},{1,0},{2,3},{3,2},{4,5},{5,4},{6,7},{7,6},{8,9},{9,8},{10,11... | collective-permute-start | bytes 3145736 | tf_op jit(solution)/shard_map/ppermute | solution.py:796
  99.2 37.3 %collective-permute-start.21 = (bf16[256,1024]{1,0:T(8,128)(2,1)S(1)}, bf16[256,1024]{1,0:T(8,128)(2,1)S(1)}, u32[]{:S(2)}, u32[]{:S(2)}) collective-permute-start(bf16[256,1024]{1,0:T(8,128)(2,1)S(1)} %select_bitcast_fusion.2), channel_id=1, source_target_pairs={{0,8},{4,12},{8,0},{12,4},{1,9},{5,13},{9,1},{13,5},{2,10},{6,14},... | collective-permute-start | bytes 1572872 | tf_op jit(solution)/shard_map/ppermute | solution.py:796
  145.5 22.8 %collective-permute-start.2 = (bf16[1040,256]{1,0:T(8,128)(2,1)S(1)}, bf16[1040,256]{1,0:T(8,128)(2,1)S(1)}, u32[]{:S(2)}, u32[]{:S(2)}) collective-permute-start(bf16[1040,256]{1,0:T(8,128)(2,1)S(1)} %get-tuple-element.138.refs_1_.refs_5_.refs_9_), channel_id=1, source_target_pairs={{0,1},{1,0},{2,3},{3,2},{4,5},{5,4},{6,7},{7,6},{8,9},{9,8},{10,11... | collective-permute-start | bytes 1597448 | tf_op jit(solution)/shard_map/ppermute | solution.py:796
  165.6 27.0 %collective-permute-start.27 = (bf16[512,1024]{1,0:T(8,128)(2,1)S(1)}, bf16[512,1024]{1,0:T(8,128)(2,1)S(1)}, u32[]{:S(2)}, u32[]{:S(2)}) collective-permute-start(bf16[512,1024]{1,0:T(8,128)(2,1)S(1)} %get-tuple-element.159), channel_id=1, source_target_pairs={{0,16},{16,0},{1,17},{17,1},{2,18},{18,2},{3,19},{19,3},{4,20},{20... | collective-permute-start | bytes 3145736 | tf_op jit(solution)/shard_map/ppermute | solution.py:796
  167.1 25.0 %collective-permute-start.7 = (bf16[1040,256]{1,0:T(8,128)(2,1)S(1)}, bf16[1040,256]{1,0:T(8,128)(2,1)S(1)}, u32[]{:S(2)}, u32[]{:S(2)}) collective-permute-start(bf16[1040,256]{1,0:T(8,128)(2,1)S(1)} %collective-permute-done.3.refs_1_.refs_10_.refs_14_), channel_id=1, source_target_pairs={{0,1},{1,0},{2,3},{3,2},{4,5},{5,4},{6,7},{7,6},{8,9},{9,8},{10,11... | collective-permute-start | bytes 1597448 | tf_op jit(solution)/shard_map/ppermute | solution.py:796
  168.3 24.3 %collective-permute-start.6 = (bf16[1040,256]{1,0:T(8,128)(2,1)S(1)}, bf16[1040,256]{1,0:T(8,128)(2,1)S(1)}, u32[]{:S(2)}, u32[]{:S(2)}) collective-permute-start(bf16[1040,256]{1,0:T(8,128)(2,1)S(1)} %collective-permute-done.2.refs_0_.refs_2_.refs_7_.refs_11_), channel_id=1, source_target_pairs={{0,2},{1,3},{2,0},{3,1},{4,6},{5,7},{6,4},{7,5},{8,10},{9,11},{10,... | collective-permute-start | bytes 1597448 | tf_op jit(solution)/shard_map/ppermute | solution.py:796
  180.7 40.4 %collective-permute-start.28 = (bf16[1024,512]{1,0:T(8,128)(2,1)}, bf16[1024,512]{1,0:T(8,128)(2,1)S(1)}, u32[]{:S(2)}, u32[]{:S(2)}) collective-permute-start(bf16[1024,512]{1,0:T(8,128)(2,1)} %get-tuple-element.160.refs_6_.refs_4_), channel_id=1, source_target_pairs={{0,1},{1,0},{2,3},{3,2},{4,5},{5,4},{6,7},{7,6},{8,9},{9,8},{10,11... | collective-permute-start | bytes 3145736 | tf_op jit(solution)/shard_map/ppermute | solution.py:796
  181.3 40.6 %collective-permute-start.30 = (bf16[1024,512]{1,0:T(8,128)(2,1)}, bf16[1024,512]{1,0:T(8,128)(2,1)S(1)}, u32[]{:S(2)}, u32[]{:S(2)}) collective-permute-start(bf16[1024,512]{1,0:T(8,128)(2,1)} %get-tuple-element.161.refs_7_.refs_5_), channel_id=1, source_target_pairs={{0,2},{1,3},{2,0},{3,1},{4,6},{5,7},{6,4},{7,5},{8,10},{9,11},{10,... | collective-permute-start | bytes 3145736 | tf_op jit(solution)/shard_map/ppermute | solution.py:796
  201.7 35.9 %collective-permute-start.32 = (bf16[1024,512]{1,0:T(8,128)(2,1)}, bf16[1024,512]{1,0:T(8,128)(2,1)S(1)}, u32[]{:S(2)}, u32[]{:S(2)}) collective-permute-start(bf16[1024,512]{1,0:T(8,128)(2,1)} %get-tuple-element.160.refs_6_.refs_4_), channel_id=1, source_target_pairs={{0,2},{1,3},{2,0},{3,1},{4,6},{5,7},{6,4},{7,5},{8,10},{9,11},{10,... | collective-permute-start | bytes 3145736 | tf_op jit(solution)/shard_map/ppermute | solution.py:796
  202.5 35.1 %collective-permute-start.33 = (bf16[1024,512]{1,0:T(8,128)(2,1)}, bf16[1024,512]{1,0:T(8,128)(2,1)S(1)}, u32[]{:S(2)}, u32[]{:S(2)}) collective-permute-start(bf16[1024,512]{1,0:T(8,128)(2,1)} %get-tuple-element.161.refs_7_.refs_5_), channel_id=1, source_target_pairs={{0,1},{1,0},{2,3},{3,2},{4,5},{5,4},{6,7},{7,6},{8,9},{9,8},{10,11... | collective-permute-start | bytes 3145736 | tf_op jit(solution)/shard_map/ppermute | solution.py:796
  221.1 38.1 %collective-permute-start.29 = (bf16[1024,512]{1,0:T(8,128)(2,1)S(1)}, bf16[1024,512]{1,0:T(8,128)(2,1)S(1)}, u32[]{:S(2)}, u32[]{:S(2)}) collective-permute-start(bf16[1024,512]{1,0:T(8,128)(2,1)S(1)} %collective-permute-done.28.refs_0_.refs_8_.refs_6_), channel_id=1, source_target_pairs={{0,2},{1,3},{2,0},{3,1},{4,6},{5,7},{6,4},{7,5},{8,10},{9,11},{10,... | collective-permute-start | bytes 3145736 | tf_op jit(solution)/shard_map/ppermute | solution.py:796
  221.8 37.4 %collective-permute-start.31 = (bf16[1024,512]{1,0:T(8,128)(2,1)S(1)}, bf16[1024,512]{1,0:T(8,128)(2,1)S(1)}, u32[]{:S(2)}, u32[]{:S(2)}) collective-permute-start(bf16[1024,512]{1,0:T(8,128)(2,1)S(1)} %collective-permute-done.30.refs_1_.refs_11_.refs_9_), channel_id=1, source_target_pairs={{0,1},{1,0},{2,3},{3,2},{4,5},{5,4},{6,7},{7,6},{8,9},{9,8},{10,11... | collective-permute-start | bytes 3145736 | tf_op jit(solution)/shard_map/ppermute | solution.py:796
  314.0 47.7 %collective-permute-start.43 = (bf16[2048,512]{1,0:T(8,128)(2,1)S(1)}, bf16[2048,512]{1,0:T(8,128)(2,1)S(1)}, u32[]{:S(2)}, u32[]{:S(2)}) collective-permute-start(bf16[2048,512]{1,0:T(8,128)(2,1)S(1)} %get-tuple-element.184), channel_id=1, source_target_pairs={{0,2},{1,3},{2,0},{3,1},{4,6},{5,7},{6,4},{7,5},{8,10},{9,11},{10,... | collective-permute-start | bytes 6291464 | tf_op jit(solution)/shard_map/ppermute | solution.py:796
  315.0 49.8 %collective-permute-start.41 = (bf16[2048,512]{1,0:T(8,128)(2,1)S(1)}, bf16[2048,512]{1,0:T(8,128)(2,1)S(1)}, u32[]{:S(2)}, u32[]{:S(2)}) collective-permute-start(bf16[2048,512]{1,0:T(8,128)(2,1)S(1)} %get-tuple-element.181.refs_0_), channel_id=1, source_target_pairs={{0,1},{1,0},{2,3},{3,2},{4,5},{5,4},{6,7},{7,6},{8,9},{9,8},{10,11... | collective-permute-start | bytes 6291464 | tf_op jit(solution)/shard_map/ppermute | solution.py:796
  363.3 25.7 %collective-permute-start.44 = (bf16[1024,512]{1,0:T(8,128)(2,1)}, bf16[1024,512]{1,0:T(8,128)(2,1)}, u32[]{:S(2)}, u32[]{:S(2)}) collective-permute-start(bf16[1024,512]{1,0:T(8,128)(2,1)} %add_convert_fusion.11), channel_id=1, source_target_pairs={{0,1},{1,0},{2,3},{3,2},{4,5},{5,4},{6,7},{7,6},{8,9},{9,8},{10,11... | collective-permute-start | bytes 3145736 | tf_op jit(solution)/shard_map/ppermute | solution.py:796
  366.2 25.6 %collective-permute-start.42 = (bf16[1024,512]{1,0:T(8,128)(2,1)}, bf16[1024,512]{1,0:T(8,128)(2,1)}, u32[]{:S(2)}, u32[]{:S(2)}) collective-permute-start(bf16[1024,512]{1,0:T(8,128)(2,1)} %add_convert_fusion.14), channel_id=1, source_target_pairs={{0,2},{1,3},{2,0},{3,1},{4,6},{5,7},{6,4},{7,5},{8,10},{9,11},{10,... | collective-permute-start | bytes 3145736 | tf_op jit(solution)/shard_map/ppermute | solution.py:796
  372.3 25.1 %collective-permute-start.49 = (bf16[512,1024]{1,0:T(8,128)(2,1)}, bf16[512,1024]{1,0:T(8,128)(2,1)}, u32[]{:S(2)}, u32[]{:S(2)}) collective-permute-start(bf16[512,1024]{1,0:T(8,128)(2,1)} %get-tuple-element.194), channel_id=1, source_target_pairs={{0,16},{16,0},{1,17},{17,1},{2,18},{18,2},{3,19},{19,3},{4,20},{20... | collective-permute-start | bytes 3145736 | tf_op jit(solution)/shard_map/ppermute | solution.py:796
  386.6 25.9 %collective-permute-start.51 = (bf16[2080,256]{1,0:T(8,128)(2,1)}, bf16[2080,256]{1,0:T(8,128)(2,1)}, u32[]{:S(2)}, u32[]{:S(2)}) collective-permute-start(bf16[2080,256]{1,0:T(8,128)(2,1)} %get-tuple-element.203), channel_id=1, source_target_pairs={{0,1},{1,0},{2,3},{3,2},{4,5},{5,4},{6,7},{7,6},{8,9},{9,8},{10,11... | collective-permute-start | bytes 3194888 | tf_op jit(solution)/shard_map/ppermute | solution.py:796
  387.5 27.9 %collective-permute-start.52 = (bf16[2080,256]{1,0:T(8,128)(2,1)}, bf16[2080,256]{1,0:T(8,128)(2,1)}, u32[]{:S(2)}, u32[]{:S(2)}) collective-permute-start(bf16[2080,256]{1,0:T(8,128)(2,1)} %get-tuple-element.204), channel_id=1, source_target_pairs={{0,2},{1,3},{2,0},{3,1},{4,6},{5,7},{6,4},{7,5},{8,10},{9,11},{10,... | collective-permute-start | bytes 3194888 | tf_op jit(solution)/shard_map/ppermute | solution.py:796
  395.6 34.1 %collective-permute-start.45 = (bf16[1024,512]{1,0:T(8,128)(2,1)S(1)}, bf16[1024,512]{1,0:T(8,128)(2,1)S(1)}, u32[]{:S(2)}, u32[]{:S(2)}) collective-permute-start(bf16[1024,512]{1,0:T(8,128)(2,1)S(1)} %broadcast_select_fusion.9), channel_id=1, source_target_pairs={{0,4},{4,0},{8,12},{12,8},{1,5},{5,1},{9,13},{13,9},{2,6},{6,2},{1... | collective-permute-start | bytes 3145736 | tf_op jit(solution)/shard_map/ppermute | solution.py:796
  439.3 63.0 %collective-permute-start.57 = (bf16[2048,512]{1,0:T(8,128)(2,1)}, bf16[2048,512]{1,0:T(8,128)(2,1)S(1)}, u32[]{:S(2)}, u32[]{:S(2)}) collective-permute-start(bf16[2048,512]{1,0:T(8,128)(2,1)} %get-tuple-element.215), channel_id=1, source_target_pairs={{0,2},{1,3},{2,0},{3,1},{4,6},{5,7},{6,4},{7,5},{8,10},{9,11},{10,... | collective-permute-start | bytes 6291464 | tf_op jit(solution)/shard_map/ppermute | solution.py:796
  441.1 62.1 %collective-permute-start.56 = (bf16[2048,512]{1,0:T(8,128)(2,1)}, bf16[2048,512]{1,0:T(8,128)(2,1)S(1)}, u32[]{:S(2)}, u32[]{:S(2)}) collective-permute-start(bf16[2048,512]{1,0:T(8,128)(2,1)} %get-tuple-element.214.refs_0_), channel_id=1, source_target_pairs={{0,1},{1,0},{2,3},{3,2},{4,5},{5,4},{6,7},{7,6},{8,9},{9,8},{10,11... | collective-permute-start | bytes 6291464 | tf_op jit(solution)/shard_map/ppermute | solution.py:796
  448.7 55.7 %collective-permute-start.46 = (bf16[1024,512]{1,0:T(8,128)(2,1)}, bf16[1024,512]{1,0:T(8,128)(2,1)S(1)}, u32[]{:S(2)}, u32[]{:S(2)}) collective-permute-start(bf16[1024,512]{1,0:T(8,128)(2,1)} %add_convert_fusion.9), channel_id=1, source_target_pairs={{0,8},{4,12},{8,0},{12,4},{1,9},{5,13},{9,1},{13,5},{2,10},{6,14},... | collective-permute-start | bytes 3145736 | tf_op jit(solution)/shard_map/ppermute | solution.py:796
  502.6 30.8 %collective-permute-start.64 = (bf16[1024,512]{1,0:T(8,128)(2,1)S(1)}, bf16[1024,512]{1,0:T(8,128)(2,1)S(1)}, u32[]{:S(2)}, u32[]{:S(2)}) collective-permute-start(bf16[1024,512]{1,0:T(8,128)(2,1)S(1)} %add_convert_fusion.4), channel_id=1, source_target_pairs={{0,1},{1,0},{2,3},{3,2},{4,5},{5,4},{6,7},{7,6},{8,9},{9,8},{10,11... | collective-permute-start | bytes 3145736 | tf_op jit(solution)/shard_map/ppermute | solution.py:796
  503.5 30.0 %collective-permute-start.63 = (bf16[1024,512]{1,0:T(8,128)(2,1)S(1)}, bf16[1024,512]{1,0:T(8,128)(2,1)S(1)}, u32[]{:S(2)}, u32[]{:S(2)}) collective-permute-start(bf16[1024,512]{1,0:T(8,128)(2,1)S(1)} %add_convert_fusion.7), channel_id=1, source_target_pairs={{0,2},{1,3},{2,0},{3,1},{4,6},{5,7},{6,4},{7,5},{8,10},{9,11},{10,... | collective-permute-start | bytes 3145736 | tf_op jit(solution)/shard_map/ppermute | solution.py:796
  506.9 46.2 %collective-permute-start.67 = (bf16[1024,512]{1,0:T(8,128)(2,1)}, bf16[1024,512]{1,0:T(8,128)(2,1)}, u32[]{:S(2)}, u32[]{:S(2)}) collective-permute-start(bf16[1024,512]{1,0:T(8,128)(2,1)} %add_convert_fusion.1), channel_id=1, source_target_pairs={{0,4},{4,0},{8,12},{12,8},{1,5},{5,1},{9,13},{13,9},{2,6},{6,2},{1... | collective-permute-start | bytes 3145736 | tf_op jit(solution)/shard_map/ppermute | solution.py:796
  530.0 22.9 %collective-permute-start.68 = (bf16[1040,256]{1,0:T(8,128)(2,1)}, bf16[1040,256]{1,0:T(8,128)(2,1)}, u32[]{:S(2)}, u32[]{:S(2)}) collective-permute-start(bf16[1040,256]{1,0:T(8,128)(2,1)} %add_convert_fusion.21), channel_id=1, source_target_pairs={{0,8},{4,12},{8,0},{12,4},{1,9},{5,13},{9,1},{13,5},{2,10},{6,14},... | collective-permute-start | bytes 1597448 | tf_op jit(solution)/shard_map/ppermute | solution.py:796
  535.4 40.0 %collective-permute-start.65 = (bf16[1024,512]{1,0:T(8,128)(2,1)}, bf16[1024,512]{1,0:T(8,128)(2,1)S(1)}, u32[]{:S(2)}, u32[]{:S(2)}) collective-permute-start(bf16[1024,512]{1,0:T(8,128)(2,1)} %broadcast_select_fusion.8), channel_id=1, source_target_pairs={{0,4},{4,0},{8,12},{12,8},{1,5},{5,1},{9,13},{13,9},{2,6},{6,2},{1... | collective-permute-start | bytes 3145736 | tf_op jit(solution)/shard_map/ppermute | solution.py:796
  558.6 24.1 %collective-permute-start.69 = (bf16[2080,256]{1,0:T(8,128)(2,1)S(1)}, bf16[2080,256]{1,0:T(8,128)(2,1)S(1)}, u32[]{:S(2)}, u32[]{:S(2)}) collective-permute-start(bf16[2080,256]{1,0:T(8,128)(2,1)S(1)} %get-tuple-element.242), channel_id=1, source_target_pairs={{0,1},{1,0},{2,3},{3,2},{4,5},{5,4},{6,7},{7,6},{8,9},{9,8},{10,11... | collective-permute-start | bytes 3194888 | tf_op jit(solution)/shard_map/ppermute | solution.py:796
  559.0 29.6 %collective-permute-start.71 = (bf16[2080,256]{1,0:T(8,128)(2,1)S(1)}, bf16[2080,256]{1,0:T(8,128)(2,1)S(1)}, u32[]{:S(2)}, u32[]{:S(2)}) collective-permute-start(bf16[2080,256]{1,0:T(8,128)(2,1)S(1)} %get-tuple-element.245), channel_id=1, source_target_pairs={{0,2},{1,3},{2,0},{3,1},{4,6},{5,7},{6,4},{7,5},{8,10},{9,11},{10,... | collective-permute-start | bytes 3194888 | tf_op jit(solution)/shard_map/ppermute | solution.py:796
  576.4 51.4 %collective-permute-start.66 = (bf16[1024,512]{1,0:T(8,128)(2,1)S(1)}, bf16[1024,512]{1,0:T(8,128)(2,1)S(1)}, u32[]{:S(2)}, u32[]{:S(2)}) collective-permute-start(bf16[1024,512]{1,0:T(8,128)(2,1)S(1)} %add_convert_fusion.2), channel_id=1, source_target_pairs={{0,8},{4,12},{8,0},{12,4},{1,9},{5,13},{9,1},{13,5},{2,10},{6,14},... | collective-permute-start | bytes 3145736 | tf_op jit(solution)/shard_map/ppermute | solution.py:796
  588.8 39.2 %collective-permute-start.72 = (bf16[1040,256]{1,0:T(8,128)(2,1)S(1)}, bf16[1040,256]{1,0:T(8,128)(2,1)S(1)}, u32[]{:S(2)}, u32[]{:S(2)}) collective-permute-start(bf16[1040,256]{1,0:T(8,128)(2,1)S(1)} %add_convert_fusion.19), channel_id=1, source_target_pairs={{0,1},{1,0},{2,3},{3,2},{4,5},{5,4},{6,7},{7,6},{8,9},{9,8},{10,11... | collective-permute-start | bytes 1597448 | tf_op jit(solution)/shard_map/ppermute | solution.py:796
  593.0 97.1 %collective-permute-start.76 = (bf16[1040,256]{1,0:T(8,128)(2,1)S(1)}, bf16[1040,256]{1,0:T(8,128)(2,1)S(1)}, u32[]{:S(2)}, u32[]{:S(2)}) collective-permute-start(bf16[1040,256]{1,0:T(8,128)(2,1)S(1)} %add_convert_fusion.16), channel_id=1, source_target_pairs={{0,4},{4,0},{8,12},{12,8},{1,5},{5,1},{9,13},{13,9},{2,6},{6,2},{1... | collective-permute-start | bytes 1597448 | tf_op jit(solution)/shard_map/ppermute | solution.py:796
  628.3 23.5 %collective-permute-start.62 = (bf16[256,1024]{1,0:T(8,128)(2,1)S(1)}, bf16[256,1024]{1,0:T(8,128)(2,1)S(1)}, u32[]{:S(2)}, u32[]{:S(2)}) collective-permute-start(bf16[256,1024]{1,0:T(8,128)(2,1)S(1)} %select_convert_fusion), channel_id=1, source_target_pairs={{0,8},{4,12},{8,0},{12,4},{1,9},{5,13},{9,1},{13,5},{2,10},{6,14},... | collective-permute-start | bytes 1572872 | tf_op jit(solution)/shard_map/ppermute | solution.py:1145
  633.3 54.3 %collective-permute-start.79 = (bf16[1024,512]{1,0:T(8,128)(2,1)S(1)}, bf16[1024,512]{1,0:T(8,128)(2,1)S(1)}, u32[]{:S(2)}, u32[]{:S(2)}) collective-permute-start(bf16[1024,512]{1,0:T(8,128)(2,1)S(1)} %add_convert_fusion), channel_id=1, source_target_pairs={{0,4},{4,0},{8,12},{12,8},{1,5},{5,1},{9,13},{13,9},{2,6},{6,2},{1... | collective-permute-start | bytes 3145736 | tf_op jit(solution)/shard_map/ppermute | solution.py:796
  649.0 33.3 %collective-permute-start.74 = (bf16[1040,256]{1,0:T(8,128)(2,1)S(1)}, bf16[1040,256]{1,0:T(8,128)(2,1)S(1)}, u32[]{:S(2)}, u32[]{:S(2)}) collective-permute-start(bf16[1040,256]{1,0:T(8,128)(2,1)S(1)} %add_convert_fusion.18), channel_id=1, source_target_pairs={{0,8},{4,12},{8,0},{12,4},{1,9},{5,13},{9,1},{13,5},{2,10},{6,14},... | collective-permute-start | bytes 1597448 | tf_op jit(solution)/shard_map/ppermute | solution.py:796
  (168 other events, 2515.0 us)
